TPU v7x, 32 devices: a whole 2x2x4 slice. The times are simulated.
32 devices in a mesh: dp: 4 (over z), seq: 8 (over y, x, core).
Axes of the slice: x: 2, y: 2, z: 4, core: 2. Of those that a mesh axis runs over, the one named last changes fastest.
Arguments:
- tokens: bfloat16 [8, 512, 1536], P('dp', 'seq'), may hold values from -6 to 6
- doc_lengths: int32 [8, 8], P('dp'), may hold values from 1 to 480, as said below
- query_weight: bfloat16 [1536, 1536], P(('dp', 'seq')), may hold values from -0.15625 to 0.15625
- key_weight: bfloat16 [1536, 256], P(('dp', 'seq')), may hold values from -0.15625 to 0.15625
- value_weight: bfloat16 [1536, 256], P(('dp', 'seq')), may hold values from -0.15625 to 0.15625
- query_bias: bfloat16 [1536], P(('dp', 'seq')), may hold values from -3 to 3
- key_bias: bfloat16 [256], P(('dp', 'seq')), may hold values from -3 to 3
- value_bias: bfloat16 [256], P(('dp', 'seq')), may hold values from -3 to 3
- output_weight: bfloat16 [1536, 1536], P(('dp', 'seq')), may hold values from -0.3125 to 0.3125
- attention_norm_gain: bfloat16 [1536], P(('dp', 'seq')), may hold values from 0.099609375 to 1.8984375
- feedforward_norm_gain: bfloat16 [1536], P(('dp', 'seq')), may hold values from 0.099609375 to 1.8984375
- gate_weight: bfloat16 [1536, 8960], P(('dp', 'seq')), may hold values from -0.15625 to 0.15625
- up_weight: bfloat16 [1536, 8960], P(('dp', 'seq')), may hold values from -0.15625 to 0.15625
- down_weight: bfloat16 [8960, 1536], P(('dp', 'seq')), may hold values from -0.125 to 0.125
- cotangent: bfloat16 [8, 512, 1536], P('dp', 'seq'), may hold values from -6 to 6
Outputs:
- layer_output: bfloat16 [8, 512, 1536], P('dp', 'seq')
- input_grad: bfloat16 [8, 512, 1536], P('dp', 'seq')
- grad_query_weight: float32 [1536, 1536], P(('dp', 'seq'))
- grad_key_weight: float32 [1536, 256], P(('dp', 'seq'))
- grad_value_weight: float32 [1536, 256], P(('dp', 'seq'))
- grad_query_bias: float32 [1536], P(('dp', 'seq'))
- grad_key_bias: float32 [256], P(('dp', 'seq'))
- grad_value_bias: float32 [256], P(('dp', 'seq'))
- grad_output_weight: float32 [1536, 1536], P(('dp', 'seq'))
- grad_input_gain: float32 [1536], P(('dp', 'seq'))
- grad_post_gain: float32 [1536], P(('dp', 'seq'))
- grad_gate_weight: float32 [1536, 8960], P(('dp', 'seq'))
- grad_up_weight: float32 [1536, 8960], P(('dp', 'seq'))
- grad_down_weight: float32 [8960, 1536], P(('dp', 'seq'))
Inputs may be any that keep to these rules, and one draw needn't show every extreme that they name: `doc_lengths`: each row's 8 lengths sum to 512.
All inputs are finite; a program needn't handle non-finite values.
Results may differ from a plain program's by a relative error of at most 0.029.
Values may be sent and summed in bfloat16 or wider, within the bound.
No kernel may reach another device: no remote copies, remote signals or barrier semaphores. Data moves between devices by JAX's collectives and lax.ppermute only.
A program may use at most 512 MiB of HBM per device.

v0:
```python
import math

import jax
import jax.numpy as jnp
from jax import lax
from jax.sharding import PartitionSpec as P

H = 12
KV = 2
HD = 128
HPG = 6


epsilon = 1e-06
rope_base = 10000.0
masked_value = -1e30


def root_mean_square_scale(values):
    return lax.rsqrt(jnp.mean(values * values, axis=-1, keepdims=True) + epsilon)


def rope_tables(within):
    steps_even = jnp.arange(0, HD, 2).astype(jnp.float32)
    inverse = rope_base ** (-steps_even / HD)
    phase = within.astype(jnp.float32)[:, None] * inverse[None, :]
    phase = jnp.concatenate([phase, phase], axis=-1)
    return (jnp.cos(phase)[:, None, :], jnp.sin(phase)[:, None, :])


def rotate(values, cosine, sine):
    halfway = values.shape[-1] // 2
    return (
        values * cosine
        + jnp.concatenate([-values[..., halfway:], values[..., :halfway]], axis=-1) * sine
    )


def rotate_back(grads, cosine, sine):
    halfway = grads.shape[-1] // 2
    turned = grads * sine
    return grads * cosine + jnp.concatenate(
        [turned[..., halfway:], -turned[..., :halfway]], axis=-1
    )


def doc_tables(doc_ends, doc_lengths, positions):
    passed = doc_ends[:, None, :] <= positions[None, :, None]
    doc_index = jnp.sum(passed.astype(jnp.int32), axis=-1)
    starts = jnp.sum(jnp.where(passed, doc_lengths[:, None, :], 0), axis=-1)
    return (doc_index, positions[None, :] - starts)


def contract_rows(left, right):
    return lax.dot_general(
        left, right, (((0,), (0,)), ((), ())), preferred_element_type=jnp.float32
    )


def contract_cols(left, right):
    return lax.dot_general(
        left, right, (((1,), (1,)), ((), ())), preferred_element_type=jnp.float32
    )


def to_groups(flat_heads, local_rows, shard_tokens):
    shaped = flat_heads.reshape(local_rows, shard_tokens, KV, HPG, HD).transpose(0, 2, 3, 1, 4)
    return shaped.reshape(local_rows, KV, HPG * shard_tokens, HD)


def from_groups(grouped, local_rows, shard_tokens):
    shaped = grouped.reshape(local_rows, KV, HPG, shard_tokens, HD).transpose(0, 3, 1, 2, 4)
    return shaped.reshape(local_rows * shard_tokens, H * HD)


def shards(
    tokens,
    doc_lengths,
    query_weight,
    key_weight,
    value_weight,
    query_bias,
    key_bias,
    value_bias,
    output_weight,
    attention_norm_gain,
    feedforward_norm_gain,
    gate_weight,
    up_weight,
    down_weight,
    cotangent,
):
    local_rows, shard_tokens, width = tokens.shape
    seq_devices = lax.axis_size("seq")
    row_length = shard_tokens * seq_devices
    flat_count = local_rows * shard_tokens
    block_len = min(512, row_length)
    block_count = row_length // block_len
    scaling = 1.0 / math.sqrt(HD)
    attention_params = (
        lax.all_gather(query_weight, ("dp", "seq"), axis=0, tiled=True),
        lax.all_gather(key_weight, ("dp", "seq"), axis=0, tiled=True),
        lax.all_gather(value_weight, ("dp", "seq"), axis=0, tiled=True),
        lax.all_gather(query_bias, ("dp", "seq"), axis=0, tiled=True),
        lax.all_gather(key_bias, ("dp", "seq"), axis=0, tiled=True),
        lax.all_gather(value_bias, ("dp", "seq"), axis=0, tiled=True),
        lax.all_gather(output_weight, ("dp", "seq"), axis=0, tiled=True),
        lax.all_gather(attention_norm_gain, ("dp", "seq"), axis=0, tiled=True),
        lax.all_gather(feedforward_norm_gain, ("dp", "seq"), axis=0, tiled=True),
    )
    (
        weight_query,
        weight_key,
        weight_value,
        bias_query,
        bias_key,
        bias_value,
        weight_output,
        input_gain_value,
        gain_post,
    ) = attention_params
    local_pos = lax.axis_index("seq") * shard_tokens + jnp.arange(shard_tokens, dtype=jnp.int32)
    all_pos = jnp.arange(row_length, dtype=jnp.int32)
    doc_ends = jnp.cumsum(doc_lengths, axis=1)
    query_doc, query_within = doc_tables(doc_ends, doc_lengths, local_pos)
    key_doc, unused_within = doc_tables(doc_ends, doc_lengths, all_pos)
    cosine, sine = rope_tables(query_within.reshape(flat_count))
    flattened_input = tokens.reshape(flat_count, width).astype(jnp.float32)
    first_inverse_norm = root_mean_square_scale(flattened_input)
    first_normalized = flattened_input * first_inverse_norm
    first_normed = (first_normalized * input_gain_value.astype(jnp.float32)).astype(jnp.bfloat16)
    query_pre = jnp.dot(
        first_normed, weight_query, preferred_element_type=jnp.float32
    ) + bias_query.astype(jnp.float32)
    key_pre = jnp.dot(
        first_normed, weight_key, preferred_element_type=jnp.float32
    ) + bias_key.astype(jnp.float32)
    value_pre = jnp.dot(
        first_normed, weight_value, preferred_element_type=jnp.float32
    ) + bias_value.astype(jnp.float32)
    queries = rotate(query_pre.reshape(flat_count, H, HD), cosine, sine).astype(jnp.bfloat16)
    key_rows = rotate(key_pre.reshape(flat_count, KV, HD), cosine, sine).astype(jnp.bfloat16)
    value_rows = value_pre.astype(jnp.bfloat16)
    gathered_keys, gathered_values = (
        lax.all_gather(
            key_rows.reshape(local_rows, shard_tokens, KV * HD), "seq", axis=1, tiled=True
        ),
        lax.all_gather(
            value_rows.reshape(local_rows, shard_tokens, KV * HD), "seq", axis=1, tiled=True
        ),
    )
    key_heads = gathered_keys.reshape(local_rows, row_length, KV, HD).transpose(0, 2, 1, 3)
    value_heads = gathered_values.reshape(local_rows, row_length, KV, HD).transpose(0, 2, 1, 3)
    query_groups = to_groups(queries.reshape(flat_count, H * HD), local_rows, shard_tokens)
    query_doc_rows = jnp.tile(query_doc, (1, HPG))
    query_pos_rows = jnp.tile(local_pos, (HPG,))
    group_rows = HPG * shard_tokens

    def block_inputs(block_index):
        block_start = block_index * block_len
        key_block = lax.dynamic_slice_in_dim(key_heads, block_start, block_len, 2)
        value_block = lax.dynamic_slice_in_dim(value_heads, block_start, block_len, 2)
        doc_block = lax.dynamic_slice_in_dim(key_doc, block_start, block_len, 1)
        key_pos = block_start + jnp.arange(block_len, dtype=jnp.int32)
        raw_scores = (
            jnp.einsum(
                "rgmd,rgkd->rgmk", query_groups, key_block, preferred_element_type=jnp.float32
            )
            * scaling
        )
        allowed = (query_doc_rows[:, None, :, None] == doc_block[:, None, None, :]) & (
            key_pos[None, None, None, :] <= query_pos_rows[None, None, :, None]
        )
        return (jnp.where(allowed, raw_scores, masked_value), key_block, value_block)

    def pass_max(state, block_index):
        row_top, row_total = state
        masked, key_block, value_block = block_inputs(block_index)
        new_top = jnp.maximum(row_top, jnp.max(masked, axis=-1, keepdims=True))
        row_total = row_total * jnp.exp(row_top - new_top) + jnp.sum(
            jnp.exp(masked - new_top), axis=-1, keepdims=True
        )
        return ((new_top, row_total), None)

    stat_shape = (local_rows, KV, group_rows, 1)
    (row_top, row_total), unused_max = lax.scan(
        pass_max,
        (jnp.full(stat_shape, masked_value, jnp.float32), jnp.zeros(stat_shape, jnp.float32)),
        jnp.arange(block_count, dtype=jnp.int32),
    )
    log_total = row_top + jnp.log(row_total)

    def pass_mix(mixed_sum, block_index):
        masked, key_block, value_block = block_inputs(block_index)
        soft_probs = jnp.exp(masked - log_total).astype(jnp.bfloat16)
        return (
            mixed_sum
            + jnp.einsum(
                "rgmk,rgkd->rgmd", soft_probs, value_block, preferred_element_type=jnp.float32
            ),
            None,
        )

    mixed_sum, unused_mix = lax.scan(
        pass_mix,
        jnp.zeros((local_rows, KV, group_rows, HD), jnp.float32),
        jnp.arange(block_count, dtype=jnp.int32),
    )
    attended = from_groups(mixed_sum, local_rows, shard_tokens).astype(jnp.bfloat16)
    first_hidden = flattened_input + jnp.dot(
        attended, weight_output, preferred_element_type=jnp.float32
    )
    second_inverse_norm = root_mean_square_scale(first_hidden)
    second_normalized = first_hidden * second_inverse_norm
    feedforward_scale = gain_post.astype(jnp.float32)
    second_normed = (second_normalized * feedforward_scale).astype(jnp.bfloat16)
    pieces = (
        lax.all_gather(gate_weight, ("dp", "seq"), axis=0, tiled=True),
        lax.all_gather(up_weight, ("dp", "seq"), axis=0, tiled=True),
    )
    columns = second_normed
    gate_pre = jnp.dot(columns, pieces[0], preferred_element_type=jnp.float32)
    up_pre = jnp.dot(columns, pieces[1], preferred_element_type=jnp.float32)
    sigmoid_gate = jax.nn.sigmoid(gate_pre)
    silu_gate = gate_pre * sigmoid_gate
    hidden = (silu_gate * up_pre).astype(jnp.bfloat16)
    columns = hidden
    mlp_out = jnp.dot(
        columns,
        lax.all_gather(down_weight, ("dp", "seq"), axis=0, tiled=True),
        preferred_element_type=jnp.float32,
    )
    layer_output = (
        (first_hidden + mlp_out).astype(jnp.bfloat16).reshape(local_rows, shard_tokens, width)
    )
    upstream = cotangent.reshape(flat_count, width)
    hidden_grad = contract_cols(
        upstream, lax.all_gather(down_weight, ("dp", "seq"), axis=0, tiled=True)
    )
    gate_grad = (
        hidden_grad * up_pre * sigmoid_gate * (1.0 + gate_pre * (1.0 - sigmoid_gate))
    ).astype(jnp.bfloat16)
    up_grad = (hidden_grad * silu_gate).astype(jnp.bfloat16)
    down_sum = lax.psum_scatter(
        contract_rows(hidden, upstream), ("dp", "seq"), scatter_dimension=0, tiled=True
    )
    gate_sum = lax.psum_scatter(
        contract_rows(second_normed, gate_grad), ("dp", "seq"), scatter_dimension=0, tiled=True
    )
    up_sum = lax.psum_scatter(
        contract_rows(second_normed, up_grad), ("dp", "seq"), scatter_dimension=0, tiled=True
    )
    pieces = lax.all_gather((gate_weight, up_weight), ("dp", "seq"), axis=0, tiled=True)
    second_normed_grad = contract_cols(gate_grad, pieces[0]) + contract_cols(up_grad, pieces[1])
    feedforward_gain_term = jnp.sum(second_normed_grad * second_normalized, axis=0)
    second_scaled = second_normed_grad * feedforward_scale
    hidden_one_grad = upstream.astype(jnp.float32) + second_inverse_norm * (
        second_scaled
        - second_normalized * jnp.mean(second_scaled * second_normalized, axis=-1, keepdims=True)
    )
    back_params = (
        lax.all_gather(query_weight, ("dp", "seq"), axis=0, tiled=True),
        lax.all_gather(key_weight, ("dp", "seq"), axis=0, tiled=True),
        lax.all_gather(value_weight, ("dp", "seq"), axis=0, tiled=True),
        lax.all_gather(query_bias, ("dp", "seq"), axis=0, tiled=True),
        lax.all_gather(key_bias, ("dp", "seq"), axis=0, tiled=True),
        lax.all_gather(value_bias, ("dp", "seq"), axis=0, tiled=True),
        lax.all_gather(output_weight, ("dp", "seq"), axis=0, tiled=True),
        lax.all_gather(attention_norm_gain, ("dp", "seq"), axis=0, tiled=True),
        lax.all_gather(feedforward_norm_gain, ("dp", "seq"), axis=0, tiled=True),
    )
    back_query, back_key, back_value = (back_params[0], back_params[1], back_params[2])
    back_output, back_gain = (back_params[6], back_params[7])
    proj_grad = hidden_one_grad.astype(jnp.bfloat16)
    output_weight_term = contract_rows(attended, proj_grad)
    attended_grad = contract_cols(proj_grad, back_output).astype(jnp.bfloat16)
    grad_groups = to_groups(attended_grad, local_rows, shard_tokens)

    def pass_delta(prob_delta, block_index):
        masked, key_block, value_block = block_inputs(block_index)
        soft_probs = jnp.exp(masked - log_total)
        prob_grad = jnp.einsum(
            "rgmd,rgkd->rgmk", grad_groups, value_block, preferred_element_type=jnp.float32
        )
        return (prob_delta + jnp.sum(soft_probs * prob_grad, axis=-1, keepdims=True), None)

    prob_delta, unused_delta = lax.scan(
        pass_delta, jnp.zeros(stat_shape, jnp.float32), jnp.arange(block_count, dtype=jnp.int32)
    )

    def pass_grads(query_sum, block_index):
        masked, key_block, value_block = block_inputs(block_index)
        soft_probs = jnp.exp(masked - log_total)
        prob_grad = jnp.einsum(
            "rgmd,rgkd->rgmk", grad_groups, value_block, preferred_element_type=jnp.float32
        )
        score_grad = (soft_probs * (prob_grad - prob_delta)).astype(jnp.bfloat16)
        query_sum = query_sum + jnp.einsum(
            "rgmk,rgkd->rgmd", score_grad, key_block, preferred_element_type=jnp.float32
        )
        key_part = jnp.einsum(
            "rgmk,rgmd->rgkd", score_grad, query_groups, preferred_element_type=jnp.float32
        )
        value_part = jnp.einsum(
            "rgmk,rgmd->rgkd",
            soft_probs.astype(jnp.bfloat16),
            grad_groups,
            preferred_element_type=jnp.float32,
        )
        return (query_sum, (key_part, value_part))

    query_sum, (key_parts, value_parts) = lax.scan(
        pass_grads,
        jnp.zeros((local_rows, KV, group_rows, HD), jnp.float32),
        jnp.arange(block_count, dtype=jnp.int32),
    )
    key_terms = (
        key_parts.transpose(1, 0, 3, 2, 4).reshape(local_rows, row_length, KV * HD) * scaling
    )
    value_terms = value_parts.transpose(1, 0, 3, 2, 4).reshape(local_rows, row_length, KV * HD)
    key_sums, value_sums = (
        lax.psum_scatter(
            key_terms.astype(jnp.bfloat16), "seq", scatter_dimension=1, tiled=True
        ).astype(jnp.float32),
        lax.psum_scatter(
            value_terms.astype(jnp.bfloat16), "seq", scatter_dimension=1, tiled=True
        ).astype(jnp.float32),
    )
    queries_grad = from_groups(query_sum, local_rows, shard_tokens) * scaling
    query_grad = (
        rotate_back(queries_grad.reshape(flat_count, H, HD), cosine, sine)
        .reshape(flat_count, H * HD)
        .astype(jnp.bfloat16)
    )
    key_grad = (
        rotate_back(key_sums.reshape(flat_count, KV, HD), cosine, sine)
        .reshape(flat_count, KV * HD)
        .astype(jnp.bfloat16)
    )
    value_grad = value_sums.reshape(flat_count, KV * HD).astype(jnp.bfloat16)
    query_weight_term = contract_rows(first_normed, query_grad)
    key_weight_term = contract_rows(first_normed, key_grad)
    value_weight_term = contract_rows(first_normed, value_grad)
    query_bias_term = jnp.sum(query_grad.astype(jnp.float32), axis=0)
    key_bias_term = jnp.sum(key_grad.astype(jnp.float32), axis=0)
    value_bias_term = jnp.sum(value_grad.astype(jnp.float32), axis=0)
    first_normed_grad = (
        contract_cols(query_grad, back_query)
        + contract_cols(key_grad, back_key)
        + contract_cols(value_grad, back_value)
    )
    attention_gain_term = jnp.sum(first_normed_grad * first_normalized, axis=0)
    first_scaled = first_normed_grad * back_gain.astype(jnp.float32)
    input_grad = hidden_one_grad + first_inverse_norm * (
        first_scaled
        - first_normalized * jnp.mean(first_scaled * first_normalized, axis=-1, keepdims=True)
    )
    input_grad = input_grad.astype(jnp.bfloat16).reshape(local_rows, shard_tokens, width)
    summed = (
        lax.psum_scatter(query_weight_term, ("dp", "seq"), scatter_dimension=0, tiled=True),
        lax.psum_scatter(key_weight_term, ("dp", "seq"), scatter_dimension=0, tiled=True),
        lax.psum_scatter(value_weight_term, ("dp", "seq"), scatter_dimension=0, tiled=True),
        lax.psum_scatter(query_bias_term, ("dp", "seq"), scatter_dimension=0, tiled=True),
        lax.psum_scatter(key_bias_term, ("dp", "seq"), scatter_dimension=0, tiled=True),
        lax.psum_scatter(value_bias_term, ("dp", "seq"), scatter_dimension=0, tiled=True),
        lax.psum_scatter(output_weight_term, ("dp", "seq"), scatter_dimension=0, tiled=True),
        lax.psum_scatter(attention_gain_term, ("dp", "seq"), scatter_dimension=0, tiled=True),
        lax.psum_scatter(feedforward_gain_term, ("dp", "seq"), scatter_dimension=0, tiled=True),
    )
    return (
        layer_output,
        input_grad,
        summed[0],
        summed[1],
        summed[2],
        summed[3],
        summed[4],
        summed[5],
        summed[6],
        summed[7],
        summed[8],
        gate_sum,
        up_sum,
        down_sum,
    )


def solution(mesh):
    in_specs = (
        P("dp", "seq", None),
        P("dp", None),
        P(("dp", "seq"), None),
        P(("dp", "seq"), None),
        P(("dp", "seq"), None),
        P(("dp", "seq")),
        P(("dp", "seq")),
        P(("dp", "seq")),
        P(("dp", "seq"), None),
        P(("dp", "seq")),
        P(("dp", "seq")),
        P(("dp", "seq"), None),
        P(("dp", "seq"), None),
        P(("dp", "seq"), None),
        P("dp", "seq", None),
    )
    out_specs = (
        P("dp", "seq", None),
        P("dp", "seq", None),
        P(("dp", "seq"), None),
        P(("dp", "seq"), None),
        P(("dp", "seq"), None),
        P(("dp", "seq")),
        P(("dp", "seq")),
        P(("dp", "seq")),
        P(("dp", "seq"), None),
        P(("dp", "seq")),
        P(("dp", "seq")),
        P(("dp", "seq"), None),
        P(("dp", "seq"), None),
        P(("dp", "seq"), None),
    )
    return jax.shard_map(shards, mesh=mesh, in_specs=in_specs, out_specs=out_specs, check_vma=False)
```

profile of v0, /device:TPU:29, one launch (start us, length us, event | category | flops | bytes accessed | tf_op | source)
XLA Modules:
  0.0 2687.7 jit_solution(10901458393588557117)
XLA Ops:
  14.9 38.9 %all-reduce.12 = (bf16[1536]{0:T(1024)(128)(2,1)S(1)}, bf16[256]{0:T(256)(128)(2,1)S(1)}, bf16[1536]{0:T(1024)(128)(2,1)S(1)}, bf16[256]{0:T(256)(128)(2,1)S(1)}, bf16[1536]{0:T(1024)(128)(2,1)S(1)}) all-reduce(bf16[1536]{0:T(1024)(128)(2,1)S(1)} %dynamic-update-slice, ...), channel_id=1, replica_groups=mesh['dp'=4,'seq'=8] {'dp','seq'}, use_global_device_ids=true, to_apply=%add | all-reduce | flops 5120 | bytes 20480
  54.1 40.2 %all_gather.56 = bf16[1536,256]{1,0:T(8,128)(2,1)S(1)} all-gather(bf16[48,256]{1,0:T(8,128)(2,1)S(1)} %copy-done.41), channel_id=1, replica_groups=mesh['dp'=4,'seq'=8] {'dp','seq'}, dimensions={0}, use_global_device_ids=true | all-gather | bytes 811008 | tf_op jit(solution)/shard_map/all_gather | solution.py:103
  107.5 41.5 %all_gather.53 = bf16[1536,256]{1,0:T(8,128)(2,1)S(1)} all-gather(bf16[48,256]{1,0:T(8,128)(2,1)S(1)} %copy-done.42), channel_id=1, replica_groups=mesh['dp'=4,'seq'=8] {'dp','seq'}, dimensions={0}, use_global_device_ids=true | all-gather | bytes 811008 | tf_op jit(solution)/shard_map/all_gather | solution.py:102
  153.6 12.7 all_gather.55
  191.7 122.0 %all-gather.10.cloned.1.call-done = bf16[1536,8960]{1,0:T(8,128)(2,1)} async-done(((bf16[48,8960]{1,0:T(8,128)(2,1)}), bf16[1536,8960]{1,0:T(8,128)(2,1)}) %all-gather.10.cloned.1.call-update) | async-done | bytes 27525136 | tf_op jit(solution)/shard_map/all_gather | solution.py:218
  313.7 14.8 fusion.35
  328.5 152.1 %all-gather.12.cloned.1.call-done = bf16[1536,8960]{1,0:T(8,128)(2,1)} async-done(((bf16[48,8960]{1,0:T(8,128)(2,1)}), bf16[1536,8960]{1,0:T(8,128)(2,1)}) %all-gather.12.cloned.1.call-update) | async-done | bytes 27525136 | tf_op jit(solution)/shard_map/all_gather | solution.py:219
  480.6 15.2 fusion.36
  495.7 151.7 %all-gather.14.cloned.1.call-done = bf16[8960,1536]{1,0:T(8,128)(2,1)} async-done(((bf16[280,1536]{1,0:T(8,128)(2,1)}), bf16[8960,1536]{1,0:T(8,128)(2,1)}) %all-gather.14.cloned.1.call-update) | async-done | bytes 27525136 | tf_op jit(solution)/shard_map/all_gather | solution.py:230
  647.5 18.6 multiply_convert_fusion
  666.1 15.3 fusion.37
  681.4 16.4 multiply_reduce_fusion.1
  724.6 26.3 reduce-scatter.12.cloned.1.call-done
  756.4 32.2 %reduce-scatter.14.cloned.1.call-done = bf16[2,64,256]{2,1,0:T(8,128)(2,1)} async-done(((bf16[2,512,256]{2,1,0:T(8,128)(2,1)}), bf16[2,64,256]{2,1,0:T(8,128)(2,1)}) %reduce-scatter.14.cloned.1.call-update) | async-done | bytes 65552 | tf_op jit(solution)/shard_map/reduce_scatter | solution.py:325
  808.2 22.8 fusion.39
  832.7 22.6 fusion.40
  856.9 22.3 fusion.41
  917.4 39.1 %all-reduce.11 = (f32[1536]{0:T(1024)S(1)}, f32[256]{0:T(256)S(1)}, f32[256]{0:T(256)S(1)}, f32[1536]{0:T(1024)S(1)}, f32[1536]{0:T(1024)S(1)}) all-reduce(f32[1536]{0:T(1024)S(1)} %copy-done.40, f32[256]{0:T(256)S(1)} %convert_reduce_fusion.2, f32[256]{0:T(256)S(1)} %convert_reduce_fusion.1, ...), channel_id=7, replica_groups=mesh['dp'=4,'seq'=8] {'dp','seq'}, use_global_device_ids=true, to_apply=%region_17.18.clone | all-reduce | flops 5120 | bytes 40960
  960.5 30.6 %reduce-scatter.20.cloned.1.call-done = f32[48,256]{1,0:T(8,128)} async-done(((f32[1536,256]{1,0:T(8,128)}), f32[48,256]{1,0:T(8,128)}) %reduce-scatter.20.cloned.1.call-update) | async-done | bytes 49168 | tf_op jit(solution)/shard_map/reduce_scatter | solution.py:362
  991.1 140.8 %reduce-scatter.16.cloned.1.call-done = f32[48,1536]{1,0:T(8,128)} async-done(((f32[1536,1536]{1,0:T(8,128)}), f32[48,1536]{1,0:T(8,128)}) %reduce-scatter.16.cloned.1.call-update) | async-done | bytes 294928 | tf_op jit(solution)/shard_map/reduce_scatter | solution.py:360
  1131.9 142.1 %reduce-scatter.22.cloned.1.call-done = f32[48,1536]{1,0:T(8,128)} async-done(((f32[1536,1536]{1,0:T(8,128)}), f32[48,1536]{1,0:T(8,128)}) %reduce-scatter.22.cloned.1.call-update) | async-done | bytes 294928 | tf_op jit(solution)/shard_map/reduce_scatter | solution.py:366
  1274.0 469.2 %reduce-scatter.24.cloned.1.call-done = f32[48,8960]{1,0:T(8,128)} async-done(((f32[1536,8960]{1,0:T(8,128)}), f32[48,8960]{1,0:T(8,128)}) %reduce-scatter.24.cloned.1.call-update) | async-done | bytes 1720336 | tf_op jit(solution)/shard_map/reduce_scatter | solution.py:247
  1743.2 469.6 %reduce-scatter.26.cloned.1.call-done = f32[48,8960]{1,0:T(8,128)} async-done(((f32[1536,8960]{1,0:T(8,128)}), f32[48,8960]{1,0:T(8,128)}) %reduce-scatter.26.cloned.1.call-update) | async-done | bytes 1720336 | tf_op jit(solution)/shard_map/reduce_scatter | solution.py:250
  2212.8 468.3 %reduce-scatter.28.cloned.1.call-done = f32[280,1536]{1,0:T(8,128)} async-done(((f32[8960,1536]{1,0:T(8,128)}), f32[280,1536]{1,0:T(8,128)}) %reduce-scatter.28.cloned.1.call-update) | async-done | bytes 1720336
  (251 shorter events, 147.6 us)
Async XLA Ops:
  7.2 46.7 %copy-start.6 = (bf16[2,64,1536]{2,1,0:T(8,128)(2,1)S(1)}, bf16[2,64,1536]{2,1,0:T(8,128)(2,1)}, u32[]{:S(2)}) copy-start(bf16[2,64,1536]{2,1,0:T(8,128)(2,1)} %param.15) | copy-start | bytes 1179652
  7.2 46.9 %copy-start.41 = (bf16[48,256]{1,0:T(8,128)(2,1)S(1)}, bf16[48,256]{1,0:T(8,128)(2,1)}, u32[]{:S(2)}) copy-start(bf16[48,256]{1,0:T(8,128)(2,1)} %param.19) | copy-start | bytes 73732
  7.2 162.7 %all-gather.6.cloned.1.call-start = ((), (), s32[]{:S(2)}) async-start(), calls=%async_computation.9 | async-start | bytes 4866048 | tf_op jit(solution)/shard_map/all_gather | solution.py:101
  7.9 178.4 %all-gather.8.cloned.1.call-start = ((), (), s32[]{:S(2)}) async-start(), calls=%async_computation.10 | async-start | bytes 4866048 | tf_op jit(solution)/shard_map/all_gather | solution.py:107
  8.7 305.0 %all-gather.10.cloned.1.call-start = ((), (), s32[]{:S(2)}) async-start(), calls=%async_computation.11 | async-start | bytes 28385280 | tf_op jit(solution)/shard_map/all_gather | solution.py:218
  9.4 471.1 %all-gather.12.cloned.1.call-start = ((), (), s32[]{:S(2)}) async-start(), calls=%async_computation.12 | async-start | bytes 28385280 | tf_op jit(solution)/shard_map/all_gather | solution.py:219
  10.0 637.5 %all-gather.14.cloned.1.call-start = ((), (), s32[]{:S(2)}) async-start(), calls=%async_computation.13 | async-start | bytes 28385280 | tf_op jit(solution)/shard_map/all_gather | solution.py:230
  10.6 96.4 %copy-start.47 = (s32[2,8]{1,0:T(2,128)S(1)}, s32[2,8]{1,0:T(2,128)}, u32[]{:S(2)}) copy-start(s32[2,8]{1,0:T(2,128)} %param.16) | copy-start | bytes 196
  10.6 96.9 %copy-start.42 = (bf16[48,256]{1,0:T(8,128)(2,1)S(1)}, bf16[48,256]{1,0:T(8,128)(2,1)}, u32[]{:S(2)}) copy-start(bf16[48,256]{1,0:T(8,128)(2,1)} %param.18) | copy-start | bytes 73732
  10.6 740.4 %reduce-scatter.12.cloned.1.call-start = ((), (), s32[]{:S(2)}) async-start(), calls=%async_computation.14 | async-start | bytes 589824 | tf_op jit(solution)/shard_map/reduce_scatter | solution.py:322
  54.0 41.5 %copy-start.46 = (f32[2,64]{1,0:T(2,128)}, f32[2,64]{1,0:T(2,128)S(1)}, u32[]{:S(2)}) copy-start(f32[2,64]{1,0:T(2,128)S(1)} %add_rsqrt_fusion) | copy-start | bytes 1540
  54.1 53.2 %copy-start.44 = (f32[128]{0:T(128)}, f32[128]{0:T(128)S(1)}, u32[]{:S(2)}) copy-start(f32[128]{0:T(128)S(1)} %rsqrt.21) | copy-start | bytes 1540
  717.4 71.1 %reduce-scatter.14.cloned.1.call-start = ((), (), s32[]{:S(2)}) async-start(), calls=%async_computation.15 | async-start | bytes 589824 | tf_op jit(solution)/shard_map/reduce_scatter | solution.py:325
  724.6 235.9 %reduce-scatter.18.cloned.1.call-start = ((), (), s32[]{:S(2)}) async-start(), calls=%async_computation.17 | async-start | bytes 1622016 | tf_op jit(solution)/shard_map/reduce_scatter | solution.py:361
  754.7 36.3 %copy-start.36 = (f32[128,128]{0,1:T(8,128)S(1)}, f32[128,128]{0,1:T(8,128)}, u32[]{:S(2)}) copy-start(f32[128,128]{0,1:T(8,128)} %get-tuple-element.171) | copy-start | bytes 196612
  756.3 35.5 %copy-start.35 = (f32[128,128]{0,1:T(8,128)S(1)}, f32[128,128]{0,1:T(8,128)}, u32[]{:S(2)}) copy-start(f32[128,128]{0,1:T(8,128)} %get-tuple-element.170) | copy-start | bytes 196612
  756.3 35.6 %copy-start.5 = (bf16[2,2,384,512]{3,2,1,0:T(8,128)(2,1)S(1)}, bf16[2,2,384,512]{3,2,1,0:T(8,128)(2,1)}, u32[]{:S(2)}) copy-start(bf16[2,2,384,512]{3,2,1,0:T(8,128)(2,1)} %copy-done.4) | copy-start | bytes 4718596
  756.3 35.6 %copy-start.20 = (bf16[2,512,2,128]{3,1,2,0:T(8,128)(2,1)S(1)}, bf16[2,512,2,128]{3,1,2,0:T(8,128)(2,1)}, u32[]{:S(2)}) copy-start(bf16[2,512,2,128]{3,1,2,0:T(8,128)(2,1)} %copy.126) | copy-start | bytes 1572868
  756.3 234.8 %reduce-scatter.20.cloned.1.call-start = ((), (), s32[]{:S(2)}) async-start(), calls=%async_computation.18 | async-start | bytes 1622016 | tf_op jit(solution)/shard_map/reduce_scatter | solution.py:362
  791.0 341.0 %reduce-scatter.16.cloned.1.call-start = ((), (), s32[]{:S(2)}) async-start(), calls=%async_computation.16 | async-start | bytes 9732096 | tf_op jit(solution)/shard_map/reduce_scatter | solution.py:360
  800.3 473.7 %reduce-scatter.22.cloned.1.call-start = ((), (), s32[]{:S(2)}) async-start(), calls=%async_computation.19 | async-start | bytes 9732096 | tf_op jit(solution)/shard_map/reduce_scatter | solution.py:366
  806.6 936.6 %reduce-scatter.24.cloned.1.call-start = ((), (), s32[]{:S(2)}) async-start(), calls=%async_computation.20 | async-start | bytes 56770560 | tf_op jit(solution)/shard_map/reduce_scatter | solution.py:247
  831.0 1381.7 %reduce-scatter.26.cloned.1.call-start = ((), (), s32[]{:S(2)}) async-start(), calls=%async_computation.21 | async-start | bytes 56770560 | tf_op jit(solution)/shard_map/reduce_scatter | solution.py:250
  855.3 1825.8 %reduce-scatter.28.cloned.1.call-start = ((), (), s32[]{:S(2)}) async-start(), calls=%async_computation.22 | async-start | bytes 56770560
  (38 other events, 124.6 us)
Sparse Core Ops, SparseCore 0:
  10.9 66.4 all-gather.5
  80.3 65.5 all-gather.7
  148.9 164.7 all-gather.9
  316.4 164.0 all-gather.11
  483.3 164.0 all-gather.13
  717.5 33.4 reduce-scatter.11
  754.4 34.1 reduce-scatter.13
  794.4 94.7 reduce-scatter.17
  895.0 96.1 reduce-scatter.19
  997.5 134.4 reduce-scatter.15
  1139.4 134.5 reduce-scatter.21
  1280.9 462.2 reduce-scatter.23
  1751.3 461.3 reduce-scatter.25
  2219.6 461.3 reduce-scatter.27
where the time goes:
time: 2700 us; the launch traced here: 2690 us
  waiting for transfers between devices  2210 us (82%)
  matrix products  203 us (8%)
  blocking collectives  182 us (7%)
  local copies, waits for them, and re-layouts  55 us (2%)
    unnamed x15, waiting for transfers between devices  472 us
    reduce_scatter x1, waiting for transfers between devices, shards(): lax.psum_scatter(contract_rows(second_normed, up_grad), ('dp', 'seq'), sc...  470 us
    reduce_scatter x1, waiting for transfers between devices, shards(): lax.psum_scatter(contract_rows(second_normed, gate_grad), ('dp', 'seq'),...  469 us
    all_gather x1, waiting for transfers between devices, shards(): lax.all_gather(up_weight, ('dp', 'seq'), axis=0, tiled=True)  152 us
    all_gather x1, waiting for transfers between devices, shards(): lax.all_gather(down_weight, ('dp', 'seq'), axis=0, tiled=True)  152 us
    reduce_scatter x1, waiting for transfers between devices, shards(): lax.psum_scatter(output_weight_term, ('dp', 'seq'), scatter_dimension=0,...  142 us
    reduce_scatter x1, waiting for transfers between devices, shards(): lax.psum_scatter(query_weight_term, ('dp', 'seq'), scatter_dimension=0, t...  141 us
    all_gather x1, waiting for transfers between devices, shards(): lax.all_gather(gate_weight, ('dp', 'seq'), axis=0, tiled=True)  122 us
  transfers between devices with their start and end apart: 14, of which 11 were waited for; matrix products, arithmetic and copies ran while one was open for 7% of the time, Pallas kernels for 0%

commit v1 on v0

v1 whole, which is shorter than its diff:
```python
import math

import jax
import jax.numpy as jnp
from jax import lax
from jax.sharding import Mesh
from jax.sharding import PartitionSpec as P

H = 12
KV = 2
HD = 128
HPG = 6


epsilon = 1e-06
rope_base = 10000.0
masked_value = -1e30


def root_mean_square_scale(values):
    return lax.rsqrt(jnp.mean(values * values, axis=-1, keepdims=True) + epsilon)


def rope_tables(within):
    steps_even = jnp.arange(0, HD, 2).astype(jnp.float32)
    inverse = rope_base ** (-steps_even / HD)
    phase = within.astype(jnp.float32)[:, None] * inverse[None, :]
    phase = jnp.concatenate([phase, phase], axis=-1)
    return (jnp.cos(phase)[:, None, :], jnp.sin(phase)[:, None, :])


def rotate(values, cosine, sine):
    halfway = values.shape[-1] // 2
    return (
        values * cosine
        + jnp.concatenate([-values[..., halfway:], values[..., :halfway]], axis=-1) * sine
    )


def rotate_back(grads, cosine, sine):
    halfway = grads.shape[-1] // 2
    turned = grads * sine
    return grads * cosine + jnp.concatenate(
        [turned[..., halfway:], -turned[..., :halfway]], axis=-1
    )


def doc_tables(doc_ends, doc_lengths, positions):
    passed = doc_ends[:, None, :] <= positions[None, :, None]
    doc_index = jnp.sum(passed.astype(jnp.int32), axis=-1)
    starts = jnp.sum(jnp.where(passed, doc_lengths[:, None, :], 0), axis=-1)
    return (doc_index, positions[None, :] - starts)


def contract_rows(left, right):
    return lax.dot_general(
        left, right, (((0,), (0,)), ((), ())), preferred_element_type=jnp.float32
    )


def contract_cols(left, right):
    return lax.dot_general(
        left, right, (((1,), (1,)), ((), ())), preferred_element_type=jnp.float32
    )


def to_groups(flat_heads, local_rows, shard_tokens):
    shaped = flat_heads.reshape(local_rows, shard_tokens, KV, HPG, HD).transpose(0, 2, 3, 1, 4)
    return shaped.reshape(local_rows, KV, HPG * shard_tokens, HD)


def from_groups(grouped, local_rows, shard_tokens):
    shaped = grouped.reshape(local_rows, KV, HPG, shard_tokens, HD).transpose(0, 3, 1, 2, 4)
    return shaped.reshape(local_rows * shard_tokens, H * HD)


def swapped(values, axis):
    return lax.ppermute(values, axis, [(0, 1), (1, 0)])


def shifted(values, amount):
    count = lax.axis_size("z")
    return lax.ppermute(values, "z", [(i, (i + amount) % count) for i in range(count)])


def pick(values, index, axis):
    return lax.dynamic_index_in_dim(values, index, axis, keepdims=False)


def place(buffer, block, index):
    rest = buffer.ndim - len(index)
    lead = (1,) * len(index)
    shaped = block.reshape(lead + buffer.shape[len(index) :])
    return lax.dynamic_update_slice(buffer, shaped, tuple(index) + (0,) * rest)


def gather_group(rows):
    pieces = [rows] + [shifted(rows, k) for k in range(1, lax.axis_size("z"))]
    mine = jnp.concatenate(pieces, axis=0)
    return jnp.concatenate([mine, swapped(mine, "c")], axis=0)


def scatter_group(partial, count):
    half = partial.shape[0] // 2
    kept = partial[:half].astype(jnp.float32) + swapped(partial[half:], "c").astype(jnp.float32)
    blocks = kept.reshape((lax.axis_size("z"), count) + partial.shape[1:])
    total = blocks[0]
    for k in range(1, lax.axis_size("z")):
        total = total + shifted(blocks[k].astype(jnp.bfloat16), -k).astype(jnp.float32)
    return total


def gather_columns(gate_weight, up_weight):
    rows, hidden = gate_weight.shape
    nz, ny, nx, nc = (lax.axis_size(a) for a in ("z", "y", "x", "c"))
    z, y, x, c = (lax.axis_index(a) for a in ("z", "y", "x", "c"))
    unit = hidden // (nz * ny * nx * nc)
    wide = ny * nx * unit
    both = jnp.stack([gate_weight, up_weight]).reshape(2, rows, nz, ny, nx, nc, unit)
    both = both.transpose(5, 2, 0, 1, 3, 4, 6).reshape(nc, nz, 2, rows, wide)
    kept = pick(both, c, 0)
    came = swapped(pick(both, 1 - c, 0), "c")
    cores = jnp.where(c == 0, jnp.stack([kept, came]), jnp.stack([came, kept]))
    cores = cores.transpose(1, 2, 0, 3, 4)
    shares = jnp.zeros((2, nz, nc, rows, wide), both.dtype)
    for k in range(nz):
        piece = pick(cores, (z + k) % nz, 0)
        if k:
            piece = shifted(piece, k)
        shares = lax.dynamic_update_slice(shares, piece[:, None], (0, (z - k) % nz, 0, 0, 0))
    if ny != 2 or nx != 2:
        whole = lax.all_gather(shares, ("y", "x"), axis=2).reshape(2, -1, wide)
        return whole[0], whole[1]
    from_x = swapped(shares, "x")
    from_y = swapped(shares, "y")
    gate_far = swapped(from_x[0], "y")
    up_far = swapped(from_y[1], "x")
    whole = []
    for m, far in enumerate((gate_far, up_far)):
        buffer = jnp.zeros((nz, ny, nx, nc, rows, wide), both.dtype)
        for piece, at_y, at_x in (
            (shares[m], y, x),
            (from_x[m], y, 1 - x),
            (from_y[m], 1 - y, x),
            (far, 1 - y, 1 - x),
        ):
            buffer = lax.dynamic_update_slice(
                buffer, piece[:, None, None], (0, at_y, at_x, 0, 0, 0)
            )
        whole.append(buffer.reshape(-1, wide))
    return whole[0], whole[1]


def scatter_columns(gate_grad, up_grad, rows):
    wide = gate_grad.shape[1]
    nz, ny, nx, nc = (lax.axis_size(a) for a in ("z", "y", "x", "c"))
    z, y, x, c = (lax.axis_index(a) for a in ("z", "y", "x", "c"))
    if ny != 2 or nx != 2:
        both = jnp.stack([gate_grad, up_grad]).reshape(2, nz, ny * nx, nc, rows, wide)
        both = lax.psum_scatter(both, ("y", "x"), scatter_dimension=2, tiled=False)
    else:
        sums = []
        for grad, order in ((gate_grad, "yx"), (up_grad, "xy")):
            left = grad.reshape(nz, ny, nx, nc, rows, wide)
            for axis in order:
                at = lax.axis_index(axis)
                dim = 1 if axis == "y" or left.ndim == 5 else 2
                came = swapped(pick(left, 1 - at, dim), axis)
                left = (
                    pick(left, at, dim).astype(jnp.float32) + came.astype(jnp.float32)
                ).astype(jnp.bfloat16)
            sums.append(left)
        both = jnp.stack(sums)
    kept = pick(both, c, 2)
    came = swapped(pick(both, 1 - c, 2), "c")
    cores = jnp.where(c == 0, jnp.stack([kept, came]), jnp.stack([came, kept]))
    cores = cores.transpose(2, 0, 1, 3, 4)
    shares = jnp.zeros((nz, nc, 2, rows, wide), both.dtype)
    for k in range(nz):
        piece = pick(cores, (z + k) % nz, 0)
        if k:
            piece = shifted(piece, k)
        shares = place(shares, piece, ((z - k) % nz,))
    unit = wide // (ny * nx)
    shares = shares.reshape(nz, nc, 2, rows, ny, nx, unit).transpose(2, 3, 0, 4, 5, 1, 6)
    shares = shares.reshape(2, rows, -1).astype(jnp.float32)
    return shares[0], shares[1]


def gather_rows(down_weight):
    rows, width = down_weight.shape
    ny, nx = (lax.axis_size(a) for a in ("y", "x"))
    y, x = (lax.axis_index(a) for a in ("y", "x"))
    if ny != 2 or nx != 2:
        return lax.all_gather(down_weight, ("y", "x"), axis=0, tiled=True)
    cut = rows // 32 * 16
    from_x = swapped(down_weight, "x")
    from_y = swapped(down_weight, "y")
    far = jnp.concatenate([swapped(from_x[:cut], "y"), swapped(from_y[cut:], "x")], axis=0)
    buffer = jnp.zeros((ny, nx, rows, width), down_weight.dtype)
    buffer = place(buffer, down_weight, (y, x))
    buffer = place(buffer, from_x, (y, 1 - x))
    buffer = place(buffer, from_y, (1 - y, x))
    buffer = place(buffer, far, (1 - y, 1 - x))
    return buffer.reshape(-1, width)


def scatter_rows(down_grad, rows):
    width = down_grad.shape[1]
    ny, nx = (lax.axis_size(a) for a in ("y", "x"))
    if ny != 2 or nx != 2:
        return lax.psum_scatter(down_grad, ("y", "x"), scatter_dimension=0, tiled=True)
    cut = rows // 32 * 16
    shaped = down_grad.reshape(ny, nx, rows, width)
    sums = []
    for part, order in ((shaped[:, :, :cut], "yx"), (shaped[:, :, cut:], "xy")):
        left = part
        for axis in order:
            at = lax.axis_index(axis)
            dim = 0 if axis == "y" or left.ndim == 3 else 1
            came = swapped(pick(left, 1 - at, dim), axis)
            left = pick(left, at, dim).astype(jnp.float32) + came.astype(jnp.float32)
            if left.ndim == 3:
                left = left.astype(jnp.bfloat16)
        sums.append(left)
    return jnp.concatenate(sums, axis=0)


def column_pack(columns, rows):
    padded = [jnp.pad(v, (0, rows - v.shape[0])) for v in columns]
    packed = jnp.stack(padded, axis=1)
    return jnp.pad(packed, ((0, 0), (0, 128 - len(columns))))


EVERY = ("z", "y", "x", "c")
ROW = ("y", "x", "c")


def shards(
    tokens,
    doc_lengths,
    query_weight,
    key_weight,
    value_weight,
    query_bias,
    key_bias,
    value_bias,
    output_weight,
    attention_norm_gain,
    feedforward_norm_gain,
    gate_weight,
    up_weight,
    down_weight,
    cotangent,
):
    local_rows, shard_tokens, width = tokens.shape
    devices = lax.axis_size(EVERY)
    row_length = shard_tokens * lax.axis_size(ROW)
    flat_count = local_rows * shard_tokens
    scaling = 1.0 / math.sqrt(HD)
    owned = query_weight.shape[0]
    query_width = query_weight.shape[1]
    key_width = key_weight.shape[1]
    owned_key = key_bias.shape[0]
    vectors = column_pack(
        (
            query_bias,
            attention_norm_gain,
            feedforward_norm_gain,
            jnp.concatenate([key_bias, value_bias]),
        ),
        owned,
    )
    packed = jnp.concatenate([query_weight, key_weight, value_weight, vectors], axis=1)
    packed = lax.all_gather(packed, EVERY, axis=0, tiled=True)
    weight_output = lax.all_gather(output_weight, EVERY, axis=0, tiled=True)
    projections = packed[:, : query_width + 2 * key_width]
    lines = packed[:, query_width + 2 * key_width :].T[:4].astype(jnp.float32)
    bias_query, input_gain, post_gain = lines[0], lines[1], lines[2]
    small = lines[3].reshape(devices, owned)
    bias_key = small[:, :owned_key].reshape(-1)
    bias_value = small[:, owned_key : 2 * owned_key].reshape(-1)
    bias_all = jnp.concatenate([bias_query, bias_key, bias_value])

    weight_gate, weight_up = gather_columns(gate_weight, up_weight)
    weight_down = gather_rows(down_weight)
    upstream = cotangent.reshape(flat_count, width)
    upstream_group = gather_group(upstream)

    local_pos = lax.axis_index(ROW) * shard_tokens + jnp.arange(shard_tokens, dtype=jnp.int32)
    all_pos = jnp.arange(row_length, dtype=jnp.int32)
    doc_ends = jnp.cumsum(doc_lengths, axis=1)
    query_doc, query_within = doc_tables(doc_ends, doc_lengths, local_pos)
    key_doc, unused_within = doc_tables(doc_ends, doc_lengths, all_pos)
    cosine, sine = rope_tables(query_within.reshape(flat_count))
    flattened_input = tokens.reshape(flat_count, width).astype(jnp.float32)
    first_inverse_norm = root_mean_square_scale(flattened_input)
    first_normalized = flattened_input * first_inverse_norm
    first_normed = (first_normalized * input_gain).astype(jnp.bfloat16)
    pre = jnp.dot(first_normed, projections, preferred_element_type=jnp.float32) + bias_all
    queries = rotate(pre[:, :query_width].reshape(flat_count, H, HD), cosine, sine).astype(
        jnp.bfloat16
    )
    key_pre = pre[:, query_width : query_width + key_width]
    key_rows = rotate(key_pre.reshape(flat_count, KV, HD), cosine, sine).astype(jnp.bfloat16)
    value_rows = pre[:, query_width + key_width :].astype(jnp.bfloat16)
    both_rows = jnp.concatenate([key_rows.reshape(flat_count, key_width), value_rows], axis=1)
    both_rows = lax.all_gather(
        both_rows.reshape(local_rows, shard_tokens, 2 * key_width), ROW, axis=1, tiled=True
    )
    both_heads = both_rows.reshape(local_rows, row_length, 2, KV, HD).transpose(2, 0, 3, 1, 4)
    key_heads, value_heads = both_heads[0], both_heads[1]
    query_groups = to_groups(queries.reshape(flat_count, H * HD), local_rows, shard_tokens)
    query_doc_rows = jnp.tile(query_doc, (1, HPG))
    query_pos_rows = jnp.tile(local_pos, (HPG,))
    scores = (
        jnp.einsum("rgmd,rgkd->rgmk", query_groups, key_heads, preferred_element_type=jnp.float32)
        * scaling
    )
    allowed = (query_doc_rows[:, None, :, None] == key_doc[:, None, None, :]) & (
        all_pos[None, None, None, :] <= query_pos_rows[None, None, :, None]
    )
    scores = jnp.where(allowed, scores, masked_value)
    row_top = jnp.max(scores, axis=-1, keepdims=True)
    log_total = row_top + jnp.log(jnp.sum(jnp.exp(scores - row_top), axis=-1, keepdims=True))
    probs = jnp.exp(scores - log_total)
    probs_low = probs.astype(jnp.bfloat16)
    mixed = jnp.einsum(
        "rgmk,rgkd->rgmd", probs_low, value_heads, preferred_element_type=jnp.float32
    )
    attended = from_groups(mixed, local_rows, shard_tokens).astype(jnp.bfloat16)
    first_hidden = flattened_input + jnp.dot(
        attended, weight_output, preferred_element_type=jnp.float32
    )
    second_inverse_norm = root_mean_square_scale(first_hidden)
    second_normalized = first_hidden * second_inverse_norm
    second_normed = (second_normalized * post_gain).astype(jnp.bfloat16)

    second_group = gather_group(second_normed)
    gate_pre = jnp.dot(second_group, weight_gate, preferred_element_type=jnp.float32)
    up_pre = jnp.dot(second_group, weight_up, preferred_element_type=jnp.float32)
    sigmoid_gate = jax.nn.sigmoid(gate_pre)
    silu_gate = gate_pre * sigmoid_gate
    hidden = (silu_gate * up_pre).astype(jnp.bfloat16)
    hidden_grad = contract_cols(upstream_group, weight_down)
    gate_grad = (
        hidden_grad * up_pre * sigmoid_gate * (1.0 + gate_pre * (1.0 - sigmoid_gate))
    ).astype(jnp.bfloat16)
    up_grad = (hidden_grad * silu_gate).astype(jnp.bfloat16)
    normed_partial = (
        contract_cols(gate_grad, weight_gate) + contract_cols(up_grad, weight_up)
    ).astype(jnp.bfloat16)
    second_normed_grad = scatter_group(normed_partial, flat_count)
    output_partial = jnp.dot(hidden, weight_down, preferred_element_type=jnp.float32)
    mlp_out = scatter_group(output_partial.astype(jnp.bfloat16), flat_count)
    layer_output = (first_hidden + mlp_out).astype(jnp.bfloat16)
    gate_sum, up_sum = scatter_columns(
        contract_rows(second_group, gate_grad).astype(jnp.bfloat16),
        contract_rows(second_group, up_grad).astype(jnp.bfloat16),
        owned,
    )
    down_sum = scatter_rows(
        contract_rows(hidden, upstream_group).astype(jnp.bfloat16), down_weight.shape[0]
    ).astype(jnp.float32)

    post_gain_term = jnp.sum(second_normed_grad * second_normalized, axis=0)
    second_scaled = second_normed_grad * post_gain
    hidden_one_grad = upstream.astype(jnp.float32) + second_inverse_norm * (
        second_scaled
        - second_normalized * jnp.mean(second_scaled * second_normalized, axis=-1, keepdims=True)
    )
    proj_grad = hidden_one_grad.astype(jnp.bfloat16)
    output_term = contract_rows(attended, proj_grad).astype(jnp.bfloat16)
    attended_grad = contract_cols(proj_grad, weight_output).astype(jnp.bfloat16)
    grad_groups = to_groups(attended_grad, local_rows, shard_tokens)
    prob_grad = jnp.einsum(
        "rgmd,rgkd->rgmk", grad_groups, value_heads, preferred_element_type=jnp.float32
    )
    prob_delta = jnp.sum(probs * prob_grad, axis=-1, keepdims=True)
    score_grad = (probs * (prob_grad - prob_delta)).astype(jnp.bfloat16)
    query_sum = jnp.einsum(
        "rgmk,rgkd->rgmd", score_grad, key_heads, preferred_element_type=jnp.float32
    )
    key_part = jnp.einsum(
        "rgmk,rgmd->rkgd", score_grad, query_groups, preferred_element_type=jnp.float32
    )
    value_part = jnp.einsum(
        "rgmk,rgmd->rkgd", probs_low, grad_groups, preferred_element_type=jnp.float32
    )
    both_terms = jnp.concatenate(
        [
            (key_part * scaling).reshape(local_rows, row_length, key_width),
            value_part.reshape(local_rows, row_length, key_width),
        ],
        axis=2,
    ).astype(jnp.bfloat16)
    both_sums = lax.psum_scatter(both_terms, ROW, scatter_dimension=1, tiled=True)
    both_sums = both_sums.reshape(flat_count, 2 * key_width).astype(jnp.float32)
    queries_grad = from_groups(query_sum, local_rows, shard_tokens) * scaling
    query_grad = (
        rotate_back(queries_grad.reshape(flat_count, H, HD), cosine, sine)
        .reshape(flat_count, H * HD)
        .astype(jnp.bfloat16)
    )
    key_grad = (
        rotate_back(both_sums[:, :key_width].reshape(flat_count, KV, HD), cosine, sine)
        .reshape(flat_count, key_width)
        .astype(jnp.bfloat16)
    )
    value_grad = both_sums[:, key_width:].astype(jnp.bfloat16)
    pair_grad = jnp.concatenate([key_grad, value_grad], axis=1)
    query_term = contract_rows(first_normed, query_grad).astype(jnp.bfloat16)
    pair_term = contract_rows(first_normed, pair_grad).astype(jnp.bfloat16)
    query_bias_term = jnp.sum(query_grad.astype(jnp.float32), axis=0)
    pair_bias_term = jnp.sum(pair_grad.astype(jnp.float32), axis=0)
    first_normed_grad = contract_cols(query_grad, projections[:, :query_width]) + contract_cols(
        pair_grad, projections[:, query_width:]
    )
    input_gain_term = jnp.sum(first_normed_grad * first_normalized, axis=0)
    first_scaled = first_normed_grad * input_gain
    input_grad = hidden_one_grad + first_inverse_norm * (
        first_scaled
        - first_normalized * jnp.mean(first_scaled * first_normalized, axis=-1, keepdims=True)
    )
    small_terms = jnp.concatenate(
        [
            pair_bias_term[:key_width].reshape(devices, owned_key),
            pair_bias_term[key_width:].reshape(devices, owned_key),
            jnp.zeros((devices, owned - 2 * owned_key), jnp.float32),
        ],
        axis=1,
    ).reshape(-1)
    vector_terms = column_pack(
        (query_bias_term, input_gain_term, post_gain_term, small_terms), width
    ).astype(jnp.bfloat16)
    output_sum = lax.psum_scatter(output_term, EVERY, scatter_dimension=0, tiled=True)
    query_sum_out = lax.psum_scatter(query_term, EVERY, scatter_dimension=0, tiled=True)
    last = lax.psum_scatter(
        jnp.concatenate([pair_term, vector_terms], axis=1), EVERY, scatter_dimension=0, tiled=True
    ).astype(jnp.float32)
    vector_sums = last[:, 2 * key_width :]
    return (
        layer_output.reshape(local_rows, shard_tokens, width),
        input_grad.astype(jnp.bfloat16).reshape(local_rows, shard_tokens, width),
        query_sum_out.astype(jnp.float32),
        last[:, :key_width],
        last[:, key_width : 2 * key_width],
        vector_sums[:, 0],
        vector_sums[:owned_key, 3],
        vector_sums[owned_key : 2 * owned_key, 3],
        output_sum.astype(jnp.float32),
        vector_sums[:, 1],
        vector_sums[:, 2],
        gate_sum,
        up_sum,
        down_sum,
    )


def solution(mesh):
    depth, across = mesh.devices.shape
    plane = across // 2
    side = math.isqrt(plane)
    inner = Mesh(mesh.devices.reshape(depth, plane // side, side, 2), EVERY)
    over_rows = P("z", ROW, None)
    whole, flat = P(EVERY, None), P(EVERY)
    in_specs = (
        (over_rows, P("z", None))
        + (whole,) * 3
        + (flat,) * 3
        + (whole, flat, flat)
        + (whole,) * 3
        + (over_rows,)
    )
    out_specs = (
        (over_rows,) * 2 + (whole,) * 3 + (flat,) * 3 + (whole, flat, flat) + (whole,) * 3
    )
    return jax.shard_map(
        shards, mesh=inner, in_specs=in_specs, out_specs=out_specs, check_vma=False
    )
```

time: 2700 us -> 835 us (0.31)
  waiting for transfers between devices: 2210 us -> 491 us
  blocking collectives: 182 us -> 0 us
  matrix products: 203 us -> 91.3 us
  local copies, waits for them, and re-layouts: 55 us -> 131 us
  starting transfers between devices: 1.14 us -> 36.3 us
  other arithmetic: 23.3 us -> 56.7 us
    reduce_scatter x8 -> x3, waiting for transfers between devices: 1310 us -> 153 us  [the longest x1 111 us: shards(): lax.psum_scatter(query_term, EVERY, scatter_dimension=0, tiled=True)]
    unnamed x15 -> x8, waiting for transfers between devices: 472 us -> 0.12 us
    all_gather x5 -> x3, waiting for transfers between devices: 426 us -> 67.2 us  [the longest x1 67.2 us: shards(): packed = lax.all_gather(packed, EVERY, axis=0, tiled=True)]
    ppermute x0 -> x40, waiting for transfers between devices: none -> 271 us  [the longest x18 178 us: shifted(): lax.ppermute(values, 'z', [(i, (i + amount) % count) for i in range(count)])]
    all_gather x4 -> x0, blocking collectives: 104 us -> none  [the longest x1 41.5 us: shards(): lax.all_gather(key_weight, ('dp', 'seq'), axis=0, tiled=True)]
    unnamed x2 -> x0, blocking collectives: 78 us -> none
    dot_general x7 -> x6, matrix products: 81.6 us -> 26.7 us  [contract_rows(): lax.dot_general(left, right, (((0,), (0,)), ((), ())), preferred_element_...]
    ppermute x0 -> x40, starting transfers between devices: none -> 35.6 us  [the longest x22 19.6 us: swapped(): return lax.ppermute(values, axis, [(0, 1), (1, 0)])]
  transfers between devices with their start and end apart: 14 -> 47, of which waited for: 11 -> 19; matrix products, arithmetic and copies ran while one was open for 7% -> 24% of each run, Pallas kernels for 0% -> 0%
where the time goes in v1:
time: 835 us; the launch traced here: 823 us
  waiting for transfers between devices  491 us (59%)
  local copies, waits for them, and re-layouts  131 us (16%)
  matrix products  91.3 us (11%)
  other arithmetic  56.7 us (7%)
  starting transfers between devices  36.3 us (4%)
  between operations  16.5 us (2%)
    ppermute x18, waiting for transfers between devices, shifted(): lax.ppermute(values, 'z', [(i, (i + amount) % count) for i in range(count)])  178 us
    reduce_scatter x1, waiting for transfers between devices, shards(): lax.psum_scatter(query_term, EVERY, scatter_dimension=0, tiled=True)  111 us
    ppermute x22, waiting for transfers between devices, swapped(): return lax.ppermute(values, axis, [(0, 1), (1, 0)])  92.7 us
    all_gather x1, waiting for transfers between devices, shards(): packed = lax.all_gather(packed, EVERY, axis=0, tiled=True)  67.2 us
    reduce_scatter x1, waiting for transfers between devices, shards(): lax.psum_scatter(both_terms, ROW, scatter_dimension=1, tiled=True)  32.2 us
    dot_general x6, matrix products, contract_cols(): lax.dot_general(left, right, (((1,), (1,)), ((), ())), preferred_element_...  28 us
    dot_general x6, matrix products, contract_rows(): lax.dot_general(left, right, (((0,), (0,)), ((), ())), preferred_element_...  26.7 us
    unnamed x182, local copies, waits for them, and re-layouts  22.2 us
  transfers between devices with their start and end apart: 47, of which 19 were waited for; matrix products, arithmetic and copies ran while one was open for 24% of the time, Pallas kernels for 0%

profile of v1, /device:TPU:29, one launch (start us, length us, event | category | flops | bytes accessed | tf_op | source)
XLA Modules:
  0.0 822.7 jit_solution(10706799105881004842)
XLA Ops:
  15.3 67.2 %all-gather.4.cloned.1.call-done = bf16[1536,2176]{1,0:T(8,128)(2,1)} async-done(((bf16[48,2176]{1,0:T(8,128)(2,1)}), bf16[1536,2176]{1,0:T(8,128)(2,1)}) %all-gather.4.cloned.1.call-update) | async-done | bytes 6684688 | tf_op jit(solution)/shard_map/all_gather | solution.py:275
  123.5 5.4 collective-permute-done.21
  148.1 34.9 %collective-permute-done.6 = bf16[2,2,48,1120]{3,2,0,1:T(8,128)(2,1)S(1)} collective-permute-done((bf16[2,2,48,1120]{3,2,0,1:T(8,128)(2,1)S(1)}, bf16[2,2,48,1120]{3,2,0,1:T(8,128)(2,1)S(1)}, u32[]{:S(2)}, u32[]{:S(2)}) %collective-permute-start.6) | collective-permute-done | bytes 430112 | tf_op jit(solution)/shard_map/ppermute | solution.py:83
  185.7 5.3 fusion.81
  191.0 40.1 %collective-permute-done.8 = bf16[2,4,2,48,1120]{4,3,2,1,0:T(8,128)(2,1)S(1)} collective-permute-done((bf16[2,4,2,48,1120]{4,3,2,1,0:T(8,128)(2,1)S(1)}, bf16[2,4,2,48,1120]{4,3,2,1,0:T(8,128)(2,1)S(1)}, u32[]{:S(2)}, u32[]{:S(2)}) %collective-permute-start.8) | collective-permute-done | bytes 1720352 | tf_op jit(solution)/shard_map/ppermute | solution.py:78
  270.7 25.2 %collective-permute-done.1 = bf16[128,1536]{1,0:T(8,128)(2,1)S(1)} collective-permute-done((bf16[128,1536]{1,0:T(8,128)(2,1)S(1)}, bf16[128,1536]{1,0:T(8,128)(2,1)S(1)}, u32[]{:S(2)}, u32[]{:S(2)}) %collective-permute-start.1) | collective-permute-done | bytes 393248 | tf_op jit(solution)/shard_map/ppermute | solution.py:83
  302.4 5.4 fusion.80
  307.8 10.0 %multiply_convert_fusion.1 = (bf16[1024,1120]{0,1:T(8,128)(2,1)}, bf16[1024,1120]{0,1:T(8,128)(2,1)}, bf16[1024,1120]{0,1:T(8,128)(2,1)}) fusion(f32[1024,1120]{0,1:T(8,128)} %fusion.81, f32[1024,1120]{0,1:T(8,128)} %fusion.80, bf16[1024,1536]{1,0:T(8,128)(2,1)S(1)} %constant_dynamic-update-slice_fusion, bf16[1536,1120]{1,0:T(8,128)(2,1)S(1)} %bitcast.322), kind=kOutput, calls=%fused_computation.11 | convolution fusion | flops 3540418560 | bytes 22642688 | tf_op jit(solution)/shard_map/dot_general | solution.py:340
  317.9 6.0 fusion.82
  323.8 6.5 add_convert_fusion
  364.3 16.1 %collective-permute-done.26 = bf16[128,1536]{1,0:T(8,128)(2,1)S(1)} collective-permute-done((bf16[128,1536]{1,0:T(8,128)(2,1)S(1)}, bf16[128,1536]{1,0:T(8,128)(2,1)S(1)}, u32[]{:S(2)}, u32[]{:S(2)}) %collective-permute-start.26) | collective-permute-done | bytes 393248 | tf_op jit(solution)/shard_map/ppermute | solution.py:83
  381.3 8.3 %collective-permute-done.17 = bf16[128,1536]{1,0:T(8,128)(2,1)S(1)} collective-permute-done((bf16[128,1536]{1,0:T(8,128)(2,1)S(1)}, bf16[128,1536]{1,0:T(8,128)(2,1)S(1)}, u32[]{:S(2)}, u32[]{:S(2)}) %collective-permute-start.17) | collective-permute-done | bytes 393248 | tf_op jit(solution)/shard_map/ppermute | solution.py:83
  389.6 24.4 %collective-permute-done.18 = bf16[128,1536]{1,0:T(8,128)(2,1)S(1)} collective-permute-done((bf16[128,1536]{1,0:T(8,128)(2,1)S(1)}, bf16[128,1536]{1,0:T(8,128)(2,1)S(1)}, u32[]{:S(2)}, u32[]{:S(2)}) %collective-permute-start.18) | collective-permute-done | bytes 393248 | tf_op jit(solution)/shard_map/ppermute | solution.py:83
  442.4 32.2 %reduce-scatter.7.cloned.1.call-done = bf16[2,64,512]{2,1,0:T(8,128)(2,1)} async-done(((bf16[2,512,512]{2,1,0:T(8,128)(2,1)}), bf16[2,64,512]{2,1,0:T(8,128)(2,1)}) %reduce-scatter.7.cloned.1.call-update) | async-done | bytes 131088 | tf_op jit(solution)/shard_map/reduce_scatter | solution.py:397
  486.3 6.3 convolution_convert_fusion.2
  504.0 5.2 convolution_convert_fusion
  535.1 32.6 %collective-permute-done.30 = bf16[4,2,2,48,1120]{4,3,2,0,1:T(8,128)(2,1)} collective-permute-done((bf16[4,2,2,48,1120]{4,3,2,0,1:T(8,128)(2,1)}, bf16[4,2,2,48,1120]{4,3,2,0,1:T(8,128)(2,1)}, u32[]{:S(2)}, u32[]{:S(2)}) %collective-permute-start.30) | collective-permute-done | bytes 1720352 | tf_op jit(solution)/shard_map/ppermute | solution.py:78
  581.8 19.4 %collective-permute-done.31 = bf16[4,2,48,1120]{3,2,1,0:T(8,128)(2,1)} collective-permute-done((bf16[4,2,48,1120]{3,2,1,0:T(8,128)(2,1)}, bf16[4,2,48,1120]{3,2,1,0:T(8,128)(2,1)}, u32[]{:S(2)}, u32[]{:S(2)}) %collective-permute-start.31) | collective-permute-done | bytes 860192 | tf_op jit(solution)/shard_map/ppermute | solution.py:78
  613.9 8.7 %collective-permute-done.33 = bf16[2,2,48,1120]{3,2,1,0:T(8,128)(2,1)S(1)} collective-permute-done((bf16[2,2,48,1120]{3,2,1,0:T(8,128)(2,1)S(1)}, bf16[2,2,48,1120]{3,2,1,0:T(8,128)(2,1)S(1)}, u32[]{:S(2)}, u32[]{:S(2)}) %collective-permute-start.33) | collective-permute-done | bytes 430112 | tf_op jit(solution)/shard_map/ppermute | solution.py:83
  622.7 41.0 %collective-permute-done.34 = bf16[2,2,48,1120]{3,2,1,0:T(8,128)(2,1)S(1)} collective-permute-done((bf16[2,2,48,1120]{3,2,1,0:T(8,128)(2,1)S(1)}, bf16[2,2,48,1120]{3,2,1,0:T(8,128)(2,1)S(1)}, u32[]{:S(2)}, u32[]{:S(2)}) %collective-permute-start.34) | collective-permute-done | bytes 430112 | tf_op jit(solution)/shard_map/ppermute | solution.py:83
  663.8 5.7 reshape.518
  669.6 5.6 fusion.72
  691.5 9.7 %reduce-scatter.11.cloned.1.call-done = bf16[48,1536]{1,0:T(8,128)(2,1)} async-done(((bf16[1536,1536]{1,0:T(8,128)(2,1)}), bf16[48,1536]{1,0:T(8,128)(2,1)}) %reduce-scatter.11.cloned.1.call-update) | async-done | bytes 147472 | tf_op jit(solution)/shard_map/reduce_scatter | solution.py:436
  702.9 110.9 %reduce-scatter.9.cloned.1.call-done = bf16[48,1536]{1,0:T(8,128)(2,1)} async-done(((bf16[1536,1536]{1,0:T(8,128)(2,1)}), bf16[48,1536]{1,0:T(8,128)(2,1)}) %reduce-scatter.9.cloned.1.call-update) | async-done | bytes 147472 | tf_op jit(solution)/shard_map/reduce_scatter | solution.py:437
  (474 shorter events, 274.0 us)
Async XLA Ops:
  7.2 75.4 %all-gather.4.cloned.1.call-start = ((), (), s32[]{:S(2)}) async-start(), calls=%async_computation.4 | async-start | bytes 6893568 | tf_op jit(solution)/shard_map/all_gather | solution.py:275
  10.5 235.8 %all-gather.6.cloned.1.call-start = ((), (), s32[]{:S(2)}) async-start(), calls=%async_computation.5 | async-start | bytes 1179648 | tf_op jit(solution)/shard_map/all_gather | solution.py:308
  91.3 166.2 %all-gather.8.cloned.1.call-start = ((), (), s32[]{:S(2)}) async-start(), calls=%async_computation.6 | async-start | bytes 4866048 | tf_op jit(solution)/shard_map/all_gather | solution.py:276
  91.4 47.7 %collective-permute-start.12 = (bf16[280,1536]{1,0:T(8,128)(2,1)}, bf16[280,1536]{1,0:T(8,128)(2,1)}, u32[]{:S(2)}, u32[]{:S(2)}) collective-permute-start(bf16[280,1536]{1,0:T(8,128)(2,1)} %param.28), channel_id=1, source_target_pairs={{0,2},{2,0},{1,3},{3,1},{4,6},{6,4},{5,7},{7,5},{8,10},{10,8},{9,1... | collective-permute-start | bytes 2580488 | tf_op jit(solution)/shard_map/ppermute | solution.py:78
  91.7 44.8 %collective-permute-start.13 = (bf16[280,1536]{1,0:T(8,128)(2,1)}, bf16[280,1536]{1,0:T(8,128)(2,1)}, u32[]{:S(2)}, u32[]{:S(2)}) collective-permute-start(bf16[280,1536]{1,0:T(8,128)(2,1)} %param.28), channel_id=1, source_target_pairs={{0,4},{4,0},{1,5},{5,1},{2,6},{6,2},{3,7},{7,3},{8,12},{12,8},{9,1... | collective-permute-start | bytes 2580488 | tf_op jit(solution)/shard_map/ppermute | solution.py:78
  96.1 378.5 %reduce-scatter.7.cloned.1.call-start = ((), (), s32[]{:S(2)}) async-start(), calls=%async_computation.7 | async-start | bytes 1179648 | tf_op jit(solution)/shard_map/reduce_scatter | solution.py:397
  130.2 55.4 %collective-permute-start.23 = (bf16[512,1536]{1,0:T(8,128)(2,1)S(1)}, bf16[512,1536]{1,0:T(8,128)(2,1)S(1)}, u32[]{:S(2)}, u32[]{:S(2)}) collective-permute-start(bf16[512,1536]{1,0:T(8,128)(2,1)S(1)} %pad_maximum_fusion.3), channel_id=1, source_target_pairs={{0,1},{1,0},{2,3},{3,2},{4,5},{5,4},{6,7},{7,6},{8,9},{9,8},{10,11... | collective-permute-start | bytes 4718600 | tf_op jit(solution)/shard_map/ppermute | solution.py:78
  134.7 48.2 %collective-permute-start.6 = (bf16[2,2,48,1120]{3,2,0,1:T(8,128)(2,1)S(1)}, bf16[2,2,48,1120]{3,2,0,1:T(8,128)(2,1)S(1)}, u32[]{:S(2)}, u32[]{:S(2)}) collective-permute-start(bf16[2,2,48,1120]{3,2,0,1:T(8,128)(2,1)S(1)} %get-tuple-element.120), channel_id=1, source_target_pairs={{0,16},{8,24},{16,0},{24,8},{1,17},{9,25},{17,1},{25,9},{2,18},{10... | collective-permute-start | bytes 1290248 | tf_op jit(solution)/shard_map/ppermute | solution.py:83
  136.5 46.5 %collective-permute-start.7 = (bf16[2,2,48,1120]{3,2,0,1:T(8,128)(2,1)S(1)}, bf16[2,2,48,1120]{3,2,0,1:T(8,128)(2,1)S(1)}, u32[]{:S(2)}, u32[]{:S(2)}) collective-permute-start(bf16[2,2,48,1120]{3,2,0,1:T(8,128)(2,1)S(1)} %get-tuple-element.119), channel_id=1, source_target_pairs={{0,24},{8,0},{16,8},{24,16},{1,25},{9,1},{17,9},{25,17},{2,26},{10... | collective-permute-start | bytes 1290248 | tf_op jit(solution)/shard_map/ppermute | solution.py:83
  139.1 46.4 %collective-permute-start.15 = (bf16[152,1536]{1,0:T(8,128)(2,1)S(1)}, bf16[152,1536]{1,0:T(8,128)(2,1)S(1)}, u32[]{:S(2)}, u32[]{:S(2)}) collective-permute-start(bf16[152,1536]{1,0:T(8,128)(2,1)S(1)} %slice.311), channel_id=1, source_target_pairs={{0,2},{2,0},{1,3},{3,1},{4,6},{6,4},{5,7},{7,5},{8,10},{10,8},{9,1... | collective-permute-start | bytes 1400840 | tf_op jit(solution)/shard_map/ppermute | solution.py:78
  183.0 48.1 %collective-permute-start.8 = (bf16[2,4,2,48,1120]{4,3,2,1,0:T(8,128)(2,1)S(1)}, bf16[2,4,2,48,1120]{4,3,2,1,0:T(8,128)(2,1)S(1)}, u32[]{:S(2)}, u32[]{:S(2)}) collective-permute-start(bf16[2,4,2,48,1120]{4,3,2,1,0:T(8,128)(2,1)S(1)} %copy_dynamic-update-slice_fusion), channel_id=1, source_target_pairs={{0,2},{2,0},{1,3},{3,1},{4,6},{6,4},{5,7},{7,5},{8,10},{10,8},{9,1... | collective-permute-start | bytes 5160968 | tf_op jit(solution)/shard_map/ppermute | solution.py:78
  183.8 48.6 %collective-permute-start.9 = (bf16[2,4,2,48,1120]{4,3,2,1,0:T(8,128)(2,1)S(1)}, bf16[2,4,2,48,1120]{4,3,2,1,0:T(8,128)(2,1)S(1)}, u32[]{:S(2)}, u32[]{:S(2)}) collective-permute-start(bf16[2,4,2,48,1120]{4,3,2,1,0:T(8,128)(2,1)S(1)} %copy_dynamic-update-slice_fusion), channel_id=1, source_target_pairs={{0,4},{4,0},{1,5},{5,1},{2,6},{6,2},{3,7},{7,3},{8,12},{12,8},{9,1... | collective-permute-start | bytes 5160968 | tf_op jit(solution)/shard_map/ppermute | solution.py:78
  232.2 66.5 %collective-permute-start.10 = (bf16[4,2,48,1120]{3,2,1,0:T(8,128)(2,1)}, bf16[4,2,48,1120]{3,2,1,0:T(8,128)(2,1)}, u32[]{:S(2)}, u32[]{:S(2)}) collective-permute-start(bf16[4,2,48,1120]{3,2,1,0:T(8,128)(2,1)} %slice_bitcast_fusion.5), channel_id=1, source_target_pairs={{0,4},{4,0},{1,5},{5,1},{2,6},{6,2},{3,7},{7,3},{8,12},{12,8},{9,1... | collective-permute-start | bytes 2580488 | tf_op jit(solution)/shard_map/ppermute | solution.py:78
  233.5 67.3 %collective-permute-start.11 = (bf16[4,2,48,1120]{3,2,1,0:T(8,128)(2,1)}, bf16[4,2,48,1120]{3,2,1,0:T(8,128)(2,1)}, u32[]{:S(2)}, u32[]{:S(2)}) collective-permute-start(bf16[4,2,48,1120]{3,2,1,0:T(8,128)(2,1)} %slice_bitcast_fusion.4), channel_id=1, source_target_pairs={{0,2},{2,0},{1,3},{3,1},{4,6},{6,4},{5,7},{7,5},{8,10},{10,8},{9,1... | collective-permute-start | bytes 2580488 | tf_op jit(solution)/shard_map/ppermute | solution.py:78
  358.2 55.8 %collective-permute-start.18 = (bf16[128,1536]{1,0:T(8,128)(2,1)S(1)}, bf16[128,1536]{1,0:T(8,128)(2,1)S(1)}, u32[]{:S(2)}, u32[]{:S(2)}) collective-permute-start(bf16[128,1536]{1,0:T(8,128)(2,1)S(1)} %get-tuple-element.130), channel_id=1, source_target_pairs={{0,16},{8,24},{16,0},{24,8},{1,17},{9,25},{17,1},{25,9},{2,18},{10... | collective-permute-start | bytes 1179656 | tf_op jit(solution)/shard_map/ppermute | solution.py:83
  364.3 49.8 %collective-permute-start.19 = (bf16[128,1536]{1,0:T(8,128)(2,1)S(1)}, bf16[128,1536]{1,0:T(8,128)(2,1)S(1)}, u32[]{:S(2)}, u32[]{:S(2)}) collective-permute-start(bf16[128,1536]{1,0:T(8,128)(2,1)S(1)} %get-tuple-element.129), channel_id=1, source_target_pairs={{0,8},{8,16},{16,24},{24,0},{1,9},{9,17},{17,25},{25,1},{2,10},{10... | collective-permute-start | bytes 1179656 | tf_op jit(solution)/shard_map/ppermute | solution.py:83
  430.1 257.9 %reduce-scatter.13.cloned.1.call-start = ((), (), s32[]{:S(2)}) async-start(), calls=%async_computation.10 | async-start | bytes 2027520
  485.3 216.0 %reduce-scatter.11.cloned.1.call-start = ((), (), s32[]{:S(2)}) async-start(), calls=%async_computation.9 | async-start | bytes 4866048 | tf_op jit(solution)/shard_map/reduce_scatter | solution.py:436
  498.4 315.4 %reduce-scatter.9.cloned.1.call-start = ((), (), s32[]{:S(2)}) async-start(), calls=%async_computation.8 | async-start | bytes 4866048 | tf_op jit(solution)/shard_map/reduce_scatter | solution.py:437
  516.6 51.2 %collective-permute-start.30 = (bf16[4,2,2,48,1120]{4,3,2,0,1:T(8,128)(2,1)}, bf16[4,2,2,48,1120]{4,3,2,0,1:T(8,128)(2,1)}, u32[]{:S(2)}, u32[]{:S(2)}) collective-permute-start(bf16[4,2,2,48,1120]{4,3,2,0,1:T(8,128)(2,1)} %bitcast.295), channel_id=1, source_target_pairs={{0,2},{2,0},{1,3},{3,1},{4,6},{6,4},{5,7},{7,5},{8,10},{10,8},{9,1... | collective-permute-start | bytes 5160968 | tf_op jit(solution)/shard_map/ppermute | solution.py:78
  531.2 75.5 %collective-permute-start.37 = (bf16[128,1536]{1,0:T(8,128)(2,1)}, bf16[128,1536]{1,0:T(8,128)(2,1)}, u32[]{:S(2)}, u32[]{:S(2)}) collective-permute-start(bf16[128,1536]{1,0:T(8,128)(2,1)} %dynamic-slice_bitcast_fusion.14), channel_id=1, source_target_pairs={{0,2},{2,0},{1,3},{3,1},{4,6},{6,4},{5,7},{7,5},{8,10},{10,8},{9,1... | collective-permute-start | bytes 1179656 | tf_op jit(solution)/shard_map/ppermute | solution.py:78
  534.8 73.0 %collective-permute-start.39 = (bf16[152,1536]{1,0:T(8,128)(2,1)}, bf16[152,1536]{1,0:T(8,128)(2,1)}, u32[]{:S(2)}, u32[]{:S(2)}) collective-permute-start(bf16[152,1536]{1,0:T(8,128)(2,1)} %dynamic-slice_bitcast_fusion.6), channel_id=1, source_target_pairs={{0,4},{4,0},{1,5},{5,1},{2,6},{6,2},{3,7},{7,3},{8,12},{12,8},{9,1... | collective-permute-start | bytes 1400840 | tf_op jit(solution)/shard_map/ppermute | solution.py:78
  611.1 52.6 %collective-permute-start.34 = (bf16[2,2,48,1120]{3,2,1,0:T(8,128)(2,1)S(1)}, bf16[2,2,48,1120]{3,2,1,0:T(8,128)(2,1)S(1)}, u32[]{:S(2)}, u32[]{:S(2)}) collective-permute-start(bf16[2,2,48,1120]{3,2,1,0:T(8,128)(2,1)S(1)} %get-tuple-element.111), channel_id=1, source_target_pairs={{0,16},{8,24},{16,0},{24,8},{1,17},{9,25},{17,1},{25,9},{2,18},{10... | collective-permute-start | bytes 1290248 | tf_op jit(solution)/shard_map/ppermute | solution.py:83
  612.4 51.4 %collective-permute-start.35 = (bf16[2,2,48,1120]{3,2,1,0:T(8,128)(2,1)S(1)}, bf16[2,2,48,1120]{3,2,1,0:T(8,128)(2,1)S(1)}, u32[]{:S(2)}, u32[]{:S(2)}) collective-permute-start(bf16[2,2,48,1120]{3,2,1,0:T(8,128)(2,1)S(1)} %get-tuple-element.110), channel_id=1, source_target_pairs={{0,24},{8,0},{16,8},{24,16},{1,25},{9,1},{17,9},{25,17},{2,26},{10... | collective-permute-start | bytes 1290248 | tf_op jit(solution)/shard_map/ppermute | solution.py:83
  (108 other events, 1832.7 us)
Sparse Core Ops, SparseCore 0:
  11.5 71.0 all-gather.3
  91.4 27.1 all-gather.5
  121.5 95.4 all-gather.7
  430.2 44.3 reduce-scatter.6
  485.4 100.1 reduce-scatter.12
  590.9 110.2 reduce-scatter.10
  707.6 106.0 reduce-scatter.8

commit v2 on v1

v2 whole, which is shorter than its diff:
```python
import math

import jax
import jax.numpy as jnp
from jax import lax
from jax.experimental import pallas as pl
from jax.experimental.pallas import tpu as pltpu
from jax.sharding import Mesh
from jax.sharding import PartitionSpec as P

H = 12
KV = 2
HD = 128
HPG = 6


epsilon = 1e-06
rope_base = 10000.0
masked_value = -1e30


def root_mean_square_scale(values):
    return lax.rsqrt(jnp.mean(values * values, axis=-1, keepdims=True) + epsilon)


def rope_tables(within):
    steps_even = jnp.arange(0, HD, 2).astype(jnp.float32)
    inverse = rope_base ** (-steps_even / HD)
    phase = within.astype(jnp.float32)[:, None] * inverse[None, :]
    phase = jnp.concatenate([phase, phase], axis=-1)
    return (jnp.cos(phase)[:, None, :], jnp.sin(phase)[:, None, :])


def rotate(values, cosine, sine):
    halfway = values.shape[-1] // 2
    return (
        values * cosine
        + jnp.concatenate([-values[..., halfway:], values[..., :halfway]], axis=-1) * sine
    )


def rotate_back(grads, cosine, sine):
    halfway = grads.shape[-1] // 2
    turned = grads * sine
    return grads * cosine + jnp.concatenate(
        [turned[..., halfway:], -turned[..., :halfway]], axis=-1
    )


def doc_tables(doc_ends, doc_lengths, positions):
    passed = doc_ends[:, None, :] <= positions[None, :, None]
    doc_index = jnp.sum(passed.astype(jnp.int32), axis=-1)
    starts = jnp.sum(jnp.where(passed, doc_lengths[:, None, :], 0), axis=-1)
    return (doc_index, positions[None, :] - starts)


def contract_rows(left, right):
    return lax.dot_general(
        left, right, (((0,), (0,)), ((), ())), preferred_element_type=jnp.float32
    )


def contract_cols(left, right):
    return lax.dot_general(
        left, right, (((1,), (1,)), ((), ())), preferred_element_type=jnp.float32
    )


EVERY = ("z", "y", "x", "c")
ROW = ("y", "x", "c")
PLANE = ("y", "x")


def low(values):
    return values.astype(jnp.bfloat16)


def wide(values):
    return values.astype(jnp.float32)


def after(values, *others):
    return lax.optimization_barrier((values, others))[0]


def swapped(values, axis):
    return lax.ppermute(values, axis, [(0, 1), (1, 0)])


def shifted(values, amount):
    count = lax.axis_size("z")
    return lax.ppermute(values, "z", [(i, (i + amount) % count) for i in range(count)])


def square():
    return lax.axis_size("y") == 2 and lax.axis_size("x") == 2


def pick(values, index, axis):
    return lax.dynamic_index_in_dim(values, index, axis, keepdims=False)


def put(buffer, block, index, axis=0):
    index = tuple(index)
    shape = buffer.shape[:axis] + (1,) * len(index) + buffer.shape[axis + len(index) :]
    start = (0,) * axis + index + (0,) * (buffer.ndim - axis - len(index))
    return lax.dynamic_update_slice(buffer, block.reshape(shape), start)


def by_core_pair(own, other):
    first = lax.axis_index("c") == 0
    return jnp.where(first, own, other), jnp.where(first, other, own)


def side_by_side(own, other):
    return jnp.where(
        lax.axis_index("c") == 0,
        jnp.concatenate([own, other], axis=-1),
        jnp.concatenate([other, own], axis=-1),
    )


def other_first(rows):
    half = rows.shape[0] // 2
    return jnp.concatenate([rows[half:], rows[:half]], axis=0)


def near_shifts():
    return sorted({1, lax.axis_size("z") - 1})


def far_shifts():
    return range(2, lax.axis_size("z") - 1)


def depth_sent(blocks, shifts):
    nz, z = lax.axis_size("z"), lax.axis_index("z")
    return {k: shifted(pick(blocks, (z + k) % nz, 0), k) for k in shifts}


def own_block(blocks):
    return {0: pick(blocks, lax.axis_index("z"), 0)}


def depth_gathered(rows, shifts):
    return {k: shifted(rows, k) for k in shifts}


def depth_returned(blocks, shifts):
    return {k: shifted(low(blocks[k]), -k) for k in shifts}


def depth_placed(pieces):
    nz, z = lax.axis_size("z"), lax.axis_index("z")
    buffer = jnp.zeros((nz,) + pieces[0].shape, pieces[0].dtype)
    for k in range(nz):
        buffer = put(buffer, pieces[k], ((z - k) % nz,))
    return buffer


def in_order(pieces):
    return [pieces[k] for k in sorted(pieces)]


def sync(*values):
    return lax.optimization_barrier(values)


def nn(left, right):
    return jnp.dot(left, right, preferred_element_type=jnp.float32)


SPACE = pltpu.CompilerParams(vmem_limit_bytes=48 << 20)


def spread_columns(gate_weight, up_weight, sizes, unit, lane):
    nz, ny, nx, nc = sizes
    rows = gate_weight.shape[0]

    def kernel(gate_ref, up_ref, out_ref):
        out_ref[...] = jnp.zeros_like(out_ref)
        for m, ref in enumerate((gate_ref, up_ref)):
            for d in range(nz * ny * nx * nc):
                z, p, c = d // (ny * nx * nc), d // nc % (ny * nx), d % nc
                out_ref[c, z, m, :, lane * p : lane * p + unit] = ref[:, unit * d : unit * d + unit]

    shape = (nc, nz, 2, rows, lane * ny * nx)
    return pl.pallas_call(
        kernel,
        out_shape=jax.ShapeDtypeStruct(shape, jnp.bfloat16),
        compiler_params=SPACE,
        cost_estimate=LITTLE,
    )(gate_weight, up_weight)


def collect_columns(blocks, sizes, unit, lane):
    nz, ny, nx, nc = sizes
    rows = blocks.shape[3]

    def kernel(blocks_ref, gate_ref, up_ref):
        for m, ref in enumerate((gate_ref, up_ref)):
            for d in range(nz * ny * nx * nc):
                z, p, c = d // (ny * nx * nc), d // nc % (ny * nx), d % nc
                ref[:, unit * d : unit * d + unit] = wide(
                    blocks_ref[z, c, m, :, lane * p : lane * p + unit]
                )

    shape = jax.ShapeDtypeStruct((rows, unit * nz * ny * nx * nc), jnp.float32)
    return pl.pallas_call(
        kernel, out_shape=(shape, shape), compiler_params=SPACE, cost_estimate=LITTLE
    )(blocks)


def feed_forward(normed, upstream, weight_gate, weight_up, weight_down):
    count, width = normed.shape
    hidden_width = weight_gate.shape[1]
    tile = min(256, count)

    def kernel(normed_ref, up_ref, wg, wu, wd, grad_ref, hidden_ref, gate_ref, upg_ref):
        normed = normed_ref[...]
        gate = nn(normed, wg[...])
        up = nn(normed, wu[...])
        back = contract_cols(up_ref[...], wd[...])
        sigmoid = jax.nn.sigmoid(gate)
        silu = gate * sigmoid
        hidden = low(silu * up)
        gate_grad = low(back * up * sigmoid * (1.0 + gate * (1.0 - sigmoid)))
        up_grad = low(back * silu)
        hidden_ref[...] = hidden
        gate_ref[...] = gate_grad
        upg_ref[...] = up_grad
        grad_ref[...] = low(contract_cols(gate_grad, wg[...]) + contract_cols(up_grad, wu[...]))

    def rows(columns):
        return pl.BlockSpec((tile, columns), lambda i: (i, 0))

    def whole(array):
        return pl.BlockSpec(array.shape, lambda i: (0, 0))

    columns = (width, hidden_width, hidden_width, hidden_width)
    return pl.pallas_call(
        kernel,
        grid=(count // tile,),
        in_specs=[rows(width), rows(width), whole(weight_gate), whole(weight_up), whole(weight_down)],
        out_specs=[rows(n) for n in columns],
        out_shape=[jax.ShapeDtypeStruct((count, n), jnp.bfloat16) for n in columns],
        compiler_params=SPACE,
        cost_estimate=LITTLE,
    )(normed, upstream, weight_gate, weight_up, weight_down)


LITTLE = pl.CostEstimate(flops=1, bytes_accessed=1, transcendentals=0)


def turn(values, cosine, sine):
    return values * cosine + pltpu.roll(values, HD // 2, 1) * sine


def inner_projections(tokens, weight, vectors, cosine, sine, core, owned, owned_key):
    cores, local_rows, count, width = tokens.shape
    total = cores * local_rows * count
    half = width // 2

    def kernel(core_ref, tokens_ref, weight_ref, vectors_ref, cos_ref, sin_ref, n_ref, q_ref, pair_ref, line_ref):
        lines = wide(vectors_ref[...]).T
        at = core_ref[0]
        values = wide(tokens_ref[...].reshape(total, width))
        scale = lax.rsqrt(jnp.mean(values * values, axis=-1, keepdims=True) + epsilon)
        normed = low(values * scale * lines[1:2])
        n_ref[...] = normed
        line_ref[...] = lines[:8]
        source = lax.broadcasted_iota(jnp.int32, (width, HD), 0)
        feature = lax.broadcasted_iota(jnp.int32, (width, HD), 1) + at * HD
        place = feature // owned_key * owned + feature % owned_key
        small = low(lines[3:4])
        key_bias = nn(small, low(wide(source == place)))
        value_bias = nn(small, low(wide(source == place + owned_key)))
        bias = jnp.where(at == 0, lines[0:1, :half], lines[0:1, half:])
        pre = nn(normed, weight_ref[...])
        cosine, sine = cos_ref[...], sin_ref[...]
        for h in range(HPG):
            block = slice(h * HD, (h + 1) * HD)
            query = low(turn(pre[:, block] + bias[:, block], cosine, sine))
            query = query.reshape(cores, local_rows, count, HD)
            for r in range(local_rows):
                q_ref[r, h] = query[:, r]
        key = low(turn(pre[:, half : half + HD] + key_bias, cosine, sine))
        value = low(pre[:, half + HD :] + value_bias)
        shape = (cores, local_rows, count, HD)
        pair_ref[..., :HD] = key.reshape(shape)
        pair_ref[..., HD:] = value.reshape(shape)

    vmem = pl.BlockSpec(memory_space=pltpu.VMEM)
    return pl.pallas_call(
        kernel,
        in_specs=[pl.BlockSpec(memory_space=pltpu.SMEM)] + [vmem] * 5,
        out_specs=[vmem] * 4,
        out_shape=[
            jax.ShapeDtypeStruct((total, width), jnp.bfloat16),
            jax.ShapeDtypeStruct((local_rows, HPG, cores, count, HD), jnp.bfloat16),
            jax.ShapeDtypeStruct((cores, local_rows, count, 2 * HD), jnp.bfloat16),
            jax.ShapeDtypeStruct((8, width), jnp.float32),
        ],
        compiler_params=SPACE,
        cost_estimate=LITTLE,
    )(core.reshape(1), tokens, weight, vectors, cosine, sine)


def row_scores(query, keys, allowed):
    scores = contract_cols(query, keys) * (1.0 / math.sqrt(HD))
    return jnp.where(allowed, scores, masked_value)


def row_specs(pairs, cores, count):
    keys = pl.BlockSpec((pairs.shape[0], cores, 1, count, 2 * HD), lambda r: (0, 0, r, 0, 0))
    queries = pl.BlockSpec((1, HPG, cores, count, HD), lambda r: (r, 0, 0, 0, 0))
    flat = pl.BlockSpec((cores, 1, count, HPG * HD), lambda r: (0, r, 0, 0))
    stats = pl.BlockSpec((1, HPG, cores * count, HD), lambda r: (r, 0, 0, 0))
    allowed = pl.BlockSpec((1, cores * count, pairs.shape[0] * cores * count), lambda r: (r, 0, 0))
    return keys, queries, flat, stats, allowed


def attend(queries, pairs, allowed):
    local_rows, heads, cores, count, hd = queries.shape
    total = cores * count
    keys, query_spec, flat, stats, allowed_spec = row_specs(pairs, cores, count)

    def kernel(q_ref, pair_ref, allowed_ref, out_ref, stat_ref):
        pair = pair_ref[...].reshape(-1, 2 * HD)
        key, value = pair[:, :HD], pair[:, HD:]
        seen = allowed_ref[0] > 0
        for h in range(heads):
            scores = row_scores(q_ref[0, h].reshape(total, HD), key, seen)
            top = jnp.max(scores, axis=-1, keepdims=True)
            log_total = top + jnp.log(jnp.sum(jnp.exp(scores - top), axis=-1, keepdims=True))
            mixed = low(nn(low(jnp.exp(scores - log_total)), value))
            out_ref[:, 0, :, h * HD : (h + 1) * HD] = mixed.reshape(cores, count, HD)
            stat_ref[0, h] = jnp.broadcast_to(log_total, (total, HD))

    return pl.pallas_call(
        kernel,
        grid=(local_rows,),
        in_specs=[query_spec, keys, allowed_spec],
        out_specs=[flat, stats],
        out_shape=[
            jax.ShapeDtypeStruct((cores, local_rows, count, heads * HD), jnp.bfloat16),
            jax.ShapeDtypeStruct((local_rows, heads, total, HD), jnp.float32),
        ],
        compiler_params=SPACE,
        cost_estimate=LITTLE,
    )(queries, pairs, allowed)


def attend_back(queries, pairs, allowed, stats, grads, cosine, sine):
    local_rows, heads, cores, count, hd = queries.shape
    total = cores * count
    scaling = 1.0 / math.sqrt(HD)
    keys, query_spec, flat, stat_spec, allowed_spec = row_specs(pairs, cores, count)
    table = pl.BlockSpec((cores, 1, count, HD), lambda r: (0, r, 0, 0))

    def kernel(q_ref, pair_ref, allowed_ref, stat_ref, grad_ref, cos_ref, sin_ref, out_ref, part_ref):
        pair = pair_ref[...].reshape(-1, 2 * HD)
        key, value = pair[:, :HD], pair[:, HD:]
        seen = allowed_ref[0] > 0
        cosine, sine = (ref[...].reshape(total, HD) for ref in (cos_ref, sin_ref))
        key_part = jnp.zeros(key.shape, jnp.float32)
        value_part = jnp.zeros(key.shape, jnp.float32)
        for h in range(heads):
            query = q_ref[0, h].reshape(total, HD)
            grad = grad_ref[:, 0, :, h * HD : (h + 1) * HD].reshape(total, HD)
            probs = jnp.exp(row_scores(query, key, seen) - stat_ref[0, h][:, :1])
            back = contract_cols(grad, value)
            delta = jnp.sum(probs * back, axis=-1, keepdims=True)
            score_grad = low(probs * (back - delta))
            key_part = key_part + contract_rows(score_grad, query)
            value_part = value_part + contract_rows(low(probs), grad)
            query_sum = nn(score_grad, key) * scaling
            turned = query_sum * cosine + pltpu.roll(query_sum * sine, HD // 2, 1)
            out_ref[:, 0, :, h * HD : (h + 1) * HD] = low(turned).reshape(cores, count, HD)
        shape = (pair_ref.shape[0], cores, count, HD)
        part_ref[:, :, 0, :, :HD] = low(key_part * scaling).reshape(shape)
        part_ref[:, :, 0, :, HD:] = low(value_part).reshape(shape)

    return pl.pallas_call(
        kernel,
        grid=(local_rows,),
        in_specs=[query_spec, keys, allowed_spec, stat_spec, flat, table, table],
        out_specs=[flat, keys],
        out_shape=[
            jax.ShapeDtypeStruct((cores, local_rows, count, heads * HD), jnp.bfloat16),
            jax.ShapeDtypeStruct(pairs.shape, jnp.bfloat16),
        ],
        compiler_params=SPACE,
        cost_estimate=LITTLE,
    )(queries, pairs, allowed, stats, grads, cosine, sine)


def weight_grads(left, rights):
    count, rows = left.shape
    tile = 256 if rows % 256 == 0 else 128

    def kernel(left_ref, *refs):
        turned = left_ref[...].T
        for right_ref, out_ref in zip(refs[: len(rights)], refs[len(rights) :]):
            out_ref[...] = low(nn(turned, right_ref[...]))

    return pl.pallas_call(
        kernel,
        grid=(rows // tile,),
        in_specs=[pl.BlockSpec((count, tile), lambda i: (0, i))]
        + [pl.BlockSpec(r.shape, lambda i: (0, 0)) for r in rights],
        out_specs=[pl.BlockSpec((tile, r.shape[1]), lambda i: (i, 0)) for r in rights],
        out_shape=[jax.ShapeDtypeStruct((rows, r.shape[1]), jnp.bfloat16) for r in rights],
        compiler_params=SPACE,
        cost_estimate=LITTLE,
    )(left, *rights)


def plane_near(values):
    if not square():
        return ()
    return swapped(values, "x"), swapped(values, "y")


def plane_far(near, first, second):
    if not square():
        return ()
    return swapped(first(near[0]), "y"), swapped(second(near[1]), "x")


def plane_place(pieces, axis):
    y, x = lax.axis_index("y"), lax.axis_index("x")
    shape = pieces[0].shape
    buffer = jnp.zeros(shape[:axis] + (2, 2) + shape[axis:], pieces[0].dtype)
    for piece, index in zip(pieces, ((y, x), (y, 1 - x), (1 - y, x), (1 - y, 1 - x))):
        buffer = put(buffer, piece, index, axis)
    return buffer


def gather_plane(own, near, far, axis):
    if square():
        return plane_place((own, *near, far), axis)
    whole = lax.all_gather(own, PLANE, axis=axis, tiled=False)
    ny, nx = lax.axis_size("y"), lax.axis_size("x")
    return whole.reshape(own.shape[:axis] + (ny, nx) + own.shape[axis:])


def plane_reduced(pair, axis, step):
    if not square():
        if step:
            return pair
        out = []
        for v in pair:
            flat = v.reshape(v.shape[:axis] + (-1,) + v.shape[axis + 2 :])
            out.append(lax.psum_scatter(flat, PLANE, scatter_dimension=axis, tiled=False))
        return out
    out = []
    for left, name in zip(pair, ("yx", "xy")[step]):
        at = lax.axis_index(name)
        dim = axis if step or name == "y" else axis + 1
        came = swapped(pick(left, 1 - at, dim), name)
        out.append(low(wide(pick(left, at, dim)) + wide(came)))
    return out


def plane_gathered(rows):
    if not square():
        return lax.all_gather(rows, PLANE, axis=0)
    pair = jnp.stack([rows, swapped(rows, "x")])
    return jnp.concatenate([pair, swapped(pair, "y")], axis=0)


def plane_summed(blocks):
    if not square():
        return wide(lax.psum_scatter(blocks, PLANE, scatter_dimension=0, tiled=False))
    pair = low(wide(blocks[:2]) + wide(swapped(blocks[2:], "y")))
    return wide(pair[0]) + wide(swapped(pair[1], "x"))


def places():
    y, x = lax.axis_index("y"), lax.axis_index("x")
    if square():
        return [(y, x), (y, 1 - x), (1 - y, x), (1 - y, 1 - x)]
    return [(i, j) for i in range(lax.axis_size("y")) for j in range(lax.axis_size("x"))]


def chip_positions(y, x, shard_tokens):
    core = lax.axis_index("c")
    place = (y * lax.axis_size("x") + x) * 2
    lanes = jnp.arange(shard_tokens, dtype=jnp.int32)
    return [(place + k) * shard_tokens + lanes for k in (core, 1 - core)]


def position_tables(doc_lengths, shard_tokens):
    local_rows = doc_lengths.shape[0]
    query_pos = jnp.concatenate(
        chip_positions(lax.axis_index("y"), lax.axis_index("x"), shard_tokens)
    )
    key_pos = jnp.concatenate(
        [p for place in places() for p in chip_positions(*place, shard_tokens)]
    )
    doc_ends = jnp.cumsum(doc_lengths, axis=1)
    query_doc, query_within = doc_tables(doc_ends, doc_lengths, query_pos)
    key_doc, unused_within = doc_tables(doc_ends, doc_lengths, key_pos)
    allowed = (query_doc[:, :, None] == key_doc[:, None, :]) & (
        key_pos[None, None, :] <= query_pos[None, :, None]
    )
    query_within = query_within.reshape(local_rows, 2, shard_tokens).transpose(1, 0, 2)
    cosine, sine = rope_tables(query_within.reshape(-1))
    sign = jnp.where(jnp.arange(HD) < HD // 2, -1.0, 1.0)
    return cosine[:, 0], sine[:, 0] * sign, wide(allowed)


def column_pack(columns, rows):
    padded = [jnp.pad(v, (0, rows - v.shape[0])) for v in columns]
    packed = jnp.stack(padded, axis=1)
    return jnp.pad(packed, ((0, 0), (0, 128 - len(columns))))


def shards(
    tokens,
    doc_lengths,
    query_weight,
    key_weight,
    value_weight,
    query_bias,
    key_bias,
    value_bias,
    output_weight,
    attention_norm_gain,
    feedforward_norm_gain,
    gate_weight,
    up_weight,
    down_weight,
    cotangent,
):
    local_rows, shard_tokens, width = tokens.shape
    nz, ny, nx, nc = (lax.axis_size(a) for a in EVERY)
    core = lax.axis_index("c")
    devices = nz * ny * nx * nc
    flat_count = local_rows * shard_tokens
    chip_count = 2 * flat_count
    row_length = shard_tokens * ny * nx * nc
    scaling = 1.0 / math.sqrt(HD)
    owned, query_width = query_weight.shape
    key_width = key_weight.shape[1]
    owned_key = key_bias.shape[0]
    half = query_width // 2

    unit = gate_weight.shape[1] // devices
    sizes = (nz, ny, nx, nc)
    lane = -(-ny * nx * unit // 128) * 128 // (ny * nx)
    hidden_width = ny * nx * lane
    own_tokens = tokens.reshape(flat_count, width)
    upstream = cotangent.reshape(flat_count, width)

    down_near = plane_near(down_weight)
    vectors = column_pack(
        (
            query_bias,
            attention_norm_gain,
            feedforward_norm_gain,
            jnp.concatenate([key_bias, value_bias]),
        ),
        owned,
    )
    packed = jnp.concatenate([query_weight, key_weight, value_weight, vectors], axis=1)
    every_shift = range(1, nz)
    pieces = depth_gathered(packed, every_shift)
    pieces[0] = packed
    both = spread_columns(gate_weight, up_weight, sizes, unit, lane)
    cosine, sine, allowed = position_tables(doc_lengths, shard_tokens)
    pieces, down_near, both, cosine, sine, allowed = sync(
        pieces, down_near, both, cosine, sine, allowed
    )

    def core_columns(of):
        return jnp.concatenate(
            [
                lax.dynamic_slice_in_dim(whole, of * half, half, 2),
                lax.dynamic_slice_in_dim(whole, query_width + of * HD, HD, 2),
                lax.dynamic_slice_in_dim(whole, query_width + key_width + of * HD, HD, 2),
                whole[..., query_width + 2 * key_width :],
            ],
            axis=2,
        )

    whole = depth_placed(pieces)
    mine, came = core_columns(core), swapped(core_columns(1 - core), "c")
    both_came = swapped(pick(both, 1 - core, 0), "c")
    both = pick(both, core, 0)
    output_weight = after(output_weight, pieces)
    output_pieces = depth_gathered(output_weight, every_shift)
    output_pieces[0] = output_weight
    mine, came, both, both_came, output_pieces = sync(mine, came, both, both_came, output_pieces)

    inner_own = jnp.stack(by_core_pair(mine, came), axis=1)
    inner_near = plane_near(inner_own)
    both_all = jnp.stack(by_core_pair(both, both_came), axis=2)
    both = depth_sent(both_all, near_shifts())
    both |= own_block(both_all)
    chip_tokens = jnp.concatenate([own_tokens, swapped(own_tokens, "c")], axis=0)
    output_all = depth_placed(output_pieces)
    output_mine = lax.dynamic_slice_in_dim(output_all, core * (width // 2), width // 2, 2)
    output_other = lax.dynamic_slice_in_dim(output_all, (1 - core) * (width // 2), width // 2, 2)
    inner_own, inner_near, output_mine, output_other, both, both_all, chip_tokens = sync(
        inner_own, inner_near, output_mine, output_other, both, both_all, chip_tokens
    )
    middle = 512
    inner_far = plane_far(inner_near, lambda v: v[..., :middle], lambda v: v[..., middle:])
    both |= depth_sent(both_all, far_shifts())
    down_far = plane_far(down_near, lambda v: v[: unit // 2], lambda v: v[unit // 2 :])
    inner_own, inner_near, inner_far, output_mine, output_other, both, down_far = sync(
        inner_own, inner_near, inner_far, output_mine, output_other, both, down_far
    )

    output_came = swapped(output_other, "c")
    output_own = jnp.stack(by_core_pair(output_mine, output_came), axis=1)
    output_near = plane_near(output_own)
    upstream_pieces = depth_gathered(after(upstream, both), near_shifts())
    both = depth_placed(both)
    if square():
        inner_far = jnp.concatenate(inner_far, axis=-1)
    attention = gather_plane(inner_own, inner_near, inner_far, 1).reshape(width, -1)
    at = half + 2 * HD
    weight_inner = attention[:, :at]
    chip_shape = (2, local_rows, shard_tokens)
    cosine = cosine.reshape(chip_shape + (HD,))
    sine = sine.reshape(chip_shape + (HD,))
    first_normed, queries, own_pair, lines = inner_projections(
        chip_tokens.reshape(chip_shape + (width,)),
        weight_inner,
        attention[:, at:],
        cosine.reshape(chip_count, HD),
        sine.reshape(chip_count, HD),
        core,
        owned,
        owned_key,
    )
    input_gain, post_gain = lines[1], lines[2]
    own_pair, output_own, output_near, upstream_pieces, both = sync(
        own_pair, output_own, output_near, upstream_pieces, both
    )
    upstream_pieces |= depth_gathered(after(upstream, own_pair), far_shifts())
    upstream_pieces[0] = upstream
    output_far = plane_far(
        output_near, lambda v: v[..., : width // 4], lambda v: v[..., width // 4 :]
    )

    pairs = plane_gathered(own_pair)
    pairs, output_far, upstream_pieces, both = sync(pairs, output_far, upstream_pieces, both)
    gate_near = plane_near(both[:, 0])
    attended, log_sums = attend(queries, pairs, allowed)
    attended = attended.reshape(chip_count, half)
    attended, gate_near, both = sync(attended, gate_near, both)
    up_near = plane_near(both[:, 1])
    if square():
        output_far = jnp.concatenate(output_far, axis=-1)
    weight_output = gather_plane(output_own, output_near, output_far, 1).reshape(width, -1)
    attended = side_by_side(attended, swapped(other_first(attended), "c"))
    output_part = nn(attended, weight_output)
    output_sum = side_by_side(
        output_part[:flat_count], swapped(output_part[flat_count:], "c")
    )
    own_wide = wide(own_tokens)
    first_hidden = own_wide + output_sum
    second_inverse_norm = root_mean_square_scale(first_hidden)
    second_normalized = first_hidden * second_inverse_norm
    second_normed = low(second_normalized * post_gain)

    second_normed, up_near = sync(second_normed, up_near)
    second_pieces = depth_gathered(second_normed, every_shift)
    second_pieces[0] = second_normed
    upstream_mine = jnp.concatenate(in_order(upstream_pieces), axis=0)
    upstream_other = swapped(upstream_mine, "c")
    gate_far = up_far = None
    if square():
        gate_far, up_far = swapped(gate_near[0], "y"), swapped(up_near[1], "x")
    second_pieces, gate_far, up_far, upstream_other = sync(
        second_pieces, gate_far, up_far, upstream_other
    )
    weight_gate = gather_plane(both[:, 0], gate_near, gate_far, 1).reshape(width, hidden_width)
    weight_up = gather_plane(both[:, 1], up_near, up_far, 1).reshape(width, hidden_width)
    if square():
        down_far = jnp.concatenate(down_far, axis=0)
    weight_down = gather_plane(down_weight, down_near, down_far, 0)
    weight_down = jnp.pad(weight_down, ((0, 0), (0, 0), (0, lane - unit), (0, 0)))
    weight_down = weight_down.reshape(hidden_width, width)

    second_mine = jnp.concatenate(in_order(second_pieces), axis=0)
    second_group = jnp.concatenate([swapped(second_mine, "c"), second_mine], axis=0)
    upstream_group = jnp.concatenate([upstream_other, upstream_mine], axis=0)
    normed_part, hidden, gate_grad, up_grad = feed_forward(
        second_group, upstream_group, weight_gate, weight_up, weight_down
    )
    group = second_mine.shape[0]
    normed_came = swapped(normed_part[:group], "c")
    gate_term, up_term = weight_grads(second_group, (gate_grad, up_grad))
    normed_came, gate_term, up_term = sync(normed_came, gate_term, up_term)
    normed_sum = (wide(normed_part[group:]) + wide(normed_came)).reshape(nz, flat_count, width)
    normed_pieces = depth_returned(normed_sum, every_shift)
    six = (nz, ny, nx, nc, owned, hidden_width)
    both = plane_reduced((gate_term.reshape(six), up_term.reshape(six)), 1, 0)
    hidden, weight_down = after((hidden, weight_down), normed_sum)
    (down_term,) = weight_grads(hidden, (upstream_group,))
    output_part = low(nn(hidden, weight_down))
    normed_pieces, down_term, output_part, normed_sum, both = sync(
        normed_pieces, down_term, output_part, normed_sum, both
    )
    second_normed_grad = normed_sum[0] + sum(wide(v) for v in in_order(normed_pieces))

    post_gain_term = jnp.sum(second_normed_grad * second_normalized, axis=0)
    second_scaled = second_normed_grad * post_gain
    hidden_one_grad = wide(upstream) + second_inverse_norm * (
        second_scaled
        - second_normalized * jnp.mean(second_scaled * second_normalized, axis=-1, keepdims=True)
    )
    proj_halves = low(hidden_one_grad).reshape(flat_count, 2, width // 2)
    proj_grad = jnp.concatenate(
        [pick(proj_halves, core, 1), swapped(pick(proj_halves, 1 - core, 1), "c")], axis=0
    )
    part = contract_cols(proj_grad, weight_output).reshape(chip_count, 2, half)
    came = swapped(other_first(pick(part, 1 - core, 1)), "c")
    attended_grad = low(pick(part, core, 1) + came)
    output_came = swapped(output_part[:group], "c")
    attended_grad, both, output_came = sync(attended_grad, both, output_came)
    output_sum = (wide(output_part[group:]) + wide(output_came)).reshape(nz, flat_count, width)
    both = plane_reduced(both, 1, 1)
    output_pieces = depth_returned(output_sum, near_shifts())
    query_grad, pair_part = attend_back(
        queries,
        pairs,
        allowed,
        log_sums,
        attended_grad.reshape(chip_shape + (half,)),
        cosine,
        sine,
    )
    query_grad = query_grad.reshape(chip_count, half)
    pair_part, both, output_pieces, output_sum = sync(pair_part, both, output_pieces, output_sum)
    pair_sum = plane_summed(pair_part)
    output_pieces |= depth_returned(output_sum, far_shifts())
    pair_sum = pair_sum.reshape(chip_count, 2 * HD)
    both = jnp.stack(both, axis=2)
    both_came = swapped(pick(both, 1 - core, 1), "c")
    both = jnp.stack(by_core_pair(pick(both, core, 1), both_came), axis=1)
    pair_sum, both, output_pieces = sync(pair_sum, both, output_pieces)
    down_term = after(down_term, pair_sum).reshape(ny, nx, lane, width)
    down_sum = plane_reduced((down_term[:, :, : lane // 2], down_term[:, :, lane // 2 :]), 0, 0)
    key_sum = pair_sum[:, :HD]
    turned = jnp.roll(key_sum * sine.reshape(chip_count, HD), HD // 2, axis=1)
    key_grad = low(key_sum * cosine.reshape(chip_count, HD) + turned)
    pair_grad = jnp.concatenate([key_grad, low(pair_sum[:, HD:])], axis=1)

    first_normed_grad = (
        contract_cols(jnp.concatenate([query_grad, pair_grad], axis=1), weight_inner)
    )
    first_normed_grad = first_normed_grad[:flat_count] + swapped(
        first_normed_grad[flat_count:], "c"
    )
    first_inverse_norm = root_mean_square_scale(own_wide)
    own_normalized = own_wide * first_inverse_norm
    input_gain_term = jnp.sum(first_normed_grad * own_normalized, axis=0)
    first_scaled = first_normed_grad * input_gain
    input_grad = hidden_one_grad + first_inverse_norm * (
        first_scaled
        - own_normalized * jnp.mean(first_scaled * own_normalized, axis=-1, keepdims=True)
    )

    query_bias_term = jnp.sum(wide(query_grad), axis=0)
    pair_bias_term = jnp.sum(wide(pair_grad), axis=0)
    inner_grad = jnp.concatenate([query_grad, pair_grad], axis=1)
    (output_term,) = weight_grads(attended, (proj_grad,))
    (inner_term,) = weight_grads(first_normed, (inner_grad,))

    def spread(term, size):
        return lax.dynamic_update_slice(jnp.zeros((size,), term.dtype), term, (core * term.shape[0],))

    small_terms = jnp.concatenate(
        [
            spread(pair_bias_term[:HD], key_width).reshape(devices, owned_key),
            spread(pair_bias_term[HD:], key_width).reshape(devices, owned_key),
            jnp.zeros((devices, owned - 2 * owned_key), jnp.float32),
        ],
        axis=1,
    ).reshape(-1)
    vector_terms = column_pack(
        (spread(query_bias_term, width), input_gain_term, post_gain_term, small_terms), width
    )
    five = (nz, ny, nx, nc, owned, -1)
    inner = (
        jnp.concatenate([output_term, low(vector_terms)], axis=1).reshape(five),
        inner_term.reshape(five),
    )
    inner, both, down_sum, output_pieces = sync(inner, both, down_sum, output_pieces)
    layer_output = low(
        first_hidden + output_sum[0] + sum(wide(v) for v in in_order(output_pieces))
    )
    inner = plane_reduced(inner, 1, 0)
    both_sent = depth_sent(both, every_shift) | own_block(both)
    inner, both_sent, down_sum = sync(inner, both_sent, down_sum)
    inner = plane_reduced(inner, 1, 1)
    gate_sum, up_sum = collect_columns(depth_placed(both_sent), sizes, unit, lane)
    inner, down_sum = sync(inner, down_sum)
    inner = jnp.concatenate(inner, axis=-1)
    pieces = depth_sent(inner, every_shift) | own_block(inner)
    down_sum = plane_reduced(down_sum, 0, 1)
    inner = sum(wide(v) for v in in_order(pieces))
    mine, came = pick(inner, core, 0), wide(swapped(low(pick(inner, 1 - core, 0)), "c"))
    ends = [width // 2, width // 2 + 128]
    ends += [ends[1] + half, ends[1] + half + HD]
    mine, came = (jnp.split(v, ends, axis=1) for v in (mine, came))
    output_term, query_term, key_term, value_term = (
        side_by_side(mine[i], came[i]) for i in (0, 2, 3, 4)
    )
    vector_sums = mine[1] + came[1]
    down_sum = wide(jnp.concatenate(down_sum, axis=0))[:unit]
    return (
        layer_output.reshape(local_rows, shard_tokens, width),
        low(input_grad).reshape(local_rows, shard_tokens, width),
        query_term,
        key_term,
        value_term,
        vector_sums[:, 0],
        vector_sums[:owned_key, 3],
        vector_sums[owned_key : 2 * owned_key, 3],
        output_term,
        vector_sums[:, 1],
        vector_sums[:, 2],
        gate_sum,
        up_sum,
        down_sum,
    )


def solution(mesh):
    depth, across = mesh.devices.shape
    plane = across // 2
    side = math.isqrt(plane)
    inner = Mesh(mesh.devices.reshape(depth, plane // side, side, 2), EVERY)
    over_rows = P("z", ROW, None)
    whole, flat = P(EVERY, None), P(EVERY)
    in_specs = (
        (over_rows, P("z", None))
        + (whole,) * 3
        + (flat,) * 3
        + (whole, flat, flat)
        + (whole,) * 3
        + (over_rows,)
    )
    out_specs = (
        (over_rows,) * 2 + (whole,) * 3 + (flat,) * 3 + (whole, flat, flat) + (whole,) * 3
    )
    return jax.shard_map(
        shards, mesh=inner, in_specs=in_specs, out_specs=out_specs, check_vma=False
    )
```

time: 835 us -> 535 us (0.64)
  waiting for transfers between devices: 491 us -> 230 us
  matrix products: 91.3 us -> 8.26 us
  Pallas kernels: 0 us -> 68.8 us
  local copies, waits for them, and re-layouts: 131 us -> 78.2 us
  starting transfers between devices: 36.3 us -> 88.7 us
  between operations: 16.5 us -> 2.73 us
    reduce_scatter x3 -> x0, waiting for transfers between devices: 153 us -> none  [the longest x1 111 us: shards(): lax.psum_scatter(query_term, EVERY, scatter_dimension=0, tiled=True)]
    pallas_call x0 -> x10, Pallas kernels: none -> 68.8 us  [the longest x1 31.6 us: feed_forward(): pl.pallas_call(kernel, grid=(count // tile,), in_specs=[rows(width), rows...]
    all_gather x3 -> x0, waiting for transfers between devices: 67.2 us -> none  [the longest x1 67.2 us: shards(): packed = lax.all_gather(packed, EVERY, axis=0, tiled=True)]
    ppermute x18 -> x27, waiting for transfers between devices: 178 us -> 114 us  [shifted(): lax.ppermute(values, 'z', [(i, (i + amount) % count) for i in range(count)])]
    dot_general x17 -> x2, matrix products: 63.3 us -> 6.45 us  [nn(): return jnp.dot(left, right, preferred_element_type=jnp.float32)]
    ppermute x22 -> x49, starting transfers between devices: 19.6 us -> 47 us  [swapped(): return lax.ppermute(values, axis, [(0, 1), (1, 0)])]
    dot_general x6 -> x2, matrix products: 28 us -> 1.81 us  [contract_cols(): lax.dot_general(left, right, (((1,), (1,)), ((), ())), preferred_element_...]
    ppermute x18 -> x27, starting transfers between devices: 16 us -> 41.7 us  [shifted(): lax.ppermute(values, 'z', [(i, (i + amount) % count) for i in range(count)])]
  transfers between devices with their start and end apart: 47 -> 76, of which waited for: 19 -> 37; matrix products, arithmetic and copies ran while one was open for 24% -> 18% of each run, Pallas kernels for 0% -> 7%
where the time goes in v2:
time: 535 us; the launch traced here: 528 us
  waiting for transfers between devices  230 us (43%)
  starting transfers between devices  88.7 us (17%)
  local copies, waits for them, and re-layouts  78.2 us (15%)
  Pallas kernels  68.8 us (13%)
  other arithmetic  51.8 us (10%)
  matrix products  8.26 us (2%)
    ppermute x49, waiting for transfers between devices, swapped(): return lax.ppermute(values, axis, [(0, 1), (1, 0)])  116 us
    ppermute x27, waiting for transfers between devices, shifted(): lax.ppermute(values, 'z', [(i, (i + amount) % count) for i in range(count)])  114 us
    ppermute x49, starting transfers between devices, swapped(): return lax.ppermute(values, axis, [(0, 1), (1, 0)])  47 us
    ppermute x27, starting transfers between devices, shifted(): lax.ppermute(values, 'z', [(i, (i + amount) % count) for i in range(count)])  41.7 us
    pallas_call x1, Pallas kernels, feed_forward(): pl.pallas_call(kernel, grid=(count // tile,), in_specs=[rows(width), rows...  31.6 us
    pallas_call x4, Pallas kernels, weight_grads(): pl.pallas_call(kernel, grid=(rows // tile,), in_specs=[pl.BlockSpec((coun...  22.3 us
    dynamic_update_slice x33, local copies, waits for them, and re-layouts, put(): return lax.dynamic_update_slice(buffer, block.reshape(shape), start)  19.8 us
    unnamed x162, local copies, waits for them, and re-layouts  18.7 us
  transfers between devices with their start and end apart: 76, of which 37 were waited for; matrix products, arithmetic and copies ran while one was open for 18% of the time, Pallas kernels for 7%

profile of v2, /device:TPU:29, one launch (start us, length us, event | category | flops | bytes accessed | tf_op | source)
XLA Modules:
  0.0 528.3 jit_solution(11843603142581495742)
XLA Ops:
  44.3 7.7 %collective-permute-done.12 = bf16[2,2,48,1152]{3,2,1,0:T(8,128)(2,1)S(1)} collective-permute-done((bf16[2,2,48,1152]{3,2,1,0:T(8,128)(2,1)S(1)}, bf16[2,2,48,1152]{3,2,1,0:T(8,128)(2,1)S(1)}, u32[]{:S(2)}, u32[]{:S(2)}) %collective-permute-start.12) | collective-permute-done | bytes 442400 | tf_op jit(solution)/shard_map/ppermute | solution.py:92
  53.2 10.1 %collective-permute-done.13 = bf16[2,2,48,1152]{3,2,1,0:T(8,128)(2,1)S(1)} collective-permute-done((bf16[2,2,48,1152]{3,2,1,0:T(8,128)(2,1)S(1)}, bf16[2,2,48,1152]{3,2,1,0:T(8,128)(2,1)S(1)}, u32[]{:S(2)}, u32[]{:S(2)}) %collective-permute-start.13) | collective-permute-done | bytes 442400 | tf_op jit(solution)/shard_map/ppermute | solution.py:92
  63.3 5.6 %collective-permute-done.11 = bf16[4,2,48,1152]{3,2,1,0:T(8,128)(2,1)S(1)} collective-permute-done((bf16[4,2,48,1152]{3,2,1,0:T(8,128)(2,1)S(1)}, bf16[4,2,48,1152]{3,2,1,0:T(8,128)(2,1)S(1)}, u32[]{:S(2)}, u32[]{:S(2)}) %collective-permute-start.11) | collective-permute-done | bytes 884768 | tf_op jit(solution)/shard_map/ppermute | solution.py:87
  72.7 7.2 %collective-permute-done.15 = bf16[4,2,48,512]{3,2,1,0:T(8,128)(2,1)S(1)} collective-permute-done((bf16[4,2,48,512]{3,2,1,0:T(8,128)(2,1)S(1)}, bf16[4,2,48,512]{3,2,1,0:T(8,128)(2,1)S(1)}, u32[]{:S(2)}, u32[]{:S(2)}) %collective-permute-start.15) | collective-permute-done | bytes 393248 | tf_op jit(solution)/shard_map/ppermute | solution.py:87
  79.9 9.7 %collective-permute-done.17 = bf16[2,2,48,1152]{3,2,1,0:T(8,128)(2,1)S(1)} collective-permute-done((bf16[2,2,48,1152]{3,2,1,0:T(8,128)(2,1)S(1)}, bf16[2,2,48,1152]{3,2,1,0:T(8,128)(2,1)S(1)}, u32[]{:S(2)}, u32[]{:S(2)}) %collective-permute-start.17) | collective-permute-done | bytes 442400 | tf_op jit(solution)/shard_map/ppermute | solution.py:92
  102.2 9.4 %collective-permute-done.24 = bf16[128,1536]{1,0:T(8,128)(2,1)S(1)} collective-permute-done((bf16[128,1536]{1,0:T(8,128)(2,1)S(1)}, bf16[128,1536]{1,0:T(8,128)(2,1)S(1)}, u32[]{:S(2)}, u32[]{:S(2)}) %collective-permute-start.24) | collective-permute-done | bytes 393248 | tf_op jit(solution)/shard_map/ppermute | solution.py:92
  120.9 6.5 %collective-permute-done.27 = bf16[4,2,48,384]{3,2,1,0:T(8,128)(2,1)S(1)} collective-permute-done((bf16[4,2,48,384]{3,2,1,0:T(8,128)(2,1)S(1)}, bf16[4,2,48,384]{3,2,1,0:T(8,128)(2,1)S(1)}, u32[]{:S(2)}, u32[]{:S(2)}) %collective-permute-start.27) | collective-permute-done | bytes 294944 | tf_op jit(solution)/shard_map/ppermute | solution.py:87
  127.4 5.5 %collective-permute-done.29 = bf16[128,1536]{1,0:T(8,128)(2,1)S(1)} collective-permute-done((bf16[128,1536]{1,0:T(8,128)(2,1)S(1)}, bf16[128,1536]{1,0:T(8,128)(2,1)S(1)}, u32[]{:S(2)}, u32[]{:S(2)}) %collective-permute-start.29) | collective-permute-done | bytes 393248 | tf_op jit(solution)/shard_map/ppermute | solution.py:92
  142.3 10.2 %collective-permute-done.30 = bf16[4,2,48,1152]{3,2,1,0:T(8,128)(2,1)} collective-permute-done((bf16[4,2,48,1152]{3,2,1,0:T(8,128)(2,1)S(1)}, bf16[4,2,48,1152]{3,2,1,0:T(8,128)(2,1)}, u32[]{:S(2)}, u32[]{:S(2)}) %collective-permute-start.30) | collective-permute-done | bytes 884768 | tf_op jit(solution)/shard_map/ppermute | solution.py:87
  183.3 8.7 %collective-permute-done.39 = bf16[4,2,48,1152]{3,2,1,0:T(8,128)(2,1)} collective-permute-done((bf16[4,2,48,1152]{3,2,1,0:T(8,128)(2,1)}, bf16[4,2,48,1152]{3,2,1,0:T(8,128)(2,1)}, u32[]{:S(2)}, u32[]{:S(2)}) %collective-permute-start.39) | collective-permute-done | bytes 884768 | tf_op jit(solution)/shard_map/ppermute | solution.py:87
  192.0 13.4 %collective-permute-done.37 = bf16[128,1536]{1,0:T(8,128)(2,1)S(1)} collective-permute-done((bf16[128,1536]{1,0:T(8,128)(2,1)S(1)}, bf16[128,1536]{1,0:T(8,128)(2,1)S(1)}, u32[]{:S(2)}, u32[]{:S(2)}) %collective-permute-start.37) | collective-permute-done | bytes 393248 | tf_op jit(solution)/shard_map/ppermute | solution.py:92
  207.2 6.4 %collective-permute-start.42 = (bf16[512,1536]{1,0:T(8,128)(2,1)S(1)}, bf16[512,1536]{1,0:T(8,128)(2,1)S(1)}, u32[]{:S(2)}, u32[]{:S(2)}) collective-permute-start(bf16[512,1536]{1,0:T(8,128)(2,1)S(1)} %pad_maximum_fusion.3), channel_id=1, source_target_pairs={{0,1},{1,0},{2,3},{3,2},{4,5},{5,4},{6,7},{7,6},{8,9},{9,8},{10,11... | collective-permute-start | bytes 4718600 | tf_op jit(solution)/shard_map/ppermute | solution.py:87
  219.2 31.6 %shard_map.257 = (bf16[1024,1536]{1,0:T(8,128)(2,1)}, bf16[1024,1152]{1,0:T(8,128)(2,1)S(1)}, bf16[1024,1152]{1,0:T(8,128)(2,1)S(1)}, bf16[1024,1152]{1,0:T(8,128)(2,1)}) custom-call(bf16[1024,1536]{1,0:T(8,128)(2,1)} %copy-done.10, bf16[1024,1536]{1,0:T(8,128)(2,1)} %copy-done, bf16[1536,1152]{1,0:T(8,128)(2,1)} %bitcast.68.wg, ...), custom_call_target="tpu_custom_call" | custom-call | flops 1 | bytes 1 | tf_op jit(solution)/shard_map/pallas_call | solution.py:241
  253.4 11.2 %shard_map.258 = (bf16[1536,1152]{1,0:T(8,128)(2,1)}, bf16[1536,1152]{1,0:T(8,128)(2,1)}) custom-call(bf16[1024,1536]{1,0:T(8,128)(2,1)} %copy-done.10, bf16[1024,1152]{1,0:T(8,128)(2,1)S(1)} %get-tuple-element.231.refs_0_, bf16[1024,1152]{1,0:T(8,128)(2,1)S(1)} %copy-done.3), custom_call_target="tpu_custom_call" | custom-call | flops 1 | bytes 1 | tf_op jit(solution)/shard_map/pallas_call | solution.py:407
  274.9 7.0 %shard_map.259 = bf16[1152,1536]{1,0:T(8,128)(2,1)} custom-call(bf16[1024,1152]{1,0:T(8,128)(2,1)S(1)} %get-tuple-element.237.left_ref, bf16[1024,1536]{1,0:T(8,128)(2,1)S(1)} %copy-done.1), custom_call_target="tpu_custom_call" | custom-call | flops 1 | bytes 1 | tf_op jit(solution)/shard_map/pallas_call | solution.py:407
  287.9 5.7 %convolution_convert_fusion = bf16[1024,1536]{1,0:T(8,128)(2,1)} fusion(bf16[1024,1152]{1,0:T(8,128)(2,1)S(1)} %get-tuple-element.237.left_ref, bf16[1152,1536]{1,0:T(8,128)(2,1)S(1)} %bitcast.354), kind=kOutput, calls=%fused_computation.2 | convolution fusion | flops 3625451520 | bytes 9043968 | tf_op jit(solution)/shard_map/dot_general | solution.py:170
  293.5 17.2 %collective-permute-done.47 = bf16[4,2,2,48,1152]{4,3,2,0,1:T(8,128)(2,1)} collective-permute-done((bf16[4,2,2,48,1152]{4,3,2,0,1:T(8,128)(2,1)}, bf16[4,2,2,48,1152]{4,3,2,0,1:T(8,128)(2,1)}, u32[]{:S(2)}, u32[]{:S(2)}) %collective-permute-start.47) | collective-permute-done | bytes 1769504 | tf_op jit(solution)/shard_map/ppermute | solution.py:87
  351.3 5.6 %shard_map.260 = (bf16[2,2,64,768]{3,2,1,0:T(8,128)(2,1)S(1)}, bf16[4,2,2,64,256]{4,3,2,1,0:T(8,128)(2,1)S(1)}) custom-call(bf16[2,6,2,64,128]{4,3,2,1,0:T(8,128)(2,1)S(1)} %get-tuple-element.185.q_ref, bf16[4,2,2,64,256]{4,3,2,1,0:T(8,128)(2,1)S(1)} %pad_maximum_fusion.11.pair_ref, f32[2,128,512]{2,1,0:T(8,128)S(1)} %and_convert_fusion.allowed_ref, ...), custom_call_target="tpu_custom_call" | custom-call | flops 1 | bytes 1 | tf_op jit(solution)/shard_map/pallas_call | solution.py:384
  357.0 7.5 %collective-permute-done.53 = bf16[4,2,48,1152]{3,2,1,0:T(8,128)(2,1)S(1)} collective-permute-done((bf16[4,2,48,1152]{3,2,1,0:T(8,128)(2,1)}, bf16[4,2,48,1152]{3,2,1,0:T(8,128)(2,1)S(1)}, u32[]{:S(2)}, u32[]{:S(2)}) %collective-permute-start.53) | collective-permute-done | bytes 884768 | tf_op jit(solution)/shard_map/ppermute | solution.py:87
  370.2 5.3 collective-permute-done.56
  381.1 14.9 %collective-permute-done.59 = bf16[128,1536]{1,0:T(8,128)(2,1)S(1)} collective-permute-done((bf16[128,1536]{1,0:T(8,128)(2,1)S(1)}, bf16[128,1536]{1,0:T(8,128)(2,1)S(1)}, u32[]{:S(2)}, u32[]{:S(2)}) %collective-permute-start.59) | collective-permute-done | bytes 393248 | tf_op jit(solution)/shard_map/ppermute | solution.py:92
  430.9 25.0 %collective-permute-done.63 = bf16[4,2,2,48,896]{4,3,2,0,1:T(8,128)(2,1)S(1)} collective-permute-done((bf16[4,2,2,48,896]{4,3,2,0,1:T(8,128)(2,1)S(1)}, bf16[4,2,2,48,896]{4,3,2,0,1:T(8,128)(2,1)S(1)}, u32[]{:S(2)}, u32[]{:S(2)}) %collective-permute-start.63) | collective-permute-done | bytes 1376288 | tf_op jit(solution)/shard_map/ppermute | solution.py:87
  475.5 5.7 %collective-permute-done.68 = bf16[4,2,48,896]{3,2,1,0:T(8,128)(2,1)S(1)} collective-permute-done((bf16[4,2,48,896]{3,2,1,0:T(8,128)(2,1)S(1)}, bf16[4,2,48,896]{3,2,1,0:T(8,128)(2,1)S(1)}, u32[]{:S(2)}, u32[]{:S(2)}) %collective-permute-start.68) | collective-permute-done | bytes 688160 | tf_op jit(solution)/shard_map/ppermute | solution.py:87
  493.2 25.6 %collective-permute-done.71 = bf16[2,48,1920]{2,1,0:T(8,128)(2,1)S(1)} collective-permute-done((bf16[2,48,1920]{2,1,0:T(8,128)(2,1)S(1)}, bf16[2,48,1920]{2,1,0:T(8,128)(2,1)S(1)}, u32[]{:S(2)}, u32[]{:S(2)}) %collective-permute-start.71) | collective-permute-done | bytes 368672 | tf_op jit(solution)/shard_map/ppermute | solution.py:92
  (515 shorter events, 262.9 us)
Async XLA Ops:
  38.6 34.1 %collective-permute-start.18 = (bf16[140,1536]{1,0:T(8,128)(2,1)S(1)}, bf16[140,1536]{1,0:T(8,128)(2,1)S(1)}, u32[]{:S(2)}, u32[]{:S(2)}) collective-permute-start(bf16[140,1536]{1,0:T(8,128)(2,1)S(1)} %slice.184), channel_id=1, source_target_pairs={{0,4},{4,0},{1,5},{5,1},{2,6},{6,2},{3,7},{7,3},{8,12},{12,8},{9,1... | collective-permute-start | bytes 1290248 | tf_op jit(solution)/shard_map/ppermute | solution.py:87
  40.7 22.5 %collective-permute-start.10 = (bf16[4,2,48,1152]{3,2,1,0:T(8,128)(2,1)S(1)}, bf16[4,2,48,1152]{3,2,1,0:T(8,128)(2,1)S(1)}, u32[]{:S(2)}, u32[]{:S(2)}) collective-permute-start(bf16[4,2,48,1152]{3,2,1,0:T(8,128)(2,1)S(1)} %pad_maximum_fusion.4), channel_id=1, source_target_pairs={{0,2},{2,0},{1,3},{3,1},{4,6},{6,4},{5,7},{7,5},{8,10},{10,8},{9,1... | collective-permute-start | bytes 2654216 | tf_op jit(solution)/shard_map/ppermute | solution.py:87
  41.1 27.8 %collective-permute-start.11 = (bf16[4,2,48,1152]{3,2,1,0:T(8,128)(2,1)S(1)}, bf16[4,2,48,1152]{3,2,1,0:T(8,128)(2,1)S(1)}, u32[]{:S(2)}, u32[]{:S(2)}) collective-permute-start(bf16[4,2,48,1152]{3,2,1,0:T(8,128)(2,1)S(1)} %pad_maximum_fusion.4), channel_id=1, source_target_pairs={{0,4},{4,0},{1,5},{5,1},{2,6},{6,2},{3,7},{7,3},{8,12},{12,8},{9,1... | collective-permute-start | bytes 2654216 | tf_op jit(solution)/shard_map/ppermute | solution.py:87
  135.5 45.1 %collective-permute-start.41 = (bf16[512,1536]{1,0:T(8,128)(2,1)}, bf16[512,1536]{1,0:T(8,128)(2,1)}, u32[]{:S(2)}, u32[]{:S(2)}) collective-permute-start(bf16[512,1536]{1,0:T(8,128)(2,1)} %pad_maximum_fusion.2), channel_id=1, source_target_pairs={{0,1},{1,0},{2,3},{3,2},{4,5},{5,4},{6,7},{7,6},{8,9},{9,8},{10,11... | collective-permute-start | bytes 4718600 | tf_op jit(solution)/shard_map/ppermute | solution.py:87
  158.9 33.1 %collective-permute-start.39 = (bf16[4,2,48,1152]{3,2,1,0:T(8,128)(2,1)}, bf16[4,2,48,1152]{3,2,1,0:T(8,128)(2,1)}, u32[]{:S(2)}, u32[]{:S(2)}) collective-permute-start(bf16[4,2,48,1152]{3,2,1,0:T(8,128)(2,1)} %collective-permute-done.30), channel_id=1, source_target_pairs={{0,4},{4,0},{1,5},{5,1},{2,6},{6,2},{3,7},{7,3},{8,12},{12,8},{9,1... | collective-permute-start | bytes 2654216 | tf_op jit(solution)/shard_map/ppermute | solution.py:87
  178.1 27.4 %collective-permute-start.37 = (bf16[128,1536]{1,0:T(8,128)(2,1)S(1)}, bf16[128,1536]{1,0:T(8,128)(2,1)S(1)}, u32[]{:S(2)}, u32[]{:S(2)}) collective-permute-start(bf16[128,1536]{1,0:T(8,128)(2,1)S(1)} %get-tuple-element.219), channel_id=1, source_target_pairs={{0,16},{8,24},{16,0},{24,8},{1,17},{9,25},{17,1},{25,9},{2,18},{10... | collective-permute-start | bytes 1179656 | tf_op jit(solution)/shard_map/ppermute | solution.py:92
  178.1 27.4 %collective-permute-start.40 = (bf16[4,2,48,1152]{3,2,1,0:T(8,128)(2,1)}, bf16[4,2,48,1152]{3,2,1,0:T(8,128)(2,1)S(1)}, u32[]{:S(2)}, u32[]{:S(2)}) collective-permute-start(bf16[4,2,48,1152]{3,2,1,0:T(8,128)(2,1)} %collective-permute-done.35), channel_id=1, source_target_pairs={{0,2},{2,0},{1,3},{3,1},{4,6},{6,4},{5,7},{7,5},{8,10},{10,8},{9,1... | collective-permute-start | bytes 2654216 | tf_op jit(solution)/shard_map/ppermute | solution.py:87
  180.6 24.9 %collective-permute-start.38 = (bf16[128,1536]{1,0:T(8,128)(2,1)S(1)}, bf16[128,1536]{1,0:T(8,128)(2,1)S(1)}, u32[]{:S(2)}, u32[]{:S(2)}) collective-permute-start(bf16[128,1536]{1,0:T(8,128)(2,1)S(1)} %get-tuple-element.219), channel_id=1, source_target_pairs={{0,24},{8,0},{16,8},{24,16},{1,25},{9,1},{17,9},{25,17},{2,26},{10... | collective-permute-start | bytes 1179656 | tf_op jit(solution)/shard_map/ppermute | solution.py:92
  267.7 46.3 %collective-permute-start.48 = (bf16[4,2,2,48,1152]{4,3,2,1,0:T(8,128)(2,1)}, bf16[4,2,2,48,1152]{4,3,2,1,0:T(8,128)(2,1)}, u32[]{:S(2)}, u32[]{:S(2)}) collective-permute-start(bf16[4,2,2,48,1152]{4,3,2,1,0:T(8,128)(2,1)} %dynamic-slice_bitcast_fusion), channel_id=1, source_target_pairs={{0,2},{2,0},{1,3},{3,1},{4,6},{6,4},{5,7},{7,5},{8,10},{10,8},{9,1... | collective-permute-start | bytes 5308424 | tf_op jit(solution)/shard_map/ppermute | solution.py:87
  270.9 39.8 %collective-permute-start.47 = (bf16[4,2,2,48,1152]{4,3,2,0,1:T(8,128)(2,1)}, bf16[4,2,2,48,1152]{4,3,2,0,1:T(8,128)(2,1)}, u32[]{:S(2)}, u32[]{:S(2)}) collective-permute-start(bf16[4,2,2,48,1152]{4,3,2,0,1:T(8,128)(2,1)} %bitcast.330), channel_id=1, source_target_pairs={{0,4},{4,0},{1,5},{5,1},{2,6},{6,2},{3,7},{7,3},{8,12},{12,8},{9,1... | collective-permute-start | bytes 5308424 | tf_op jit(solution)/shard_map/ppermute | solution.py:87
  281.9 35.3 %collective-permute-start.44 = (bf16[128,1536]{1,0:T(8,128)(2,1)S(1)}, bf16[128,1536]{1,0:T(8,128)(2,1)S(1)}, u32[]{:S(2)}, u32[]{:S(2)}) collective-permute-start(bf16[128,1536]{1,0:T(8,128)(2,1)S(1)} %get-tuple-element.337), channel_id=1, source_target_pairs={{0,24},{8,0},{16,8},{24,16},{1,25},{9,1},{17,9},{25,17},{2,26},{10... | collective-permute-start | bytes 1179656 | tf_op jit(solution)/shard_map/ppermute | solution.py:92
  283.1 34.1 %collective-permute-start.45 = (bf16[128,1536]{1,0:T(8,128)(2,1)S(1)}, bf16[128,1536]{1,0:T(8,128)(2,1)S(1)}, u32[]{:S(2)}, u32[]{:S(2)}) collective-permute-start(bf16[128,1536]{1,0:T(8,128)(2,1)S(1)} %get-tuple-element.336), channel_id=1, source_target_pairs={{0,16},{8,24},{16,0},{24,8},{1,17},{9,25},{17,1},{25,9},{2,18},{10... | collective-permute-start | bytes 1179656 | tf_op jit(solution)/shard_map/ppermute | solution.py:92
  285.1 32.1 %collective-permute-start.46 = (bf16[128,1536]{1,0:T(8,128)(2,1)S(1)}, bf16[128,1536]{1,0:T(8,128)(2,1)S(1)}, u32[]{:S(2)}, u32[]{:S(2)}) collective-permute-start(bf16[128,1536]{1,0:T(8,128)(2,1)S(1)} %get-tuple-element.335), channel_id=1, source_target_pairs={{0,8},{8,16},{16,24},{24,0},{1,9},{9,17},{17,25},{25,1},{2,10},{10... | collective-permute-start | bytes 1179656 | tf_op jit(solution)/shard_map/ppermute | solution.py:92
  398.1 23.4 %collective-permute-start.62 = (bf16[2,144,1536]{2,1,0:T(8,128)(2,1)}, bf16[2,144,1536]{2,1,0:T(8,128)(2,1)}, u32[]{:S(2)}, u32[]{:S(2)}) collective-permute-start(bf16[2,144,1536]{2,1,0:T(8,128)(2,1)} %dynamic-slice_bitcast_fusion.1), channel_id=1, source_target_pairs={{0,2},{2,0},{1,3},{3,1},{4,6},{6,4},{5,7},{7,5},{8,10},{10,8},{9,1... | collective-permute-start | bytes 2654216 | tf_op jit(solution)/shard_map/ppermute | solution.py:87
  399.8 23.4 %collective-permute-start.61 = (bf16[2,144,1536]{2,1,0:T(8,128)(2,1)}, bf16[2,144,1536]{2,1,0:T(8,128)(2,1)}, u32[]{:S(2)}, u32[]{:S(2)}) collective-permute-start(bf16[2,144,1536]{2,1,0:T(8,128)(2,1)} %dynamic-slice_bitcast_fusion.2), channel_id=1, source_target_pairs={{0,4},{4,0},{1,5},{5,1},{2,6},{6,2},{3,7},{7,3},{8,12},{12,8},{9,1... | collective-permute-start | bytes 2654216 | tf_op jit(solution)/shard_map/ppermute | solution.py:87
  424.8 31.1 %collective-permute-start.63 = (bf16[4,2,2,48,896]{4,3,2,0,1:T(8,128)(2,1)S(1)}, bf16[4,2,2,48,896]{4,3,2,0,1:T(8,128)(2,1)S(1)}, u32[]{:S(2)}, u32[]{:S(2)}) collective-permute-start(bf16[4,2,2,48,896]{4,3,2,0,1:T(8,128)(2,1)S(1)} %copy_bitcast_fusion.3), channel_id=1, source_target_pairs={{0,4},{4,0},{1,5},{5,1},{2,6},{6,2},{3,7},{7,3},{8,12},{12,8},{9,1... | collective-permute-start | bytes 4128776 | tf_op jit(solution)/shard_map/ppermute | solution.py:87
  425.8 35.0 %collective-permute-start.64 = (bf16[4,2,2,48,1024]{4,3,2,0,1:T(8,128)(2,1)S(1)}, bf16[4,2,2,48,1024]{4,3,2,0,1:T(8,128)(2,1)S(1)}, u32[]{:S(2)}, u32[]{:S(2)}) collective-permute-start(bf16[4,2,2,48,1024]{4,3,2,0,1:T(8,128)(2,1)S(1)} %copy_bitcast_fusion.2), channel_id=1, source_target_pairs={{0,2},{2,0},{1,3},{3,1},{4,6},{6,4},{5,7},{7,5},{8,10},{10,8},{9,1... | collective-permute-start | bytes 4718600 | tf_op jit(solution)/shard_map/ppermute | solution.py:87
  427.1 34.5 %collective-permute-start.65 = (bf16[2,2,48,1152]{3,2,1,0:T(8,128)(2,1)S(1)}, bf16[2,2,48,1152]{3,2,1,0:T(8,128)(2,1)S(1)}, u32[]{:S(2)}, u32[]{:S(2)}) collective-permute-start(bf16[2,2,48,1152]{3,2,1,0:T(8,128)(2,1)S(1)} %get-tuple-element.318), channel_id=1, source_target_pairs={{0,8},{8,16},{16,24},{24,0},{1,9},{9,17},{17,25},{25,1},{2,10},{10... | collective-permute-start | bytes 1327112 | tf_op jit(solution)/shard_map/ppermute | solution.py:92
  430.4 35.8 %collective-permute-start.66 = (bf16[2,2,48,1152]{3,2,1,0:T(8,128)(2,1)S(1)}, bf16[2,2,48,1152]{3,2,1,0:T(8,128)(2,1)S(1)}, u32[]{:S(2)}, u32[]{:S(2)}) collective-permute-start(bf16[2,2,48,1152]{3,2,1,0:T(8,128)(2,1)S(1)} %get-tuple-element.317), channel_id=1, source_target_pairs={{0,16},{8,24},{16,0},{24,8},{1,17},{9,25},{17,1},{25,9},{2,18},{10... | collective-permute-start | bytes 1327112 | tf_op jit(solution)/shard_map/ppermute | solution.py:92
  430.4 35.8 %collective-permute-start.67 = (bf16[2,2,48,1152]{3,2,1,0:T(8,128)(2,1)S(1)}, bf16[2,2,48,1152]{3,2,1,0:T(8,128)(2,1)S(1)}, u32[]{:S(2)}, u32[]{:S(2)}) collective-permute-start(bf16[2,2,48,1152]{3,2,1,0:T(8,128)(2,1)S(1)} %get-tuple-element.316), channel_id=1, source_target_pairs={{0,24},{8,0},{16,8},{24,16},{1,25},{9,1},{17,9},{25,17},{2,26},{10... | collective-permute-start | bytes 1327112 | tf_op jit(solution)/shard_map/ppermute | solution.py:92
  483.8 35.0 %collective-permute-start.71 = (bf16[2,48,1920]{2,1,0:T(8,128)(2,1)S(1)}, bf16[2,48,1920]{2,1,0:T(8,128)(2,1)S(1)}, u32[]{:S(2)}, u32[]{:S(2)}) collective-permute-start(bf16[2,48,1920]{2,1,0:T(8,128)(2,1)S(1)} %get-tuple-element.340), channel_id=1, source_target_pairs={{0,16},{8,24},{16,0},{24,8},{1,17},{9,25},{17,1},{25,9},{2,18},{10... | collective-permute-start | bytes 1105928 | tf_op jit(solution)/shard_map/ppermute | solution.py:92
  488.6 30.2 %collective-permute-start.72 = (bf16[2,48,1920]{2,1,0:T(8,128)(2,1)S(1)}, bf16[2,48,1920]{2,1,0:T(8,128)(2,1)S(1)}, u32[]{:S(2)}, u32[]{:S(2)}) collective-permute-start(bf16[2,48,1920]{2,1,0:T(8,128)(2,1)S(1)} %get-tuple-element.339), channel_id=1, source_target_pairs={{0,24},{8,0},{16,8},{24,16},{1,25},{9,1},{17,9},{25,17},{2,26},{10... | collective-permute-start | bytes 1105928 | tf_op jit(solution)/shard_map/ppermute | solution.py:92
  490.0 32.1 %collective-permute-start.74 = (bf16[144,1536]{1,0:T(8,128)(2,1)S(1)}, bf16[144,1536]{1,0:T(8,128)(2,1)S(1)}, u32[]{:S(2)}, u32[]{:S(2)}) collective-permute-start(bf16[144,1536]{1,0:T(8,128)(2,1)S(1)} %dynamic-slice_bitcast_fusion.10), channel_id=1, source_target_pairs={{0,2},{2,0},{1,3},{3,1},{4,6},{6,4},{5,7},{7,5},{8,10},{10,8},{9,1... | collective-permute-start | bytes 1327112 | tf_op jit(solution)/shard_map/ppermute | solution.py:87
  490.5 31.7 %collective-permute-start.75 = (bf16[144,1536]{1,0:T(8,128)(2,1)S(1)}, bf16[144,1536]{1,0:T(8,128)(2,1)S(1)}, u32[]{:S(2)}, u32[]{:S(2)}) collective-permute-start(bf16[144,1536]{1,0:T(8,128)(2,1)S(1)} %dynamic-slice_bitcast_fusion.9), channel_id=1, source_target_pairs={{0,4},{4,0},{1,5},{5,1},{2,6},{6,2},{3,7},{7,3},{8,12},{12,8},{9,1... | collective-permute-start | bytes 1327112 | tf_op jit(solution)/shard_map/ppermute | solution.py:87
  (127 other events, 1488.8 us)

commit v3 on v1

v3 whole, which is shorter than its diff:
```python
import math

import jax
import jax.numpy as jnp
from jax import lax
from jax.experimental import pallas as pl
from jax.experimental.pallas import tpu as pltpu
from jax.sharding import Mesh
from jax.sharding import PartitionSpec as P

H = 12
KV = 2
HD = 128
HPG = 6

epsilon = 1e-06
rope_base = 10000.0
masked_value = -1e30

EVERY = ("z", "y", "x", "c")
ROW = ("y", "x", "c")
PLANE = ("y", "x")


def low(values):
    return values.astype(jnp.bfloat16)


def wide(values):
    return values.astype(jnp.float32)


def nn(left, right):
    return jnp.dot(left, right, preferred_element_type=jnp.float32)


def nt(left, right):
    return lax.dot_general(
        left, right, (((1,), (1,)), ((), ())), preferred_element_type=jnp.float32
    )


def tn(left, right):
    return lax.dot_general(
        left, right, (((0,), (0,)), ((), ())), preferred_element_type=jnp.float32
    )


def doc_tables(doc_ends, doc_lengths, positions):
    passed = doc_ends[:, None, :] <= positions[None, :, None]
    doc_index = jnp.sum(passed.astype(jnp.int32), axis=-1)
    starts = jnp.sum(jnp.where(passed, doc_lengths[:, None, :], 0), axis=-1)
    return (doc_index, positions[None, :] - starts)


def rope_tables(within):
    steps_even = jnp.arange(0, HD, 2).astype(jnp.float32)
    inverse = rope_base ** (-steps_even / HD)
    phase = within.astype(jnp.float32)[:, None] * inverse[None, :]
    phase = jnp.concatenate([phase, phase], axis=-1)
    return jnp.cos(phase), jnp.sin(phase)


def square():
    return lax.axis_size("y") == 2 and lax.axis_size("x") == 2


def places():
    y, x = lax.axis_index("y"), lax.axis_index("x")
    if square():
        return [(y, x), (y, 1 - x), (1 - y, x), (1 - y, 1 - x)]
    return [(i, j) for i in range(lax.axis_size("y")) for j in range(lax.axis_size("x"))]


def chip_positions(y, x, shard_tokens):
    core = lax.axis_index("c")
    place = (y * lax.axis_size("x") + x) * 2
    lanes = jnp.arange(shard_tokens, dtype=jnp.int32)
    return [(place + k) * shard_tokens + lanes for k in (core, 1 - core)]


def position_tables(doc_lengths, shard_tokens):
    local_rows = doc_lengths.shape[0]
    query_pos = jnp.concatenate(
        chip_positions(lax.axis_index("y"), lax.axis_index("x"), shard_tokens)
    )
    key_pos = jnp.concatenate(
        [p for place in places() for p in chip_positions(*place, shard_tokens)]
    )
    doc_ends = jnp.cumsum(doc_lengths, axis=1)
    query_doc, query_within = doc_tables(doc_ends, doc_lengths, query_pos)
    key_doc, unused_within = doc_tables(doc_ends, doc_lengths, key_pos)
    allowed = (query_doc[:, :, None] == key_doc[:, None, :]) & (
        key_pos[None, None, :] <= query_pos[None, :, None]
    )
    query_within = query_within.reshape(local_rows, 2, shard_tokens).transpose(1, 0, 2)
    cosine, sine = rope_tables(query_within.reshape(-1))
    sign = jnp.where(jnp.arange(HD) < HD // 2, -1.0, 1.0)
    return cosine, sine * sign, wide(allowed)


def sync(*values):
    return lax.optimization_barrier(values)


def after(values, *others):
    return lax.optimization_barrier((values, others))[0]


def swapped(values, axis):
    return lax.ppermute(values, axis, [(0, 1), (1, 0)])


def shifted(values, amount):
    count = lax.axis_size("z")
    return lax.ppermute(values, "z", [(i, (i + amount) % count) for i in range(count)])


def every_shift():
    return range(1, lax.axis_size("z"))


def near_shifts():
    return sorted({1, lax.axis_size("z") - 1})


def far_shifts():
    return range(2, lax.axis_size("z") - 1)


def depth_gathered(rows, shifts):
    return {k: shifted(rows, k) for k in shifts}


def depth_sent(blocks, shifts):
    return {k: shifted(blocks[k], k) for k in shifts}


def in_order(pieces):
    return [pieces[k] for k in sorted(pieces)]


def plane_near(values):
    return swapped(values, "x"), swapped(values, "y")


def plane_gathered(rows):
    if not square():
        return lax.all_gather(rows, PLANE, axis=0)
    pair = jnp.stack([rows, swapped(rows, "x")])
    return jnp.concatenate([pair, swapped(pair, "y")], axis=0)


def plane_summed(blocks):
    if not square():
        return wide(lax.psum_scatter(blocks, PLANE, scatter_dimension=0, tiled=False))
    pair = low(wide(blocks[:2]) + wide(swapped(blocks[2:], "y")))
    return wide(pair[0]) + wide(swapped(pair[1], "x"))


def plane_whole(own):
    own = jnp.where(lax.axis_index("c") == 0, own, own[:, ::-1])
    whole = lax.all_gather(own, PLANE, axis=1, tiled=False)
    ny, nx = lax.axis_size("y"), lax.axis_size("x")
    return whole.reshape(own.shape[:1] + (ny, nx) + own.shape[1:])


LITTLE = pl.CostEstimate(flops=1, bytes_accessed=1, transcendentals=0)
SPACE = pltpu.CompilerParams(vmem_limit_bytes=48 << 20)
VMEM = pl.BlockSpec(memory_space=pltpu.VMEM)
SMEM = pl.BlockSpec(memory_space=pltpu.SMEM)


def shape_of(dims, kind=jnp.bfloat16):
    return jax.ShapeDtypeStruct(tuple(dims), kind)


def run(kernel, shapes, here, *arrays):
    return pl.pallas_call(
        kernel,
        in_specs=[SMEM] + [VMEM] * len(arrays),
        out_specs=[VMEM] * len(shapes),
        out_shape=list(shapes),
        compiler_params=SPACE,
        cost_estimate=LITTLE,
    )(here, *arrays)


def run_grid(kernel, grid, specs, outs, here, *arrays):
    return pl.pallas_call(
        kernel,
        grid=(grid,),
        in_specs=[SMEM] + list(specs),
        out_specs=[spec for spec, shape in outs],
        out_shape=[shape for spec, shape in outs],
        compiler_params=SPACE,
        cost_estimate=LITTLE,
    )(here, *arrays)


def whole_block(array):
    dims = len(array.shape)
    return pl.BlockSpec(array.shape, lambda i: (0,) * dims)


def lead_block(shape):
    dims = len(shape)
    return pl.BlockSpec((1,) + tuple(shape[1:]), lambda i: (i,) + (0,) * (dims - 1))


def around(z, k, count):
    return lax.rem(z + (k + count), count)


def split_shares(here, pieces, gate_weight, up_weight, sizes, unit, lane, query_width, key_width):
    nz, ny, nx, nc = sizes
    rows = gate_weight.shape[0]
    half = query_width // 2
    hidden_width = lane * ny * nx
    inner_width = half + 2 * HD + 128
    count = len(pieces)

    def columns(piece, of):
        first, second = query_width + of * HD, query_width + key_width + of * HD
        return jnp.concatenate(
            [
                piece[:, of * half : (of + 1) * half],
                piece[:, first : first + HD],
                piece[:, second : second + HD],
                piece[:, query_width + 2 * key_width :],
            ],
            axis=1,
        )

    def kernel(here_ref, *refs):
        piece_refs, (gate_ref, up_ref) = refs[:count], refs[count : count + 2]
        mine_ref, share_ref, send_ref, send_share_ref = refs[count + 2 :]
        core = here_ref[3]
        for k, ref in enumerate(piece_refs):
            at = around(here_ref[0], -k, nz)
            piece = ref[...]
            zero, one = columns(piece, 0), columns(piece, 1)
            mine_ref[at] = jnp.where(core == 0, zero, one)
            send_ref[at] = jnp.where(core == 0, one, zero)
        share_ref[...] = jnp.zeros_like(share_ref)
        send_share_ref[...] = jnp.zeros_like(send_share_ref)
        for own in range(nc):

            @pl.when(core == own)
            def _():
                for m, ref in enumerate((gate_ref, up_ref)):
                    for d in range(nz * ny * nx * nc):
                        z, p, c = d // (ny * nx * nc), d // nc % (ny * nx), d % nc
                        out = share_ref if c == own else send_share_ref
                        out[z, m, :, lane * p : lane * p + unit] = ref[
                            :, unit * d : unit * d + unit
                        ]

    return run(
        kernel,
        (
            shape_of((nz, rows, inner_width)),
            shape_of((nz, 2, rows, hidden_width)),
            shape_of((nz, rows, inner_width)),
            shape_of((nz, 2, rows, hidden_width)),
        ),
        here,
        *pieces,
        gate_weight,
        up_weight,
    )


def share_blocks(here, mine, came):
    nz = mine.shape[0]

    def kernel(here_ref, mine_ref, came_ref, *outs):
        for k, out in enumerate(outs):
            at = around(here_ref[0], k, nz)
            out[0] = mine_ref[at]
            out[1] = came_ref[at]

    return run(kernel, [shape_of((2,) + mine.shape[1:])] * nz, here, mine, came)


def split_output(here, pieces):
    nz = len(pieces)
    rows, width = pieces[0].shape
    half = width // 2

    def kernel(here_ref, *refs):
        mine_ref, other_ref = refs[nz:]
        first = here_ref[3] == 0
        for k, ref in enumerate(refs[:nz]):
            at = around(here_ref[0], -k, nz)
            left, right = ref[:, :half], ref[:, half:]
            mine_ref[at] = jnp.where(first, left, right)
            other_ref[at] = jnp.where(first, right, left)

    return run(kernel, [shape_of((nz, rows, half))] * 2, here, *pieces)


def place_shares(here, pieces):
    nz = len(pieces)

    def kernel(here_ref, *refs):
        gate_ref, up_ref = refs[nz:]
        for k, ref in enumerate(refs[:nz]):
            at = around(here_ref[0], -k, nz)
            for i in range(2):
                gate_ref[at, i] = ref[i, 0]
                up_ref[at, i] = ref[i, 1]

    return run(kernel, [shape_of((nz, 2) + pieces[0].shape[2:])] * 2, here, *pieces)


def assemble(here_ref, refs, out):
    y, x, c = here_ref[1], here_ref[2], here_ref[3]
    own, from_x, from_y, *far = refs
    for ref, at_y, at_x in ((own, y, x), (from_x, y, 1 - x), (from_y, 1 - y, x)):
        for z in range(out.shape[0]):
            for i in range(2):
                out[z, at_y, at_x, c if i == 0 else 1 - c] = ref[z, i]
    for z in range(out.shape[0]):
        for i in range(2):
            block = [ref[z, i] for ref in far]
            block = block[0] if len(block) == 1 else jnp.concatenate(block, axis=1)
            out[z, 1 - y, 1 - x, c if i == 0 else 1 - c] = block


def six(own):
    return (own.shape[0], lax.axis_size("y"), lax.axis_size("x")) + own.shape[1:]


def turn(values, cosine, sine):
    return values * cosine + pltpu.roll(values, HD // 2, 1) * sine


def turn_back(values, cosine, sine):
    return values * cosine + pltpu.roll(values * sine, HD // 2, 1)


def key_places(core, width, owned, owned_key, shift):
    source = lax.broadcasted_iota(jnp.int32, (width, HD), 0)
    feature = lax.broadcasted_iota(jnp.int32, (width, HD), 1) + core * HD
    place = feature // owned_key * owned + feature % owned_key + shift
    return low(wide(source == place))


def inner_projections(here, own, other, weights, cosine, sine, owned, owned_key):
    local_rows, count, width = own.shape
    total = 2 * local_rows * count
    half = width // 2
    tables = len(weights)
    pieces = tables > 1
    dims = six(weights[0]) if pieces else weights[0].shape
    columns = dims[-1]

    def kernel(here_ref, own_ref, other_ref, cos_ref, sin_ref, *refs):
        weight_refs = refs[:tables]
        n_ref, q_ref, pair_ref, line_ref = refs[tables : tables + 4]
        if pieces:
            assemble(here_ref, weight_refs, refs[-1])
            weight = refs[-1][...].reshape(width, columns)
        else:
            weight = weight_refs[0][...]
        lines = wide(weight[:, columns - 128 :]).T
        core = here_ref[3]
        values = jnp.concatenate([own_ref[...], other_ref[...]], axis=0)
        values = wide(values.reshape(total, width))
        scale = lax.rsqrt(jnp.mean(values * values, axis=-1, keepdims=True) + epsilon)
        normed = low(values * scale * lines[1:2])
        n_ref[...] = normed
        line_ref[...] = lines[:8]
        small = low(lines[3:4])
        key_bias = nn(small, key_places(core, width, owned, owned_key, 0))
        value_bias = nn(small, key_places(core, width, owned, owned_key, owned_key))
        bias = jnp.where(core == 0, lines[0:1, :half], lines[0:1, half:])
        pre = nn(normed, weight[:, : half + 2 * HD])
        cosine, sine = cos_ref[...], sin_ref[...]
        for h in range(HPG):
            block = slice(h * HD, (h + 1) * HD)
            query = low(turn(pre[:, block] + bias[:, block], cosine, sine))
            query = query.reshape(2, local_rows, count, HD)
            for r in range(local_rows):
                q_ref[r, h] = query[:, r]
        key = low(turn(pre[:, half : half + HD] + key_bias, cosine, sine))
        value = low(pre[:, half + HD : half + 2 * HD] + value_bias)
        shape = (2, local_rows, count, HD)
        pair_ref[..., :HD] = key.reshape(shape)
        pair_ref[..., HD:] = value.reshape(shape)

    shapes = [
        shape_of((total, width)),
        shape_of((local_rows, HPG, 2, count, HD)),
        shape_of((2, local_rows, count, 2 * HD)),
        shape_of((8, width), jnp.float32),
    ]
    if pieces:
        shapes.append(shape_of(dims))
    out = run(kernel, shapes, here, own, other, cosine, sine, *weights)
    return out if pieces else list(out) + [weights[0]]


def row_scores(query, keys, allowed):
    return jnp.where(allowed, nt(query, keys) * (1.0 / math.sqrt(HD)), masked_value)


def row_specs(pairs, count):
    keys = pl.BlockSpec((pairs.shape[0], 2, 1, count, 2 * HD), lambda r: (0, 0, r, 0, 0))
    queries = pl.BlockSpec((1, HPG, 2, count, HD), lambda r: (r, 0, 0, 0, 0))
    flat = pl.BlockSpec((2, 1, count, HPG * HD), lambda r: (0, r, 0, 0))
    stats = pl.BlockSpec((1, HPG, 2 * count, HD), lambda r: (r, 0, 0, 0))
    allowed = pl.BlockSpec((1, 2 * count, pairs.shape[0] * 2 * count), lambda r: (r, 0, 0))
    return keys, queries, flat, stats, allowed


def attend(here, queries, pairs, allowed):
    local_rows, heads, cores, count, hd = queries.shape
    total = 2 * count
    keys, query_spec, flat, stats, allowed_spec = row_specs(pairs, count)

    def kernel(here_ref, q_ref, pair_ref, allowed_ref, out_ref, other_ref, stat_ref):
        pair = pair_ref[...].reshape(-1, 2 * HD)
        key, value = pair[:, :HD], pair[:, HD:]
        seen = allowed_ref[0] > 0
        for h in range(heads):
            scores = row_scores(q_ref[0, h].reshape(total, HD), key, seen)
            top = jnp.max(scores, axis=-1, keepdims=True)
            log_total = top + jnp.log(jnp.sum(jnp.exp(scores - top), axis=-1, keepdims=True))
            mixed = low(nn(low(jnp.exp(scores - log_total)), value)).reshape(2, count, HD)
            columns = slice(h * HD, (h + 1) * HD)
            for c in range(2):
                out_ref[c, 0, :, columns] = mixed[c]
                other_ref[1 - c, 0, :, columns] = mixed[c]
            stat_ref[0, h] = jnp.broadcast_to(log_total, (total, HD))

    flat_shape = shape_of((2, local_rows, count, heads * HD))
    stat_shape = shape_of((local_rows, heads, total, HD), jnp.float32)
    return run_grid(
        kernel,
        local_rows,
        [query_spec, keys, allowed_spec],
        [(flat, flat_shape), (flat, flat_shape), (stats, stat_shape)],
        here,
        queries,
        pairs,
        allowed,
    )


def attend_back(here, queries, pairs, allowed, stats, grads, came, cosine, sine):
    local_rows, heads, cores, count, hd = queries.shape
    total = 2 * count
    spots = pairs.shape[0]
    scaling = 1.0 / math.sqrt(HD)
    keys, query_spec, flat, stat_spec, allowed_spec = row_specs(pairs, count)
    table = pl.BlockSpec((2, 1, count, HD), lambda r: (0, r, 0, 0))
    half_keys = pl.BlockSpec((spots // 2, 2, 1, count, 2 * HD), lambda r: (0, 0, r, 0, 0))

    def kernel(here_ref, q_ref, pair_ref, allowed_ref, stat_ref, grad_ref, came_ref, cos_ref, sin_ref, out_ref, *parts):
        pair = pair_ref[...].reshape(-1, 2 * HD)
        key, value = pair[:, :HD], pair[:, HD:]
        seen = allowed_ref[0] > 0
        cosine, sine = (ref[...].reshape(total, HD) for ref in (cos_ref, sin_ref))
        key_part = jnp.zeros(key.shape, jnp.float32)
        value_part = jnp.zeros(key.shape, jnp.float32)
        for h in range(heads):
            columns = slice(h * HD, (h + 1) * HD)
            query = q_ref[0, h].reshape(total, HD)
            grad = low(grad_ref[:, 0, :, columns] + came_ref[:, 0, :, columns]).reshape(total, HD)
            probs = jnp.exp(row_scores(query, key, seen) - stat_ref[0, h][:, :1])
            back = nt(grad, value)
            delta = jnp.sum(probs * back, axis=-1, keepdims=True)
            score_grad = low(probs * (back - delta))
            key_part = key_part + tn(score_grad, query)
            value_part = value_part + tn(low(probs), grad)
            query_sum = nn(score_grad, key) * scaling
            turned = low(turn_back(query_sum, cosine, sine))
            out_ref[:, 0, :, columns] = turned.reshape(2, count, HD)
        shape = (2, spots // 2, 2, count, HD)
        key_part = low(key_part * scaling).reshape(shape)
        value_part = low(value_part).reshape(shape)
        for i, ref in enumerate(parts):
            ref[:, :, 0, :, :HD] = key_part[i]
            ref[:, :, 0, :, HD:] = value_part[i]

    part_shape = shape_of((spots // 2,) + pairs.shape[1:])
    return run_grid(
        kernel,
        local_rows,
        [query_spec, keys, allowed_spec, stat_spec, flat, flat, table, table],
        [
            (flat, shape_of((2, local_rows, count, heads * HD))),
            (half_keys, part_shape),
            (half_keys, part_shape),
        ],
        here,
        queries,
        pairs,
        allowed,
        stats,
        grads,
        came,
        cosine,
        sine,
    )


def output_projection(here, attended, came, weights):
    total, half = attended.shape
    width = 2 * half
    tables = len(weights)
    pieces = tables > 1
    dims = six(weights[0]) if pieces else weights[0].shape

    def kernel(here_ref, own_ref, came_ref, *refs):
        weight_refs = refs[:tables]
        part_ref, other_ref, all_ref = refs[tables : tables + 3]
        if pieces:
            assemble(here_ref, weight_refs, refs[-1])
            weight = refs[-1][...].reshape(width, half)
        else:
            weight = weight_refs[0][...]
        own, came = own_ref[...], came_ref[...]
        first = here_ref[3] == 0
        heads = jnp.concatenate([jnp.where(first, own, came), jnp.where(first, came, own)], axis=1)
        all_ref[...] = heads
        part = nn(heads, weight)
        part_ref[...] = part[: total // 2]
        other_ref[...] = part[total // 2 :]

    part_shape = shape_of((total // 2, half), jnp.float32)
    shapes = [part_shape, part_shape, shape_of((total, width))]
    if pieces:
        shapes.append(shape_of(dims))
    out = run(kernel, shapes, here, attended, came, *weights)
    return out if pieces else list(out) + [weights[0]]


def joined(first, own, came):
    return jnp.concatenate([jnp.where(first, own, came), jnp.where(first, came, own)], axis=1)


def second_norm(here, tokens, part, came, lines):
    count, width = tokens.shape

    def kernel(here_ref, tokens_ref, part_ref, came_ref, line_ref, hidden_ref, normed_ref):
        hidden = wide(tokens_ref[...]) + joined(here_ref[3] == 0, part_ref[...], came_ref[...])
        scale = lax.rsqrt(jnp.mean(hidden * hidden, axis=-1, keepdims=True) + epsilon)
        hidden_ref[...] = hidden
        normed_ref[...] = low(hidden * scale * line_ref[2:3])

    shapes = (shape_of((count, width), jnp.float32), shape_of((count, width)))
    return run(kernel, shapes, here, tokens, part, came, lines)


def halves_specs(width, tile, steps):
    first = pl.BlockSpec((tile, width), lambda i: (jnp.minimum(i, steps - 1), 0))
    second = pl.BlockSpec((tile, width), lambda i: (jnp.maximum(i - steps, 0), 0))
    return first, second


def feed_forward(here, normed, upstream, weights, weight_down):
    count, width = normed[0].shape
    hidden_width = weight_down.shape[0]
    tile = min(256, count)
    steps = count // tile
    tables = len(weights)
    pieces = tables > 2
    chunk = hidden_width // 3 if hidden_width % 384 == 0 else hidden_width
    spec_a, spec_b = halves_specs(width, tile, steps)

    def kernel(here_ref, na_ref, nb_ref, ua_ref, ub_ref, wd, *refs):
        weight_refs = refs[:tables]
        grad_a, grad_b, hidden_ref, gate_ref, up_ref = refs[tables : tables + 5]
        step = pl.program_id(0)
        if pieces:
            scratch = refs[-2:]

            @pl.when(step == 0)
            def _():
                assemble(here_ref, weight_refs[: tables // 2], scratch[0])
                assemble(here_ref, weight_refs[tables // 2 :], scratch[1])

            wg, wu = (ref[...].reshape(width, hidden_width) for ref in scratch)
        else:
            wg, wu = (ref[...] for ref in weight_refs)
        early = step < steps
        normed = jnp.where(early, na_ref[...], nb_ref[...])
        upstream = jnp.where(early, ua_ref[...], ub_ref[...])
        for k in range(0, hidden_width, chunk):
            columns = slice(k, k + chunk)
            gate = nn(normed, wg[:, columns])
            up = nn(normed, wu[:, columns])
            back = nt(upstream, wd[columns, :])
            sigmoid = jax.nn.sigmoid(gate)
            silu = gate * sigmoid
            hidden_ref[:, columns] = low(silu * up)
            gate_ref[:, columns] = low(back * up * sigmoid * (1.0 + gate * (1.0 - sigmoid)))
            up_ref[:, columns] = low(back * silu)
        grad = low(nt(gate_ref[...], wg) + nt(up_ref[...], wu))

        @pl.when(early)
        def _():
            grad_a[...] = grad

        @pl.when(jnp.logical_not(early))
        def _():
            grad_b[...] = grad

    rows = pl.BlockSpec((tile, hidden_width), lambda i: (i, 0))
    group = shape_of((count, width))
    wide_rows = shape_of((2 * count, hidden_width))
    scratch = [pltpu.VMEM(six(weights[0]), jnp.bfloat16)] * 2 if pieces else []
    return pl.pallas_call(
        kernel,
        grid=(2 * steps,),
        in_specs=[SMEM, spec_a, spec_b, spec_a, spec_b, whole_block(weight_down)]
        + [whole_block(w) for w in weights],
        out_specs=[spec_a, spec_b, rows, rows, rows],
        out_shape=[group, group, wide_rows, wide_rows, wide_rows],
        scratch_shapes=scratch,
        compiler_params=pltpu.CompilerParams(vmem_limit_bytes=56 << 20),
        cost_estimate=LITTLE,
    )(here, *normed, *upstream, weight_down, *weights)


def feed_forward_output(here, hidden, weight_down):
    count = hidden.shape[0] // 2
    width = weight_down.shape[1]
    tile = min(256, count)
    steps = count // tile
    specs = halves_specs(width, tile, steps)

    def kernel(here_ref, hidden_ref, weight_ref, out_a, out_b):
        part = low(nn(hidden_ref[...], weight_ref[...]))

        @pl.when(pl.program_id(0) < steps)
        def _():
            out_a[...] = part

        @pl.when(pl.program_id(0) >= steps)
        def _():
            out_b[...] = part

    rows = pl.BlockSpec((tile, hidden.shape[1]), lambda i: (i, 0))
    shape = shape_of((count, width))
    return run_grid(
        kernel,
        2 * steps,
        [rows, whole_block(weight_down)],
        [(spec, shape) for spec in specs],
        here,
        hidden,
        weight_down,
    )


def column_block(array, width):
    return pl.BlockSpec((array.shape[0], width), lambda i: (0, i))


def weight_grads(here, lefts, rights):
    counts = [v.shape[0] for v in lefts]
    rows = lefts[0].shape[1]
    tile = 384 if rows % 384 == 0 else 128
    number = len(lefts)

    def kernel(here_ref, *refs):
        turned = jnp.concatenate([ref[...] for ref in refs[:number]], axis=0).T
        for right, out in zip(refs[number : number + len(rights)], refs[number + len(rights) :]):
            out[...] = low(nn(turned, right[...]))

    return run_grid(
        kernel,
        rows // tile,
        [column_block(v, tile) for v in lefts] + [whole_block(v) for v in rights],
        [
            (pl.BlockSpec((tile, v.shape[1]), lambda i: (i, 0)), shape_of((rows, v.shape[1])))
            for v in rights
        ],
        here,
        *lefts,
        *rights,
    )


def split_by_plane(here_ref, first, second, refs, rows):
    y, x = here_ref[1], here_ref[2]
    first_send, first_keep, second_send, second_keep = refs
    first = first.reshape(2, 2, rows, first.shape[1])
    second = second.reshape(2, 2, rows, second.shape[1])
    first_send[0] = jnp.where(y == 0, first[1], first[0])
    first_keep[0] = jnp.where(y == 0, first[0], first[1])
    second_send[0] = jnp.where(x == 0, second[:, 1], second[:, 0])
    second_keep[0] = jnp.where(x == 0, second[:, 0], second[:, 1])


def plane_outs(nz, rows, first, second):
    shapes = [shape_of((nz, 2, rows, n)) for n in (first, first, second, second)]
    return [(lead_block(s.shape), s) for s in shapes]


def share_grads(here, lefts, first, second, nz, rows, vectors=None):
    width = lefts[0].shape[1]
    block = width // nz
    number = len(lefts)
    (first, first_from, first_to), (second, second_from, second_to) = first, second
    arrays = list(lefts) + [first, second] + ([] if vectors is None else [vectors])

    def kernel(here_ref, *refs):
        turned = jnp.concatenate([ref[...] for ref in refs[:number]], axis=0).T
        one = low(nn(turned, refs[number][:, first_from:first_to]))
        two = low(nn(turned, refs[number + 1][:, second_from:second_to]))
        if vectors is not None:
            filled = jnp.concatenate(
                [refs[number + 2][...], jnp.zeros((120, block), jnp.float32)], axis=0
            )
            two = jnp.concatenate([two, low(filled.T)], axis=1)
        split_by_plane(here_ref, one, two, refs[len(arrays) :], rows)

    extra = 0 if vectors is None else 128
    return run_grid(
        kernel,
        nz,
        [column_block(v, block) for v in lefts]
        + [whole_block(first), whole_block(second)]
        + ([] if vectors is None else [column_block(vectors, block)]),
        plane_outs(nz, rows, first_to - first_from, second_to - second_from + extra),
        here,
        *arrays,
    )


def plane_step(here, keeps, cames):
    nz = keeps[0].shape[0]

    def kernel(here_ref, first_ref, first_came, second_ref, second_came, *outs):
        y, x = here_ref[1], here_ref[2]
        first = low(wide(first_ref[0]) + wide(first_came[0]))
        second = low(wide(second_ref[0]) + wide(second_came[0]))
        for value, at, send, keep in ((first, x, *outs[:2]), (second, y, *outs[2:])):
            send[0] = jnp.where(at == 0, value[1], value[0])
            keep[0] = jnp.where(at == 0, value[0], value[1])

    shapes = []
    for v in keeps:
        shapes += [shape_of((nz,) + v.shape[2:])] * 2
    return run_grid(
        kernel,
        nz,
        [lead_block(v.shape) for v in (keeps[0], cames[0], keeps[1], cames[1])],
        [(lead_block(s.shape), s) for s in shapes],
        here,
        keeps[0],
        cames[0],
        keeps[1],
        cames[1],
    )


def share_sums(here, keeps, cames):
    nz, cores, rows, width = keeps[0].shape

    def kernel(here_ref, g_ref, g_came, u_ref, u_came, mine_ref, send_ref):
        core = here_ref[3]
        for m, (ref, came) in enumerate(((g_ref, g_came), (u_ref, u_came))):
            mine_ref[0, m] = low(wide(ref[0, core]) + wide(came[0, core]))
            send_ref[0, m] = low(wide(ref[0, 1 - core]) + wide(came[0, 1 - core]))

    shape = shape_of((nz, 2, rows, width))
    arrays = (keeps[0], cames[0], keeps[1], cames[1])
    return run_grid(
        kernel,
        nz,
        [lead_block(v.shape) for v in arrays],
        [(lead_block(shape.shape), shape)] * 2,
        here,
        *arrays,
    )


def collect_columns(here, pieces, sizes, unit, lane):
    nz, ny, nx, nc = sizes
    rows = pieces[0].shape[2]

    def kernel(here_ref, *refs):
        gate_ref, up_ref, placed = refs[nz:]
        core = here_ref[3]
        for k, ref in enumerate(refs[:nz]):
            at = around(here_ref[0], -k, nz)
            placed[at, core] = ref[0]
            placed[at, 1 - core] = ref[1]
        for m, ref in enumerate((gate_ref, up_ref)):
            for d in range(nz * ny * nx * nc):
                z, p, c = d // (ny * nx * nc), d // nc % (ny * nx), d % nc
                ref[:, unit * d : unit * d + unit] = wide(
                    placed[z, c, m, :, lane * p : lane * p + unit]
                )

    shape = shape_of((rows, unit * nz * ny * nx * nc), jnp.float32)
    return pl.pallas_call(
        kernel,
        in_specs=[SMEM] + [VMEM] * nz,
        out_specs=[VMEM] * 2,
        out_shape=[shape, shape],
        scratch_shapes=[pltpu.VMEM((nz,) + pieces[0].shape, jnp.bfloat16)],
        compiler_params=SPACE,
        cost_estimate=LITTLE,
    )(here, *pieces)


def down_grads(here, hidden, upstream, lane):
    hidden_width = hidden.shape[1]
    width = upstream[0].shape[1]
    count = upstream[0].shape[0]
    part = lane // 2

    def kernel(here_ref, hidden_ref, other_ref, own_ref, *outs):
        refs, turned_ref = outs[:4], outs[4]
        y, x = here_ref[1], here_ref[2]
        turned_ref[...] = hidden_ref[...].T
        for p in range(4):
            left = turned_ref[lane * p : lane * (p + 1), :]
            block = low(nn(left[:, :count], other_ref[...]) + nn(left[:, count:], own_ref[...]))
            for half, at, here_at, slot in ((0, p // 2, y, p % 2), (1, p % 2, x, p // 2)):
                value = block[half * part : (half + 1) * part]

                @pl.when(here_at == at)
                def _():
                    refs[2 * half + 1][slot] = value

                @pl.when(here_at != at)
                def _():
                    refs[2 * half][slot] = value

    shape = shape_of((2, part, width))
    return pl.pallas_call(
        kernel,
        in_specs=[SMEM] + [VMEM] * 3,
        out_specs=[VMEM] * 4,
        out_shape=[shape] * 4,
        scratch_shapes=[pltpu.VMEM((hidden_width, 2 * count), jnp.bfloat16)],
        compiler_params=SPACE,
        cost_estimate=LITTLE,
    )(here, hidden, *upstream)


def down_step(here, keeps, cames):
    def kernel(here_ref, first_ref, first_came, second_ref, second_came, *outs):
        for at, ref, came, send, keep in (
            (here_ref[2], first_ref, first_came, *outs[:2]),
            (here_ref[1], second_ref, second_came, *outs[2:]),
        ):
            send[...] = low(wide(ref[1 - at]) + wide(came[1 - at]))
            keep[...] = low(wide(ref[at]) + wide(came[at]))

    shape = shape_of(keeps[0].shape[1:])
    return run(kernel, [shape] * 4, here, keeps[0], cames[0], keeps[1], cames[1])


def depth_blocks(here, own, came):
    nz = lax.axis_size("z")
    shape = (own.shape[0] // nz, own.shape[1])
    own, came = (v.reshape((nz,) + shape) for v in (own, came))

    def kernel(here_ref, own_ref, came_ref, *outs):
        for k, out in enumerate(outs):
            at = (nz - k) % nz
            out[...] = (wide(own_ref[at]) + wide(came_ref[at])).astype(out.dtype)

    shapes = [shape_of(shape, jnp.float32)] + [shape_of(shape)] * (nz - 1)
    return run(kernel, shapes, here, own, came)


def first_backward(here, own, pieces, hidden, upstream, lines):
    count, width = hidden.shape
    half = width // 2
    number = len(pieces)

    def kernel(here_ref, own_ref, hidden_ref, up_ref, line_ref, *refs):
        out_ref, mine_ref, other_ref, term_ref = refs[number:]
        grad = own_ref[...]
        for ref in refs[:number]:
            grad = grad + wide(ref[...])
        hidden = hidden_ref[...]
        scale = lax.rsqrt(jnp.mean(hidden * hidden, axis=-1, keepdims=True) + epsilon)
        normalized = hidden * scale
        term_ref[...] = jnp.sum(grad * normalized, axis=0, keepdims=True)
        scaled = grad * line_ref[2:3]
        mean = jnp.mean(scaled * normalized, axis=-1, keepdims=True)
        result = wide(up_ref[...]) + scale * (scaled - normalized * mean)
        out_ref[...] = result
        proj = low(result)
        first = here_ref[3] == 0
        mine_ref[...] = jnp.where(first, proj[:, :half], proj[:, half:])
        other_ref[...] = jnp.where(first, proj[:, half:], proj[:, :half])

    shapes = (
        shape_of((count, width), jnp.float32),
        shape_of((count, half)),
        shape_of((count, half)),
        shape_of((1, width), jnp.float32),
    )
    return run(kernel, shapes, here, own, hidden, upstream, lines, *pieces)


def attended_backward(here, mine, came, weight):
    count, half = mine.shape

    def kernel(here_ref, mine_ref, came_ref, weight_ref, keep_ref, send_ref, proj_ref):
        proj = jnp.concatenate([mine_ref[...], came_ref[...]], axis=0)
        proj_ref[...] = proj
        part = nt(proj, weight_ref[...])
        first = here_ref[3] == 0
        keep_ref[...] = jnp.where(first, part[:, :half], part[:, half:])
        send = jnp.where(first, part[:, half:], part[:, :half])
        send_ref[:count] = send[count:]
        send_ref[count:] = send[:count]

    shape = shape_of((2 * count, half), jnp.float32)
    return run(kernel, (shape, shape, shape_of((2 * count, half))), here, mine, came, weight)


def inner_backward(here, query_grad, pair_sum, cosine, sine, weight, owned, owned_key):
    total, half = query_grad.shape
    width = 2 * half
    inner = half + 2 * HD

    def kernel(here_ref, q_ref, pair_ref, cos_ref, sin_ref, weight_ref, out_ref, own_ref, other_ref, line_ref):
        core = here_ref[3]
        pair = pair_ref[...]
        key = low(turn_back(pair[:, :HD], cos_ref[...], sin_ref[...]))
        value = low(pair[:, HD:])
        grad = jnp.concatenate([q_ref[...], key, value], axis=1)
        out_ref[...] = grad
        part = nt(grad, weight_ref[:, :inner])
        own_ref[...] = part[: total // 2]
        other_ref[...] = part[total // 2 :]
        terms = jnp.sum(wide(grad), axis=0, keepdims=True)
        query = terms[:, :half]
        nothing = jnp.zeros_like(query)
        first = core == 0
        line_ref[0:1] = jnp.concatenate(
            [jnp.where(first, query, nothing), jnp.where(first, nothing, query)], axis=1
        )
        line_ref[1:2] = nt(
            low(terms[:, half : half + HD]), key_places(core, width, owned, owned_key, 0)
        ) + nt(
            low(terms[:, half + HD :]), key_places(core, width, owned, owned_key, owned_key)
        )

    shapes = (
        shape_of((total, inner)),
        shape_of((total // 2, width), jnp.float32),
        shape_of((total // 2, width), jnp.float32),
        shape_of((2, width), jnp.float32),
    )
    return run(kernel, shapes, here, query_grad, pair_sum, cosine, sine, weight)


def input_backward(here, tokens, own, came, hidden_grad, lines, post_term, bias_terms):
    count, width = tokens.shape

    def kernel(here_ref, t_ref, own_ref, came_ref, h_ref, line_ref, post_ref, bias_ref, out_ref, term_ref):
        values = wide(t_ref[...])
        scale = lax.rsqrt(jnp.mean(values * values, axis=-1, keepdims=True) + epsilon)
        normalized = values * scale
        grad = own_ref[...] + came_ref[...]
        scaled = grad * line_ref[1:2]
        mean = jnp.mean(scaled * normalized, axis=-1, keepdims=True)
        out_ref[...] = low(h_ref[...] + scale * (scaled - normalized * mean))
        term_ref[...] = jnp.concatenate(
            [
                bias_ref[0:1],
                jnp.sum(grad * normalized, axis=0, keepdims=True),
                post_ref[...],
                bias_ref[1:2],
                jnp.zeros((4, width), jnp.float32),
            ],
            axis=0,
        )

    shapes = (shape_of((count, width)), shape_of((8, width), jnp.float32))
    return run(
        kernel, shapes, here, tokens, own, came, hidden_grad, lines, post_term, bias_terms
    )


def inner_blocks(here, keeps, cames):
    nz, cores, rows, columns = keeps[0].shape
    columns = sum(v.shape[3] for v in keeps)
    number = len(keeps)

    def kernel(here_ref, *refs):
        pairs = list(zip(refs[:number], refs[number : 2 * number]))
        for k, out in enumerate(refs[2 * number :]):
            at = around(here_ref[0], k, nz)
            for c in range(cores):
                sums = [wide(a[at, c]) + wide(b[at, c]) for a, b in pairs]
                out[c] = jnp.concatenate(sums, axis=1).astype(out.dtype)

    shape = (cores, rows, columns)
    shapes = [shape_of(shape, jnp.float32)] + [shape_of(shape)] * (nz - 1)
    return run(kernel, shapes, here, *keeps, *cames)


def inner_sums(here, own, pieces):
    cores, rows, columns = own.shape
    number = len(pieces)

    def kernel(here_ref, own_ref, *refs):
        mine_ref, send_ref = refs[number:]
        core = here_ref[3]
        for at, out in ((core, mine_ref), (1 - core, send_ref)):
            total = own_ref[at]
            for ref in refs[:number]:
                total = total + wide(ref[at])
            out[...] = total.astype(out.dtype)

    shapes = (shape_of((rows, columns), jnp.float32), shape_of((rows, columns)))
    return run(kernel, shapes, here, own, *pieces)


def inner_results(here, mine, came, width, key_width):
    rows = mine.shape[0]
    half = width // 2
    ends = (half, 2 * half, 2 * half + HD, 2 * half + 2 * HD)

    def kernel(here_ref, mine_ref, came_ref, output_ref, query_ref, key_ref, value_ref, line_ref):
        first = here_ref[3] == 0
        mine, came = mine_ref[...], wide(came_ref[...])
        line_ref[...] = mine[:, ends[-1] :] + came[:, ends[-1] :]
        output_ref[...] = joined(first, mine[:, :half], came[:, :half])
        for ref, a, b in zip((query_ref, key_ref, value_ref), ends, ends[1:]):
            ref[...] = joined(first, mine[:, a:b], came[:, a:b])

    shapes = [
        shape_of((rows, n), jnp.float32) for n in (width, width, key_width, key_width, 128)
    ]
    return run(kernel, shapes, here, mine, came)


def column_pack(columns, rows):
    padded = [jnp.pad(v, (0, rows - v.shape[0])) for v in columns]
    packed = jnp.stack(padded, axis=1)
    return jnp.pad(packed, ((0, 0), (0, 128 - len(columns))))


def shards(
    tokens,
    doc_lengths,
    query_weight,
    key_weight,
    value_weight,
    query_bias,
    key_bias,
    value_bias,
    output_weight,
    attention_norm_gain,
    feedforward_norm_gain,
    gate_weight,
    up_weight,
    down_weight,
    cotangent,
):
    local_rows, shard_tokens, width = tokens.shape
    sizes = nz, ny, nx, nc = tuple(lax.axis_size(a) for a in EVERY)
    here = jnp.stack([lax.axis_index(a) for a in EVERY]).astype(jnp.int32)
    devices = nz * ny * nx * nc
    flat_count = local_rows * shard_tokens
    chip_count = 2 * flat_count
    owned, query_width = query_weight.shape
    key_width = key_weight.shape[1]
    owned_key = key_bias.shape[0]
    half = query_width // 2
    unit = gate_weight.shape[1] // devices
    lane = -(-ny * nx * unit // 128) * 128 // (ny * nx)
    hidden_width = ny * nx * lane
    in_square = square()
    own_tokens = tokens.reshape(flat_count, width)
    upstream = cotangent.reshape(flat_count, width)
    chip_shape = (2, local_rows, shard_tokens)

    vectors = column_pack(
        (
            query_bias,
            attention_norm_gain,
            feedforward_norm_gain,
            jnp.concatenate([key_bias, value_bias]),
        ),
        owned,
    )
    packed = jnp.concatenate([query_weight, key_weight, value_weight, vectors], axis=1)
    pieces = depth_gathered(packed, every_shift()) | {0: packed}
    down_near = plane_near(down_weight) if in_square else ()
    cosine, sine, allowed = position_tables(doc_lengths, shard_tokens)
    pieces, down_near, cosine, sine, allowed = sync(pieces, down_near, cosine, sine, allowed)
    first_shift, *more_shifts = every_shift()

    mine, shares, send, send_shares = split_shares(
        here, in_order(pieces), gate_weight, up_weight, sizes, unit, lane, query_width, key_width
    )
    came, came_shares = swapped(send, "c"), swapped(send_shares, "c")
    late_output = after(output_weight, pieces)
    output_pieces = depth_gathered(late_output, [first_shift]) | {0: late_output}
    cut = down_weight.shape[0] // 32 * 16
    down_far = ()
    if in_square:
        down_far = swapped(down_near[0][:cut], "y"), swapped(down_near[1][cut:], "x")
    mine, came, shares, came_shares, output_pieces, down_far = sync(
        mine, came, shares, came_shares, output_pieces, down_far
    )

    inner_own = jnp.stack([mine, came], axis=1)
    share_parts = dict(enumerate(share_blocks(here, shares, came_shares)))
    if in_square:
        inner_near = plane_near(inner_own)
    else:
        inner_near = ()
    output_pieces |= depth_gathered(after(late_output, mine), more_shifts)
    share_pieces = depth_sent(share_parts, [first_shift]) | {0: share_parts[0]}
    inner_own, inner_near, output_pieces, share_parts, share_pieces = sync(
        inner_own, inner_near, output_pieces, share_parts, share_pieces
    )

    middle = 512
    if in_square:
        inner_far = (
            swapped(inner_near[0][..., :middle], "y"),
            swapped(inner_near[1][..., middle:], "x"),
        )
        inner_weights = (inner_own, *inner_near, *inner_far)
    else:
        inner_weights = (plane_whole(inner_own).reshape(width, -1),)
    output_mine, output_send = split_output(here, in_order(output_pieces))
    output_came = swapped(output_send, "c")
    other_tokens = swapped(after(own_tokens, inner_own), "c")
    share_pieces |= depth_sent(after(share_parts, inner_own), more_shifts[1:])
    inner_weights, output_mine, output_came, other_tokens, share_pieces = sync(
        inner_weights, output_mine, output_came, other_tokens, share_pieces
    )

    output_own = jnp.stack([output_mine, output_came], axis=1)
    share_pieces |= depth_sent(after(share_parts, output_mine), more_shifts[:1])
    output_near = plane_near(output_own) if in_square else ()
    first_normed, queries, own_pair, lines, weight_inner = inner_projections(
        here,
        own_tokens.reshape(chip_shape[1:] + (width,)),
        other_tokens.reshape(chip_shape[1:] + (width,)),
        inner_weights,
        cosine,
        sine,
        owned,
        owned_key,
    )
    weight_inner = weight_inner.reshape(width, -1)
    cosine_chip = cosine.reshape(chip_shape + (HD,))
    sine_chip = sine.reshape(chip_shape + (HD,))
    own_pair, output_own, output_near, share_pieces = sync(
        own_pair, output_own, output_near, share_pieces
    )

    middle = half // 2
    if in_square:
        pairs = jnp.stack([own_pair, swapped(own_pair, "x")])
        output_near = after(output_near, pairs)
        output_far = (
            swapped(output_near[0][..., :middle], "y"),
            swapped(output_near[1][..., middle:], "x"),
        )
        output_weights = (output_own, *output_near, *output_far)
        pairs = jnp.concatenate([pairs, swapped(pairs, "y")], axis=0)
    else:
        pairs = plane_gathered(own_pair)
        output_weights = (plane_whole(output_own).reshape(width, -1),)
    gate_own, up_own = place_shares(here, in_order(share_pieces))
    late_upstream = after(upstream, share_pieces)
    upstream_pieces = depth_gathered(late_upstream, near_shifts()) | {0: late_upstream}
    pairs, upstream_pieces, gate_own, up_own, output_weights = sync(
        pairs, upstream_pieces, gate_own, up_own, output_weights
    )

    gate_near = plane_near(gate_own) if in_square else ()
    upstream_pieces |= depth_gathered(after(late_upstream, pairs), far_shifts())
    attended, turned, log_sums = attend(here, queries, pairs, allowed)
    attended, turned, gate_near, upstream_pieces = sync(
        attended, turned, gate_near, upstream_pieces
    )

    up_near = plane_near(after(up_own, attended)) if in_square else ()
    upstream_mine = jnp.concatenate(in_order(upstream_pieces), axis=0)
    upstream_other = swapped(upstream_mine, "c")
    came = swapped(turned.reshape(chip_count, half), "c")
    part, send, attended_all, weight_output = output_projection(
        here, attended.reshape(chip_count, half), came, output_weights
    )
    weight_output = weight_output.reshape(width, half)
    first_hidden, second_normed = second_norm(here, own_tokens, part, swapped(send, "c"), lines)
    second_normed, up_near, upstream_other = sync(second_normed, up_near, upstream_other)

    second_pieces = depth_gathered(second_normed, every_shift()) | {0: second_normed}
    if in_square:
        gate_far, up_far = swapped(gate_near[0], "y"), swapped(up_near[1], "x")
        weights = (gate_own, *gate_near, gate_far, up_own, *up_near, up_far)
        second_pieces, weights = sync(second_pieces, weights)
        y, x = lax.axis_index("y"), lax.axis_index("x")
        weight_down = jnp.zeros((2, 2, lane, width), jnp.bfloat16)
        for block, index in (
            (down_weight, (y, x, 0, 0)),
            (down_near[0], (y, 1 - x, 0, 0)),
            (down_near[1], (1 - y, x, 0, 0)),
            (down_far[0], (1 - y, 1 - x, 0, 0)),
            (down_far[1], (1 - y, 1 - x, cut, 0)),
        ):
            weight_down = lax.dynamic_update_slice(weight_down, block[None, None], index)
    else:
        weights = tuple(plane_whole(v).reshape(width, -1) for v in (gate_own, up_own))
        weight_down = lax.all_gather(down_weight, PLANE, axis=0)
        weight_down = jnp.pad(weight_down, ((0, 0), (0, lane - unit), (0, 0)))
        second_pieces, weights, weight_down = sync(second_pieces, weights, weight_down)
    weight_down = weight_down.reshape(hidden_width, width)

    second_mine = jnp.concatenate(in_order(second_pieces), axis=0)
    second_group = (swapped(second_mine, "c"), second_mine)
    upstream_group = (upstream_other, upstream_mine)
    normed_send, normed_own, hidden, gate_grad, up_grad = feed_forward(
        here, second_group, upstream_group, weights, weight_down
    )
    normed_came = swapped(normed_send, "c")
    rows = nc * owned
    if in_square:
        send_gate, gate_sum, send_up, up_sum = share_grads(
            here,
            second_group,
            (gate_grad, 0, hidden_width),
            (up_grad, 0, hidden_width),
            nz,
            rows,
        )
    else:
        send_gate, send_up = weight_grads(here, second_group, (gate_grad, up_grad))
        gate_sum = up_sum = ()
    normed_own, *normed_parts = depth_blocks(here, normed_own, normed_came)
    normed_parts = dict(enumerate(normed_parts, 1))
    normed_own, normed_parts, send_gate, gate_sum, send_up, up_sum = sync(
        normed_own, normed_parts, send_gate, gate_sum, send_up, up_sum
    )

    normed_pieces = depth_sent(normed_parts, every_shift())
    if in_square:
        came_gate, came_up = swapped(send_gate, "y"), swapped(send_up, "x")
        down_parts = down_grads(here, after(hidden, normed_own), upstream_group, lane)
    else:
        blocks = (nz, ny * nx, nc, owned, hidden_width)
        gate_sum, up_sum = (
            lax.psum_scatter(v.reshape(blocks), PLANE, scatter_dimension=1, tiled=False)
            for v in (send_gate, send_up)
        )
        (down_parts,) = weight_grads(
            here, (hidden,), (jnp.concatenate(upstream_group, axis=0),)
        )
    output_send, output_own = feed_forward_output(here, after(hidden, normed_own), weight_down)
    normed_pieces, down_parts, output_send, output_own = sync(
        normed_pieces, down_parts, output_send, output_own
    )

    hidden_one_grad, proj_mine, proj_send, post_term = first_backward(
        here, normed_own, in_order(normed_pieces), first_hidden, upstream, lines
    )
    keep, send, proj_grad = attended_backward(
        here, proj_mine, swapped(proj_send, "c"), weight_output
    )
    attended_came = swapped(send, "c")
    output_came = swapped(after(output_send, proj_mine), "c")
    if in_square:
        keep, attended_came, output_own, output_came, came_gate, came_up = sync(
            keep, attended_came, output_own, output_came, came_gate, came_up
        )
        send_gate, gate_sum, send_up, up_sum = plane_step(
            here, (gate_sum, up_sum), (came_gate, came_up)
        )
    else:
        keep, attended_came = sync(keep, attended_came)
    output_own, *output_parts = depth_blocks(here, output_own, output_came)
    output_parts = dict(enumerate(output_parts, 1))

    four = (nz, nc, owned, hidden_width)
    if in_square:
        came_gate, came_up = swapped(send_gate, "x"), swapped(send_up, "y")
    output_pieces = depth_sent(output_parts, near_shifts())
    if in_square:
        send_a, keep_a, send_b, keep_b = share_grads(
            here,
            (attended_all,),
            (proj_grad, 0, half // 2),
            (proj_grad, half // 2, half),
            nz,
            rows,
        )
    query_grad, part_near, part_far = attend_back(
        here,
        queries,
        pairs,
        allowed,
        log_sums,
        keep.reshape(chip_shape + (half,)),
        attended_came.reshape(chip_shape + (half,)),
        cosine_chip,
        sine_chip,
    )
    if in_square:
        part_near, part_far, came_gate, came_up, output_pieces, send_a, send_b = sync(
            part_near, part_far, came_gate, came_up, output_pieces, send_a, send_b
        )
    else:
        came_gate = came_up = jnp.zeros(four, jnp.bfloat16)

    shares, send_shares = share_sums(
        here,
        (gate_sum.reshape(four), up_sum.reshape(four)),
        (came_gate.reshape(four), came_up.reshape(four)),
    )
    came_shares = swapped(send_shares, "c")
    output_pieces |= depth_sent(after(output_parts, part_near), far_shifts())
    if in_square:
        step = low(wide(part_near) + wide(swapped(part_far, "y")))
        send_a, send_b = after((send_a, send_b), step)
        pair_sum = wide(step[0]) + wide(swapped(step[1], "x"))
        came_a, came_b = swapped(send_a, "y"), swapped(send_b, "x")
    else:
        pair_sum = plane_summed(jnp.concatenate([part_near, part_far], axis=0))
    else_came = (came_a, came_b) if in_square else ()
    pair_sum, shares, came_shares, output_pieces, else_came = sync(
        pair_sum, shares, came_shares, output_pieces, else_came
    )
    layer_output = first_hidden + output_own + sum(wide(v) for v in in_order(output_pieces))

    share_parts = dict(enumerate(share_blocks(here, shares, came_shares)))
    share_pieces = depth_sent(share_parts, near_shifts()) | {0: share_parts[0]}
    if in_square:
        came_a, came_b = else_came
        first_send, first_keep, second_send, second_keep = after(down_parts, pair_sum)
        came_first, came_second = swapped(first_send, "y"), swapped(second_send, "x")
    else:
        down_sum = lax.psum_scatter(
            down_parts.reshape(ny * nx, lane, width), PLANE, scatter_dimension=0, tiled=False
        )
    inner_grad, own_part, send, bias_terms = inner_backward(
        here,
        query_grad.reshape(chip_count, half),
        pair_sum.reshape(chip_count, 2 * HD),
        cosine,
        sine,
        weight_inner,
        owned,
        owned_key,
    )
    input_grad, vector_terms = input_backward(
        here, own_tokens, own_part, swapped(send, "c"), hidden_one_grad, lines, post_term, bias_terms
    )
    share_parts = after(share_parts, inner_grad)
    if in_square:
        send_c, keep_c, send_d, keep_d = share_grads(
            here,
            (first_normed,),
            (inner_grad, 0, 512),
            (inner_grad, 512, half + 2 * HD),
            nz,
            rows,
            vector_terms,
        )
        send_c, keep_c, send_d, keep_d, came_first, came_second, share_parts, share_pieces = sync(
            send_c, keep_c, send_d, keep_d, came_first, came_second, share_parts, share_pieces
        )
        share_pieces |= depth_sent(share_parts, far_shifts())
        send_a, keep_a, send_b, keep_b = plane_step(here, (keep_a, keep_b), (came_a, came_b))
        came_a, came_b = swapped(send_a, "x"), swapped(send_b, "y")
        came_c, came_d = swapped(send_c, "y"), swapped(send_d, "x")
        came_a, came_b, came_c, came_d, share_pieces = sync(
            came_a, came_b, came_c, came_d, share_pieces
        )
        send_c, keep_c, send_d, keep_d = plane_step(here, (keep_c, keep_d), (came_c, came_d))
        came_c, came_d = swapped(send_c, "x"), swapped(send_d, "y")
        first_send, first_keep, second_send, second_keep = down_step(
            here, (first_keep, second_keep), (came_first, came_second)
        )
        came_c, came_d, first_send, second_send = sync(came_c, came_d, first_send, second_send)
        keeps, cames = (
            [v.reshape(nz, nc, owned, -1) for v in group]
            for group in ((keep_a, keep_b, keep_c, keep_d), (came_a, came_b, came_c, came_d))
        )
    else:
        share_pieces |= depth_sent(share_parts, far_shifts())
        (output_term,) = weight_grads(here, (attended_all,), (proj_grad,))
        (inner_term,) = weight_grads(here, (first_normed,), (inner_grad,))
        inner_term = jnp.concatenate(
            [inner_term, jnp.pad(low(vector_terms.T), ((0, 0), (0, 120)))], axis=1
        )
        blocks = (nz, ny * nx, nc, owned, -1)
        keeps = [
            lax.psum_scatter(v.reshape(blocks), PLANE, scatter_dimension=1, tiled=False)
            for v in (output_term, inner_term)
        ]
        cames = [jnp.zeros_like(v) for v in keeps]
    gate_sum, up_sum = collect_columns(here, in_order(share_pieces), sizes, unit, lane)

    own, *parts = inner_blocks(here, keeps, cames)
    parts = dict(enumerate(parts, 1))
    pieces = depth_sent(parts, every_shift())
    if in_square:
        came_first, came_second = swapped(first_send, "x"), swapped(second_send, "y")
        down_sum = jnp.concatenate(
            [
                wide(first_keep) + wide(came_first),
                wide(second_keep) + wide(came_second),
            ],
            axis=0,
        )
    pieces, down_sum = sync(pieces, down_sum)
    mine, send = inner_sums(here, own, in_order(pieces))
    output_sum, query_sum, key_sum, value_sum, vector_sums = inner_results(
        here, mine, swapped(send, "c"), width, key_width
    )
    return (
        low(layer_output).reshape(local_rows, shard_tokens, width),
        input_grad.reshape(local_rows, shard_tokens, width),
        query_sum,
        key_sum,
        value_sum,
        vector_sums[:, 0],
        vector_sums[:owned_key, 3],
        vector_sums[owned_key : 2 * owned_key, 3],
        output_sum,
        vector_sums[:, 1],
        vector_sums[:, 2],
        gate_sum,
        up_sum,
        wide(down_sum)[:unit],
    )


def solution(mesh):
    depth, across = mesh.devices.shape
    plane = across // 2
    side = math.isqrt(plane)
    inner = Mesh(mesh.devices.reshape(depth, plane // side, side, 2), EVERY)
    over_rows = P("z", ROW, None)
    whole, flat = P(EVERY, None), P(EVERY)
    in_specs = (
        (over_rows, P("z", None))
        + (whole,) * 3
        + (flat,) * 3
        + (whole, flat, flat)
        + (whole,) * 3
        + (over_rows,)
    )
    out_specs = (
        (over_rows,) * 2 + (whole,) * 3 + (flat,) * 3 + (whole, flat, flat) + (whole,) * 3
    )
    return jax.shard_map(
        shards, mesh=inner, in_specs=in_specs, out_specs=out_specs, check_vma=False
    )
```

time: 835 us -> 493 us (0.59)
  waiting for transfers between devices: 491 us -> 246 us
  Pallas kernels: 0 us -> 114 us
  local copies, waits for them, and re-layouts: 131 us -> 25.7 us
  matrix products: 91.3 us -> 0 us
  starting transfers between devices: 36.3 us -> 88.2 us
  other arithmetic: 56.7 us -> 6.99 us
  between operations: 16.5 us -> 2.04 us
    reduce_scatter x3 -> x0, waiting for transfers between devices: 153 us -> none  [the longest x1 111 us: shards(): lax.psum_scatter(query_term, EVERY, scatter_dimension=0, tiled=True)]
    pallas_call x0 -> x31, Pallas kernels: none -> 114 us  [the longest x10 45.1 us: run_grid(): pl.pallas_call(kernel, grid=(grid,), in_specs=[SMEM] + list(specs), out_s...]
    dot_general x23 -> x0, matrix products: 91.3 us -> none  [the longest x6 28 us: contract_cols(): lax.dot_general(left, right, (((1,), (1,)), ((), ())), preferred_element_...]
    all_gather x3 -> x0, waiting for transfers between devices: 67.2 us -> none  [the longest x1 67.2 us: shards(): packed = lax.all_gather(packed, EVERY, axis=0, tiled=True)]
    ppermute x18 -> x27, waiting for transfers between devices: 178 us -> 137 us  [shifted(): lax.ppermute(values, 'z', [(i, (i + amount) % count) for i in range(count)])]
    ppermute x22 -> x53, starting transfers between devices: 19.6 us -> 48.8 us  [swapped(): return lax.ppermute(values, axis, [(0, 1), (1, 0)])]
    ppermute x18 -> x27, starting transfers between devices: 16 us -> 39.4 us  [shifted(): lax.ppermute(values, 'z', [(i, (i + amount) % count) for i in range(count)])]
    convert_element_type x6 -> x0, local copies, waits for them, and re-layouts: 18.9 us -> none  [the longest x1 5.71 us: scatter_columns(): shares = shares.reshape(2, rows, -1).astype(jnp.float32)]
  transfers between devices with their start and end apart: 47 -> 80, of which waited for: 19 -> 42; matrix products, arithmetic and copies ran while one was open for 24% -> 2% of each run, Pallas kernels for 0% -> 15%
where the time goes in v3:
time: 493 us; the launch traced here: 483 us
  waiting for transfers between devices  246 us (50%)
  Pallas kernels  114 us (23%)
  starting transfers between devices  88.2 us (18%)
  local copies, waits for them, and re-layouts  25.7 us (5%)
  other arithmetic  6.99 us (1%)
    ppermute x27, waiting for transfers between devices, shifted(): lax.ppermute(values, 'z', [(i, (i + amount) % count) for i in range(count)])  137 us
    ppermute x53, waiting for transfers between devices, swapped(): return lax.ppermute(values, axis, [(0, 1), (1, 0)])  109 us
    ppermute x53, starting transfers between devices, swapped(): return lax.ppermute(values, axis, [(0, 1), (1, 0)])  48.8 us
    pallas_call x10, Pallas kernels, run_grid(): pl.pallas_call(kernel, grid=(grid,), in_specs=[SMEM] + list(specs), out_s...  45.1 us
    ppermute x27, starting transfers between devices, shifted(): lax.ppermute(values, 'z', [(i, (i + amount) % count) for i in range(count)])  39.4 us
    pallas_call x1, Pallas kernels, feed_forward(): pl.pallas_call(kernel, grid=(2 * steps,), in_specs=[SMEM, spec_a, spec_b,...  32.1 us
    pallas_call x18, Pallas kernels, run(): pl.pallas_call(kernel, in_specs=[SMEM] + [VMEM] * len(arrays), out_specs=...  25.7 us
    unnamed x134, local copies, waits for them, and re-layouts  17.2 us
  transfers between devices with their start and end apart: 80, of which 42 were waited for; matrix products, arithmetic and copies ran while one was open for 2% of the time, Pallas kernels for 15%

profile of v3, /device:TPU:29, one launch (start us, length us, event | category | flops | bytes accessed | tf_op | source)
XLA Modules:
  0.0 482.9 jit_solution(16623064054479441163)
XLA Ops:
  11.3 8.4 %collective-permute-done.1.refs_2_ = bf16[48,2176]{1,0:T(8,128)(2,1)S(1)} collective-permute-done((bf16[48,2176]{1,0:T(8,128)(2,1)S(1)}, bf16[48,2176]{1,0:T(8,128)(2,1)S(1)}, u32[]{:S(2)}, u32[]{:S(2)}) %collective-permute-start.1) | collective-permute-done | bytes 208928 | tf_op jit(solution)/shard_map/ppermute | solution.py:116
  19.7 6.6 %collective-permute-done.3 = bf16[280,1536]{1,0:T(8,128)(2,1)} collective-permute-done((bf16[280,1536]{1,0:T(8,128)(2,1)}, bf16[280,1536]{1,0:T(8,128)(2,1)}, u32[]{:S(2)}, u32[]{:S(2)}) %collective-permute-start.3) | collective-permute-done | bytes 860192 | tf_op jit(solution)/shard_map/ppermute | solution.py:111
  39.7 5.4 %collective-permute-done.8 = bf16[128,1536]{1,0:T(8,128)(2,1)S(1)} collective-permute-done((bf16[128,1536]{1,0:T(8,128)(2,1)S(1)}, bf16[128,1536]{1,0:T(8,128)(2,1)S(1)}, u32[]{:S(2)}, u32[]{:S(2)}) %collective-permute-start.8) | collective-permute-done | bytes 393248 | tf_op jit(solution)/shard_map/ppermute | solution.py:111
  51.2 11.2 %collective-permute-done.13.refs_3_ = bf16[48,1536]{1,0:T(8,128)(2,1)S(1)} collective-permute-done((bf16[48,1536]{1,0:T(8,128)(2,1)S(1)}, bf16[48,1536]{1,0:T(8,128)(2,1)S(1)}, u32[]{:S(2)}, u32[]{:S(2)}) %collective-permute-start.13) | collective-permute-done | bytes 147488 | tf_op jit(solution)/shard_map/ppermute | solution.py:116
  89.1 16.4 %collective-permute-done.22.refs_2_ = bf16[2,2,48,1152]{3,2,1,0:T(8,128)(2,1)S(1)} collective-permute-done((bf16[2,2,48,1152]{3,2,1,0:T(8,128)(2,1)S(1)}, bf16[2,2,48,1152]{3,2,1,0:T(8,128)(2,1)S(1)}, u32[]{:S(2)}, u32[]{:S(2)}) %collective-permute-start.22) | collective-permute-done | bytes 442400 | tf_op jit(solution)/shard_map/ppermute | solution.py:116
  116.7 7.1 %collective-permute-done.25 = bf16[128,1536]{1,0:T(8,128)(2,1)S(1)} collective-permute-done((bf16[128,1536]{1,0:T(8,128)(2,1)S(1)}, bf16[128,1536]{1,0:T(8,128)(2,1)S(1)}, u32[]{:S(2)}, u32[]{:S(2)}) %collective-permute-start.25) | collective-permute-done | bytes 393248 | tf_op jit(solution)/shard_map/ppermute | solution.py:116
  132.9 9.6 %collective-permute-done.31 = bf16[128,1536]{1,0:T(8,128)(2,1)S(1)} collective-permute-done((bf16[128,1536]{1,0:T(8,128)(2,1)S(1)}, bf16[128,1536]{1,0:T(8,128)(2,1)S(1)}, u32[]{:S(2)}, u32[]{:S(2)}) %collective-permute-start.31) | collective-permute-done | bytes 393248 | tf_op jit(solution)/shard_map/ppermute | solution.py:116
  158.1 10.5 %collective-permute-done.35.refs_6_ = bf16[4,2,48,1152]{3,2,1,0:T(8,128)(2,1)} collective-permute-done((bf16[4,2,48,1152]{3,2,1,0:T(8,128)(2,1)S(1)}, bf16[4,2,48,1152]{3,2,1,0:T(8,128)(2,1)}, u32[]{:S(2)}, u32[]{:S(2)}) %collective-permute-start.35) | collective-permute-done | bytes 884768 | tf_op jit(solution)/shard_map/ppermute | solution.py:111
  176.8 10.7 %collective-permute-done.40.refs_3_ = bf16[4,2,48,1152]{3,2,1,0:T(8,128)(2,1)} collective-permute-done((bf16[4,2,48,1152]{3,2,1,0:T(8,128)(2,1)}, bf16[4,2,48,1152]{3,2,1,0:T(8,128)(2,1)}, u32[]{:S(2)}, u32[]{:S(2)}) %collective-permute-start.40) | collective-permute-done | bytes 884768 | tf_op jit(solution)/shard_map/ppermute | solution.py:111
  187.5 13.2 %collective-permute-done.38 = bf16[128,1536]{1,0:T(8,128)(2,1)S(1)} collective-permute-done((bf16[128,1536]{1,0:T(8,128)(2,1)}, bf16[128,1536]{1,0:T(8,128)(2,1)S(1)}, u32[]{:S(2)}, u32[]{:S(2)}) %collective-permute-start.38) | collective-permute-done | bytes 393248 | tf_op jit(solution)/shard_map/ppermute | solution.py:116
  207.3 32.1 %shard_map.262 = (bf16[512,1536]{1,0:T(8,128)(2,1)}, bf16[512,1536]{1,0:T(8,128)(2,1)}, bf16[1024,1152]{1,0:T(8,128)(2,1)}, bf16[1024,1152]{1,0:T(8,128)(2,1)}, bf16[1024,1152]{1,0:T(8,128)(2,1)}) custom-call(s32[4]{0:T(128)} %copy-done.39, bf16[512,1536]{1,0:T(8,128)(2,1)} %copy-done.5, bf16[512,1536]{1,0:T(8,128)(2,1)} %copy-done.1, ...), custom_call_target="tpu_custom_call" | custom-call | flops 1 | bytes 1 | tf_op jit(solution)/shard_map/pallas_call | solution.py:616
  241.3 12.7 %shard_map.264 = (bf16[4,2,96,1152]{3,2,1,0:T(8,128)(2,1)}, bf16[4,2,96,1152]{3,2,1,0:T(8,128)(2,1)}, bf16[4,2,96,1152]{3,2,1,0:T(8,128)(2,1)}, bf16[4,2,96,1152]{3,2,1,0:T(8,128)(2,1)}) custom-call(s32[4]{0:T(128)S(1)} %copy-done.40, bf16[512,1536]{1,0:T(8,128)(2,1)S(1)} %copy-done.6, bf16[512,1536]{1,0:T(8,128)(2,1)S(1)} %copy-done.2, ...), custom_call_target="tpu_custom_call" | custom-call | flops 1 | bytes 1 | tf_op jit(solution)/shard_map/pallas_call | solution.py:190
  255.0 10.5 %collective-permute-start.44 = (bf16[128,1536]{1,0:T(8,128)(2,1)S(1)}, bf16[128,1536]{1,0:T(8,128)(2,1)S(1)}, u32[]{:S(2)}, u32[]{:S(2)}) collective-permute-start(bf16[128,1536]{1,0:T(8,128)(2,1)S(1)} %get-tuple-element.419), channel_id=1, source_target_pairs={{0,8},{8,16},{16,24},{24,0},{1,9},{9,17},{17,25},{25,1},{2,10},{10... | collective-permute-start | bytes 1179656 | tf_op jit(solution)/shard_map/ppermute | solution.py:116
  267.1 7.3 %shard_map.266 = (bf16[512,1536]{1,0:T(8,128)(2,1)S(1)}, bf16[512,1536]{1,0:T(8,128)(2,1)S(1)}) custom-call(s32[4]{0:T(128)S(1)} %copy-done.40, bf16[1024,1152]{1,0:T(8,128)(2,1)S(1)} %copy-done, bf16[1152,1536]{1,0:T(8,128)(2,1)} %bitcast.104), custom_call_target="tpu_custom_call" | custom-call | flops 1 | bytes 1 | tf_op jit(solution)/shard_map/pallas_call | solution.py:190
  275.6 8.4 %shard_map.265 = (bf16[2,144,1536]{2,1,0:T(8,128)(2,1)}, bf16[2,144,1536]{2,1,0:T(8,128)(2,1)S(1)}, bf16[2,144,1536]{2,1,0:T(8,128)(2,1)}, bf16[2,144,1536]{2,1,0:T(8,128)(2,1)S(1)}) custom-call(s32[4]{0:T(128)S(1)} %copy-done.40, bf16[1024,1152]{1,0:T(8,128)(2,1)} %get-tuple-element.423.hidden_ref, bf16[512,1536]{1,0:T(8,128)(2,1)S(1)} %copy-done.4, ...), custom_call_target="tpu_custom_call" | custom-call | flops 1 | bytes 1 | tf_op jit(solution)/shard_map/pallas_call | solution.py:839
  284.0 15.4 %collective-permute-done.45.refs_1_ = bf16[128,1536]{1,0:T(8,128)(2,1)S(1)} collective-permute-done((bf16[128,1536]{1,0:T(8,128)(2,1)S(1)}, bf16[128,1536]{1,0:T(8,128)(2,1)S(1)}, u32[]{:S(2)}, u32[]{:S(2)}) %collective-permute-start.45) | collective-permute-done | bytes 393248 | tf_op jit(solution)/shard_map/ppermute | solution.py:116
  323.3 6.1 %shard_map.270 = (bf16[2,2,64,768]{3,2,1,0:T(8,128)(2,1)S(1)}, bf16[2,2,2,64,256]{4,3,2,1,0:T(8,128)(2,1)S(1)}, bf16[2,2,2,64,256]{4,3,2,1,0:T(8,128)(2,1)S(1)}) custom-call(s32[4]{0:T(128)S(1)} %copy-done.40, bf16[2,6,2,64,128]{4,3,2,1,0:T(8,128)(2,1)S(1)} %copy-done.13, bf16[4,2,2,64,256]{4,3,2,1,0:T(8,128)(2,1)S(1)} %pad_maximum_fusion.3.pair_ref, ...), custom_call_target="tpu_custom_call" | custom-call | flops 1 | bytes 1 | tf_op jit(solution)/shard_map/pallas_call | solution.py:190
  329.5 8.7 %collective-permute-done.55 = bf16[128,1536]{1,0:T(8,128)(2,1)S(1)} collective-permute-done((bf16[128,1536]{1,0:T(8,128)(2,1)S(1)}, bf16[128,1536]{1,0:T(8,128)(2,1)S(1)}, u32[]{:S(2)}, u32[]{:S(2)}) %collective-permute-start.55) | collective-permute-done | bytes 393248 | tf_op jit(solution)/shard_map/ppermute | solution.py:116
  346.8 13.3 %collective-permute-done.57 = bf16[2,2,64,256]{3,2,1,0:T(8,128)(2,1)S(1)} collective-permute-done((bf16[2,2,64,256]{3,2,1,0:T(8,128)(2,1)S(1)}, bf16[2,2,64,256]{3,2,1,0:T(8,128)(2,1)S(1)}, u32[]{:S(2)}, u32[]{:S(2)}) %collective-permute-start.57) | collective-permute-done | bytes 131104 | tf_op jit(solution)/shard_map/ppermute | solution.py:111
  378.4 5.6 %collective-permute-done.65.refs_1_ = bf16[2,2,48,1152]{3,2,1,0:T(8,128)(2,1)S(1)} collective-permute-done((bf16[2,2,48,1152]{3,2,1,0:T(8,128)(2,1)}, bf16[2,2,48,1152]{3,2,1,0:T(8,128)(2,1)S(1)}, u32[]{:S(2)}, u32[]{:S(2)}) %collective-permute-start.65) | collective-permute-done | bytes 442400 | tf_op jit(solution)/shard_map/ppermute | solution.py:116
  384.8 9.5 %collective-permute-done.66.refs_3_ = bf16[2,2,48,1152]{3,2,1,0:T(8,128)(2,1)S(1)} collective-permute-done((bf16[2,2,48,1152]{3,2,1,0:T(8,128)(2,1)S(1)}, bf16[2,2,48,1152]{3,2,1,0:T(8,128)(2,1)S(1)}, u32[]{:S(2)}, u32[]{:S(2)}) %collective-permute-start.66) | collective-permute-done | bytes 442400 | tf_op jit(solution)/shard_map/ppermute | solution.py:116
  399.5 24.4 %collective-permute-done.67 = bf16[4,96,384]{2,1,0:T(8,128)(2,1)S(1)} collective-permute-done((bf16[4,96,384]{2,1,0:T(8,128)(2,1)S(1)}, bf16[4,96,384]{2,1,0:T(8,128)(2,1)S(1)}, u32[]{:S(2)}, u32[]{:S(2)}) %collective-permute-start.67) | collective-permute-done | bytes 294944 | tf_op jit(solution)/shard_map/ppermute | solution.py:111
  427.7 6.9 %collective-permute-done.72 = bf16[4,96,512]{2,1,0:T(8,128)(2,1)S(1)} collective-permute-done((bf16[4,96,512]{2,1,0:T(8,128)(2,1)S(1)}, bf16[4,96,512]{2,1,0:T(8,128)(2,1)S(1)}, u32[]{:S(2)}, u32[]{:S(2)}) %collective-permute-start.72) | collective-permute-done | bytes 393248 | tf_op jit(solution)/shard_map/ppermute | solution.py:111
  448.7 20.9 %collective-permute-done.75.refs_1_ = bf16[2,48,1920]{2,1,0:T(8,128)(2,1)S(1)} collective-permute-done((bf16[2,48,1920]{2,1,0:T(8,128)(2,1)S(1)}, bf16[2,48,1920]{2,1,0:T(8,128)(2,1)S(1)}, u32[]{:S(2)}, u32[]{:S(2)}) %collective-permute-start.75) | collective-permute-done | bytes 368672 | tf_op jit(solution)/shard_map/ppermute | solution.py:116
  (354 shorter events, 199.7 us)
Async XLA Ops:
  81.0 24.5 %collective-permute-start.21 = (bf16[4,2,48,768]{3,2,1,0:T(8,128)(2,1)S(1)}, bf16[4,2,48,768]{3,2,1,0:T(8,128)(2,1)S(1)}, u32[]{:S(2)}, u32[]{:S(2)}) collective-permute-start(bf16[4,2,48,768]{3,2,1,0:T(8,128)(2,1)S(1)} %pad_maximum_fusion.2.refs_0_), channel_id=1, source_target_pairs={{0,4},{4,0},{1,5},{5,1},{2,6},{6,2},{3,7},{7,3},{8,12},{12,8},{9,1... | collective-permute-start | bytes 1769480 | tf_op jit(solution)/shard_map/ppermute | solution.py:111
  82.3 23.2 %collective-permute-start.20 = (bf16[4,2,48,768]{3,2,1,0:T(8,128)(2,1)S(1)}, bf16[4,2,48,768]{3,2,1,0:T(8,128)(2,1)S(1)}, u32[]{:S(2)}, u32[]{:S(2)}) collective-permute-start(bf16[4,2,48,768]{3,2,1,0:T(8,128)(2,1)S(1)} %pad_maximum_fusion.2.refs_0_), channel_id=1, source_target_pairs={{0,2},{2,0},{1,3},{3,1},{4,6},{6,4},{5,7},{7,5},{8,10},{10,8},{9,1... | collective-permute-start | bytes 1769480 | tf_op jit(solution)/shard_map/ppermute | solution.py:111
  83.5 22.1 %collective-permute-start.22 = (bf16[2,2,48,1152]{3,2,1,0:T(8,128)(2,1)S(1)}, bf16[2,2,48,1152]{3,2,1,0:T(8,128)(2,1)S(1)}, u32[]{:S(2)}, u32[]{:S(2)}) collective-permute-start(bf16[2,2,48,1152]{3,2,1,0:T(8,128)(2,1)S(1)} %get-tuple-element.344), channel_id=1, source_target_pairs={{0,16},{8,24},{16,0},{24,8},{1,17},{9,25},{17,1},{25,9},{2,18},{10... | collective-permute-start | bytes 1327112 | tf_op jit(solution)/shard_map/ppermute | solution.py:116
  144.1 25.4 %collective-permute-start.36 = (bf16[512,1536]{1,0:T(8,128)(2,1)S(1)}, bf16[512,1536]{1,0:T(8,128)(2,1)S(1)}, u32[]{:S(2)}, u32[]{:S(2)}) collective-permute-start(bf16[512,1536]{1,0:T(8,128)(2,1)S(1)} %constant_dynamic-update-slice_fusion.ub_ref.own_ref), channel_id=1, source_target_pairs={{0,1},{1,0},{2,3},{3,2},{4,5},{5,4},{6,7},{7,6},{8,9},{9,8},{10,11... | collective-permute-start | bytes 4718600 | tf_op jit(solution)/shard_map/ppermute | solution.py:111
  154.2 33.3 %collective-permute-start.40 = (bf16[4,2,48,1152]{3,2,1,0:T(8,128)(2,1)}, bf16[4,2,48,1152]{3,2,1,0:T(8,128)(2,1)}, u32[]{:S(2)}, u32[]{:S(2)}) collective-permute-start(bf16[4,2,48,1152]{3,2,1,0:T(8,128)(2,1)} %collective-permute-done.29.refs_1_), channel_id=1, source_target_pairs={{0,4},{4,0},{1,5},{5,1},{2,6},{6,2},{3,7},{7,3},{8,12},{12,8},{9,1... | collective-permute-start | bytes 2654216 | tf_op jit(solution)/shard_map/ppermute | solution.py:111
  170.4 30.3 %collective-permute-start.41 = (bf16[4,2,48,1152]{3,2,1,0:T(8,128)(2,1)}, bf16[4,2,48,1152]{3,2,1,0:T(8,128)(2,1)}, u32[]{:S(2)}, u32[]{:S(2)}) collective-permute-start(bf16[4,2,48,1152]{3,2,1,0:T(8,128)(2,1)} %collective-permute-done.35.refs_6_), channel_id=1, source_target_pairs={{0,2},{2,0},{1,3},{3,1},{4,6},{6,4},{5,7},{7,5},{8,10},{10,8},{9,1... | collective-permute-start | bytes 2654216 | tf_op jit(solution)/shard_map/ppermute | solution.py:111
  174.2 26.6 %collective-permute-start.38 = (bf16[128,1536]{1,0:T(8,128)(2,1)}, bf16[128,1536]{1,0:T(8,128)(2,1)S(1)}, u32[]{:S(2)}, u32[]{:S(2)}) collective-permute-start(bf16[128,1536]{1,0:T(8,128)(2,1)} %copy-done.45), channel_id=1, source_target_pairs={{0,16},{8,24},{16,0},{24,8},{1,17},{9,25},{17,1},{25,9},{2,18},{10... | collective-permute-start | bytes 1179656 | tf_op jit(solution)/shard_map/ppermute | solution.py:116
  174.2 26.6 %collective-permute-start.37 = (bf16[128,1536]{1,0:T(8,128)(2,1)}, bf16[128,1536]{1,0:T(8,128)(2,1)S(1)}, u32[]{:S(2)}, u32[]{:S(2)}) collective-permute-start(bf16[128,1536]{1,0:T(8,128)(2,1)} %copy-done.45), channel_id=1, source_target_pairs={{0,8},{8,16},{16,24},{24,0},{1,9},{9,17},{17,25},{25,1},{2,10},{10... | collective-permute-start | bytes 1179656 | tf_op jit(solution)/shard_map/ppermute | solution.py:116
  255.0 29.0 %collective-permute-start.44 = (bf16[128,1536]{1,0:T(8,128)(2,1)S(1)}, bf16[128,1536]{1,0:T(8,128)(2,1)S(1)}, u32[]{:S(2)}, u32[]{:S(2)}) collective-permute-start(bf16[128,1536]{1,0:T(8,128)(2,1)S(1)} %get-tuple-element.419), channel_id=1, source_target_pairs={{0,8},{8,16},{16,24},{24,0},{1,9},{9,17},{17,25},{25,1},{2,10},{10... | collective-permute-start | bytes 1179656 | tf_op jit(solution)/shard_map/ppermute | solution.py:116
  265.6 33.8 %collective-permute-start.45 = (bf16[128,1536]{1,0:T(8,128)(2,1)S(1)}, bf16[128,1536]{1,0:T(8,128)(2,1)S(1)}, u32[]{:S(2)}, u32[]{:S(2)}) collective-permute-start(bf16[128,1536]{1,0:T(8,128)(2,1)S(1)} %get-tuple-element.420), channel_id=1, source_target_pairs={{0,16},{8,24},{16,0},{24,8},{1,17},{9,25},{17,1},{25,9},{2,18},{10... | collective-permute-start | bytes 1179656 | tf_op jit(solution)/shard_map/ppermute | solution.py:116
  265.6 33.8 %collective-permute-start.46 = (bf16[128,1536]{1,0:T(8,128)(2,1)S(1)}, bf16[128,1536]{1,0:T(8,128)(2,1)S(1)}, u32[]{:S(2)}, u32[]{:S(2)}) collective-permute-start(bf16[128,1536]{1,0:T(8,128)(2,1)S(1)} %get-tuple-element.421), channel_id=1, source_target_pairs={{0,24},{8,0},{16,8},{24,16},{1,25},{9,1},{17,9},{25,17},{2,26},{10... | collective-permute-start | bytes 1179656 | tf_op jit(solution)/shard_map/ppermute | solution.py:116
  265.9 44.4 %collective-permute-start.50 = (bf16[4,2,96,1152]{3,2,1,0:T(8,128)(2,1)}, bf16[4,2,96,1152]{3,2,1,0:T(8,128)(2,1)}, u32[]{:S(2)}, u32[]{:S(2)}) collective-permute-start(bf16[4,2,96,1152]{3,2,1,0:T(8,128)(2,1)} %get-tuple-element.441), channel_id=1, source_target_pairs={{0,4},{4,0},{1,5},{5,1},{2,6},{6,2},{3,7},{7,3},{8,12},{12,8},{9,1... | collective-permute-start | bytes 5308424 | tf_op jit(solution)/shard_map/ppermute | solution.py:111
  266.8 43.5 %collective-permute-start.51 = (bf16[4,2,96,1152]{3,2,1,0:T(8,128)(2,1)}, bf16[4,2,96,1152]{3,2,1,0:T(8,128)(2,1)}, u32[]{:S(2)}, u32[]{:S(2)}) collective-permute-start(bf16[4,2,96,1152]{3,2,1,0:T(8,128)(2,1)} %get-tuple-element.442), channel_id=1, source_target_pairs={{0,2},{2,0},{1,3},{3,1},{4,6},{6,4},{5,7},{7,5},{8,10},{10,8},{9,1... | collective-permute-start | bytes 5308424 | tf_op jit(solution)/shard_map/ppermute | solution.py:111
  314.9 23.3 %collective-permute-start.52 = (bf16[4,96,1152]{2,1,0:T(8,128)(2,1)}, bf16[4,96,1152]{2,1,0:T(8,128)(2,1)S(1)}, u32[]{:S(2)}, u32[]{:S(2)}) collective-permute-start(bf16[4,96,1152]{2,1,0:T(8,128)(2,1)} %get-tuple-element.455), channel_id=1, source_target_pairs={{0,2},{2,0},{1,3},{3,1},{4,6},{6,4},{5,7},{7,5},{8,10},{10,8},{9,1... | collective-permute-start | bytes 2654216 | tf_op jit(solution)/shard_map/ppermute | solution.py:111
  316.1 22.1 %collective-permute-start.53 = (bf16[4,96,1152]{2,1,0:T(8,128)(2,1)}, bf16[4,96,1152]{2,1,0:T(8,128)(2,1)}, u32[]{:S(2)}, u32[]{:S(2)}) collective-permute-start(bf16[4,96,1152]{2,1,0:T(8,128)(2,1)} %get-tuple-element.456), channel_id=1, source_target_pairs={{0,4},{4,0},{1,5},{5,1},{2,6},{6,2},{3,7},{7,3},{8,12},{12,8},{9,1... | collective-permute-start | bytes 2654216 | tf_op jit(solution)/shard_map/ppermute | solution.py:111
  363.1 32.0 %collective-permute-start.63 = (bf16[2,144,1536]{2,1,0:T(8,128)(2,1)}, bf16[2,144,1536]{2,1,0:T(8,128)(2,1)S(1)}, u32[]{:S(2)}, u32[]{:S(2)}) collective-permute-start(bf16[2,144,1536]{2,1,0:T(8,128)(2,1)} %get-tuple-element.508), channel_id=1, source_target_pairs={{0,4},{4,0},{1,5},{5,1},{2,6},{6,2},{3,7},{7,3},{8,12},{12,8},{9,1... | collective-permute-start | bytes 2654216 | tf_op jit(solution)/shard_map/ppermute | solution.py:111
  363.4 31.7 %collective-permute-start.64 = (bf16[2,144,1536]{2,1,0:T(8,128)(2,1)}, bf16[2,144,1536]{2,1,0:T(8,128)(2,1)S(1)}, u32[]{:S(2)}, u32[]{:S(2)}) collective-permute-start(bf16[2,144,1536]{2,1,0:T(8,128)(2,1)} %get-tuple-element.509), channel_id=1, source_target_pairs={{0,2},{2,0},{1,3},{3,1},{4,6},{6,4},{5,7},{7,5},{8,10},{10,8},{9,1... | collective-permute-start | bytes 2654216 | tf_op jit(solution)/shard_map/ppermute | solution.py:111
  395.1 28.8 %collective-permute-start.70 = (bf16[4,2,96,640]{3,2,1,0:T(8,128)(2,1)S(1)}, bf16[4,2,96,640]{3,2,1,0:T(8,128)(2,1)S(1)}, u32[]{:S(2)}, u32[]{:S(2)}) collective-permute-start(bf16[4,2,96,640]{3,2,1,0:T(8,128)(2,1)S(1)} %get-tuple-element.521), channel_id=1, source_target_pairs={{0,2},{2,0},{1,3},{3,1},{4,6},{6,4},{5,7},{7,5},{8,10},{10,8},{9,1... | collective-permute-start | bytes 2949128 | tf_op jit(solution)/shard_map/ppermute | solution.py:111
  395.6 28.3 %collective-permute-start.69 = (bf16[4,2,96,512]{3,2,1,0:T(8,128)(2,1)S(1)}, bf16[4,2,96,512]{3,2,1,0:T(8,128)(2,1)S(1)}, u32[]{:S(2)}, u32[]{:S(2)}) collective-permute-start(bf16[4,2,96,512]{3,2,1,0:T(8,128)(2,1)S(1)} %get-tuple-element.520), channel_id=1, source_target_pairs={{0,4},{4,0},{1,5},{5,1},{2,6},{6,2},{3,7},{7,3},{8,12},{12,8},{9,1... | collective-permute-start | bytes 2359304 | tf_op jit(solution)/shard_map/ppermute | solution.py:111
  396.7 27.2 %collective-permute-start.71 = (bf16[2,2,48,1152]{3,2,1,0:T(8,128)(2,1)S(1)}, bf16[2,2,48,1152]{3,2,1,0:T(8,128)(2,1)S(1)}, u32[]{:S(2)}, u32[]{:S(2)}) collective-permute-start(bf16[2,2,48,1152]{3,2,1,0:T(8,128)(2,1)S(1)} %get-tuple-element.524), channel_id=1, source_target_pairs={{0,16},{8,24},{16,0},{24,8},{1,17},{9,25},{17,1},{25,9},{2,18},{10... | collective-permute-start | bytes 1327112 | tf_op jit(solution)/shard_map/ppermute | solution.py:116
  397.9 25.9 %collective-permute-start.67 = (bf16[4,96,384]{2,1,0:T(8,128)(2,1)S(1)}, bf16[4,96,384]{2,1,0:T(8,128)(2,1)S(1)}, u32[]{:S(2)}, u32[]{:S(2)}) collective-permute-start(bf16[4,96,384]{2,1,0:T(8,128)(2,1)S(1)} %get-tuple-element.518), channel_id=1, source_target_pairs={{0,2},{2,0},{1,3},{3,1},{4,6},{6,4},{5,7},{7,5},{8,10},{10,8},{9,1... | collective-permute-start | bytes 884744 | tf_op jit(solution)/shard_map/ppermute | solution.py:111
  398.8 25.1 %collective-permute-start.68 = (bf16[4,96,384]{2,1,0:T(8,128)(2,1)S(1)}, bf16[4,96,384]{2,1,0:T(8,128)(2,1)S(1)}, u32[]{:S(2)}, u32[]{:S(2)}) collective-permute-start(bf16[4,96,384]{2,1,0:T(8,128)(2,1)S(1)} %get-tuple-element.519), channel_id=1, source_target_pairs={{0,4},{4,0},{1,5},{5,1},{2,6},{6,2},{3,7},{7,3},{8,12},{12,8},{9,1... | collective-permute-start | bytes 884744 | tf_op jit(solution)/shard_map/ppermute | solution.py:111
  438.3 31.4 %collective-permute-start.75 = (bf16[2,48,1920]{2,1,0:T(8,128)(2,1)S(1)}, bf16[2,48,1920]{2,1,0:T(8,128)(2,1)S(1)}, u32[]{:S(2)}, u32[]{:S(2)}) collective-permute-start(bf16[2,48,1920]{2,1,0:T(8,128)(2,1)S(1)} %get-tuple-element.545), channel_id=1, source_target_pairs={{0,16},{8,24},{16,0},{24,8},{1,17},{9,25},{17,1},{25,9},{2,18},{10... | collective-permute-start | bytes 1105928 | tf_op jit(solution)/shard_map/ppermute | solution.py:116
  440.2 29.4 %collective-permute-start.76 = (bf16[2,48,1920]{2,1,0:T(8,128)(2,1)S(1)}, bf16[2,48,1920]{2,1,0:T(8,128)(2,1)S(1)}, u32[]{:S(2)}, u32[]{:S(2)}) collective-permute-start(bf16[2,48,1920]{2,1,0:T(8,128)(2,1)S(1)} %get-tuple-element.546), channel_id=1, source_target_pairs={{0,24},{8,0},{16,8},{24,16},{1,25},{9,1},{17,9},{25,17},{2,26},{10... | collective-permute-start | bytes 1105928 | tf_op jit(solution)/shard_map/ppermute | solution.py:116
  (120 other events, 1576.4 us)

commit v4 on v3

--- a/solution.py
+++ b/solution.py
@@ -133,7 +133,7 @@
 
 
 def depth_sent(blocks, shifts):
-    return {k: shifted(blocks[k], k) for k in shifts}
+    return {k: jax.tree.map(lambda v: shifted(v, k), blocks[k]) for k in shifts}
 
 
 def in_order(pieces):
@@ -166,7 +166,8 @@
 
 
 LITTLE = pl.CostEstimate(flops=1, bytes_accessed=1, transcendentals=0)
-SPACE = pltpu.CompilerParams(vmem_limit_bytes=48 << 20)
+SPACE = pltpu.CompilerParams(vmem_limit_bytes=20 << 20)
+ROOM = pltpu.CompilerParams(vmem_limit_bytes=14 << 20)
 VMEM = pl.BlockSpec(memory_space=pltpu.VMEM)
 SMEM = pl.BlockSpec(memory_space=pltpu.SMEM)
 
@@ -181,7 +182,7 @@
         in_specs=[SMEM] + [VMEM] * len(arrays),
         out_specs=[VMEM] * len(shapes),
         out_shape=list(shapes),
-        compiler_params=SPACE,
+        compiler_params=ROOM,
         cost_estimate=LITTLE,
     )(here, *arrays)
 
@@ -234,16 +235,16 @@
 
     def kernel(here_ref, *refs):
         piece_refs, (gate_ref, up_ref) = refs[:count], refs[count : count + 2]
-        mine_ref, share_ref, send_ref, send_share_ref = refs[count + 2 :]
+        mine_ref, share_ref, send_ref = refs[count + 2 :]
         core = here_ref[3]
         for k, ref in enumerate(piece_refs):
             at = around(here_ref[0], -k, nz)
             piece = ref[...]
             zero, one = columns(piece, 0), columns(piece, 1)
             mine_ref[at] = jnp.where(core == 0, zero, one)
-            send_ref[at] = jnp.where(core == 0, one, zero)
+            send_ref[at, 0, :, :inner_width] = jnp.where(core == 0, one, zero)
         share_ref[...] = jnp.zeros_like(share_ref)
-        send_share_ref[...] = jnp.zeros_like(send_share_ref)
+        send_ref[:, 1:] = jnp.zeros_like(send_ref[:, 1:])
         for own in range(nc):
 
             @pl.when(core == own)
@@ -251,18 +252,19 @@
                 for m, ref in enumerate((gate_ref, up_ref)):
                     for d in range(nz * ny * nx * nc):
                         z, p, c = d // (ny * nx * nc), d // nc % (ny * nx), d % nc
-                        out = share_ref if c == own else send_share_ref
-                        out[z, m, :, lane * p : lane * p + unit] = ref[
-                            :, unit * d : unit * d + unit
-                        ]
+                        columns = slice(lane * p, lane * p + unit)
+                        value = ref[:, unit * d : unit * d + unit]
+                        if c == own:
+                            share_ref[z, m, :, columns] = value
+                        else:
+                            send_ref[z, 1 + m, :, columns] = value
 
     return run(
         kernel,
         (
             shape_of((nz, rows, inner_width)),
             shape_of((nz, 2, rows, hidden_width)),
-            shape_of((nz, rows, inner_width)),
-            shape_of((nz, 2, rows, hidden_width)),
+            shape_of((nz, 3, rows, max(inner_width, hidden_width))),
         ),
         here,
         *pieces,
@@ -271,16 +273,31 @@
     )
 
 
-def share_blocks(here, mine, came):
-    nz = mine.shape[0]
+def share_blocks(here, mine, came, skip=0):
+    nz, matrices = mine.shape[:2]
+    width = mine.shape[3]
+    block = (2,) + mine.shape[1:]
+    single = (2,) + mine.shape[2:]
 
     def kernel(here_ref, mine_ref, came_ref, *outs):
-        for k, out in enumerate(outs):
+        outs = list(outs)
+        for k in range(nz):
             at = around(here_ref[0], k, nz)
-            out[0] = mine_ref[at]
-            out[1] = came_ref[at]
-
-    return run(kernel, [shape_of((2,) + mine.shape[1:])] * nz, here, mine, came)
+            if nz == 4 and k == 2:
+                for m in range(matrices):
+                    out = outs.pop(0)
+                    out[0] = mine_ref[at, m]
+                    out[1] = came_ref[at, skip + m, :, :width]
+            else:
+                out = outs.pop(0)
+                out[0] = mine_ref[at]
+                out[1] = came_ref[at, skip:, :, :width]
+
+    shapes = []
+    for k in range(nz):
+        shapes += [shape_of(single)] * matrices if nz == 4 and k == 2 else [shape_of(block)]
+    out = list(run(kernel, shapes, here, mine, came))
+    return [out[0], out[1], (out[2], out[3]), out[4]] if nz == 4 else out
 
 
 def split_output(here, pieces):
@@ -300,32 +317,48 @@
     return run(kernel, [shape_of((nz, rows, half))] * 2, here, *pieces)
 
 
-def place_shares(here, pieces):
-    nz = len(pieces)
+def place_shares(here, pieces, last, split):
+    nz = len(pieces) + (1 if last else 0)
+    shifts = [0, 1, *range(2 + (1 if last else 0), nz)]
+    pieces, number = list(pieces), len(pieces)
+    cores, matrices, rows, width = pieces[0].shape
 
     def kernel(here_ref, *refs):
-        gate_ref, up_ref = refs[nz:]
-        for k, ref in enumerate(refs[:nz]):
+        first_ref, second_ref = refs[number + len(last) :]
+        for k, ref in zip(shifts, refs[:number]):
             at = around(here_ref[0], -k, nz)
-            for i in range(2):
-                gate_ref[at, i] = ref[i, 0]
-                up_ref[at, i] = ref[i, 1]
-
-    return run(kernel, [shape_of((nz, 2) + pieces[0].shape[2:])] * 2, here, *pieces)
-
-
-def assemble(here_ref, refs, out):
+            for i in range(cores):
+                for m in range(matrices):
+                    first_ref[m, at, i] = ref[i, m, :, :split]
+                    second_ref[m, at, i] = ref[i, m, :, split:]
+        for m, ref in enumerate(refs[number : number + len(last)]):
+            at = around(here_ref[0], -2, nz)
+            for i in range(cores):
+                first_ref[m, at, i] = ref[i, :, :split]
+                second_ref[m, at, i] = ref[i, :, split:]
+
+    return run(
+        kernel,
+        [shape_of((matrices, nz, cores, rows, n)) for n in (split, width - split)],
+        here,
+        *pieces,
+        *last,
+    )
+
+
+def assemble(here_ref, refs, out, view=lambda ref: ref, at=0):
     y, x, c = here_ref[1], here_ref[2], here_ref[3]
     own, from_x, from_y, *far = refs
+    columns = slice(at, at + own.shape[-1])
     for ref, at_y, at_x in ((own, y, x), (from_x, y, 1 - x), (from_y, 1 - y, x)):
         for z in range(out.shape[0]):
             for i in range(2):
-                out[z, at_y, at_x, c if i == 0 else 1 - c] = ref[z, i]
+                out[z, at_y, at_x, c if i == 0 else 1 - c, :, columns] = view(ref)[z, i]
     for z in range(out.shape[0]):
         for i in range(2):
             block = [ref[z, i] for ref in far]
             block = block[0] if len(block) == 1 else jnp.concatenate(block, axis=1)
-            out[z, 1 - y, 1 - x, c if i == 0 else 1 - c] = block
+            out[z, 1 - y, 1 - x, c if i == 0 else 1 - c, :, columns] = block
 
 
 def six(own):
@@ -580,8 +613,12 @@
 
             @pl.when(step == 0)
             def _():
-                assemble(here_ref, weight_refs[: tables // 2], scratch[0])
-                assemble(here_ref, weight_refs[tables // 2 :], scratch[1])
+                at = 0
+                for pack in (weight_refs[:5], weight_refs[5:]):
+                    for m in range(2):
+                        group = (*pack[:3], pack[3 + m])
+                        assemble(here_ref, group, scratch[m], lambda ref, m=m: ref.at[m], at)
+                    at += pack[0].shape[-1]
 
             wg, wu = (ref[...].reshape(width, hidden_width) for ref in scratch)
         else:
@@ -612,7 +649,10 @@
     rows = pl.BlockSpec((tile, hidden_width), lambda i: (i, 0))
     group = shape_of((count, width))
     wide_rows = shape_of((2 * count, hidden_width))
-    scratch = [pltpu.VMEM(six(weights[0]), jnp.bfloat16)] * 2 if pieces else []
+    scratch = []
+    if pieces:
+        dims = six(weights[0][0])[:-1] + (hidden_width,)
+        scratch = [pltpu.VMEM(dims, jnp.bfloat16)] * 2
     return pl.pallas_call(
         kernel,
         grid=(2 * steps,),
@@ -621,7 +661,7 @@
         out_specs=[spec_a, spec_b, rows, rows, rows],
         out_shape=[group, group, wide_rows, wide_rows, wide_rows],
         scratch_shapes=scratch,
-        compiler_params=pltpu.CompilerParams(vmem_limit_bytes=56 << 20),
+        compiler_params=pltpu.CompilerParams(vmem_limit_bytes=42 << 20),
         cost_estimate=LITTLE,
     )(here, *normed, *upstream, weight_down, *weights)
 
@@ -784,14 +824,24 @@
 def collect_columns(here, pieces, sizes, unit, lane):
     nz, ny, nx, nc = sizes
     rows = pieces[0].shape[2]
+    flat = [v for piece in pieces for v in (piece if isinstance(piece, tuple) else (piece,))]
+    number = len(flat)
 
     def kernel(here_ref, *refs):
-        gate_ref, up_ref, placed = refs[nz:]
+        gate_ref, up_ref, placed = refs[number:]
+        refs = list(refs[:number])
         core = here_ref[3]
-        for k, ref in enumerate(refs[:nz]):
+        for k, piece in enumerate(pieces):
             at = around(here_ref[0], -k, nz)
-            placed[at, core] = ref[0]
-            placed[at, 1 - core] = ref[1]
+            if isinstance(piece, tuple):
+                for m in range(2):
+                    ref = refs.pop(0)
+                    placed[at, core, m] = ref[0]
+                    placed[at, 1 - core, m] = ref[1]
+            else:
+                ref = refs.pop(0)
+                placed[at, core] = ref[0]
+                placed[at, 1 - core] = ref[1]
         for m, ref in enumerate((gate_ref, up_ref)):
             for d in range(nz * ny * nx * nc):
                 z, p, c = d // (ny * nx * nc), d // nc % (ny * nx), d % nc
@@ -802,13 +852,13 @@
     shape = shape_of((rows, unit * nz * ny * nx * nc), jnp.float32)
     return pl.pallas_call(
         kernel,
-        in_specs=[SMEM] + [VMEM] * nz,
+        in_specs=[SMEM] + [VMEM] * number,
         out_specs=[VMEM] * 2,
         out_shape=[shape, shape],
         scratch_shapes=[pltpu.VMEM((nz,) + pieces[0].shape, jnp.bfloat16)],
         compiler_params=SPACE,
         cost_estimate=LITTLE,
-    )(here, *pieces)
+    )(here, *flat)
 
 
 def down_grads(here, hidden, upstream, lane):
@@ -1094,35 +1144,34 @@
     )
     packed = jnp.concatenate([query_weight, key_weight, value_weight, vectors], axis=1)
     pieces = depth_gathered(packed, every_shift()) | {0: packed}
-    down_near = plane_near(down_weight) if in_square else ()
+    cut = down_weight.shape[0] // 32 * 16
+    down_near = [plane_near(down_weight[:cut])] if in_square else ()
     cosine, sine, allowed = position_tables(doc_lengths, shard_tokens)
+    first_shift, last_shift = every_shift()[0], every_shift()[-1]
     pieces, down_near, cosine, sine, allowed = sync(pieces, down_near, cosine, sine, allowed)
-    first_shift, *more_shifts = every_shift()
-
-    mine, shares, send, send_shares = split_shares(
+
+    mine, shares, send = split_shares(
         here, in_order(pieces), gate_weight, up_weight, sizes, unit, lane, query_width, key_width
     )
-    came, came_shares = swapped(send, "c"), swapped(send_shares, "c")
+    came = swapped(send, "c")
     late_output = after(output_weight, pieces)
-    output_pieces = depth_gathered(late_output, [first_shift]) | {0: late_output}
-    cut = down_weight.shape[0] // 32 * 16
+    output_pieces = depth_gathered(late_output, near_shifts()) | {0: late_output}
+    if in_square:
+        down_near = [*down_near, plane_near(after(down_weight[cut:], pieces))]
+    mine, came, shares, output_pieces, down_near = sync(
+        mine, came, shares, output_pieces, down_near
+    )
+
+    inner_own = jnp.stack([mine, came[:, 0, :, : mine.shape[2]]], axis=1)
+    share_parts = dict(enumerate(share_blocks(here, shares, came, 1)))
+    inner_near = plane_near(inner_own) if in_square else ()
+    output_pieces |= depth_gathered(after(late_output, mine), far_shifts())
+    share_pieces = depth_sent(share_parts, [first_shift]) | {0: share_parts[0]}
     down_far = ()
     if in_square:
-        down_far = swapped(down_near[0][:cut], "y"), swapped(down_near[1][cut:], "x")
-    mine, came, shares, came_shares, output_pieces, down_far = sync(
-        mine, came, shares, came_shares, output_pieces, down_far
-    )
-
-    inner_own = jnp.stack([mine, came], axis=1)
-    share_parts = dict(enumerate(share_blocks(here, shares, came_shares)))
-    if in_square:
-        inner_near = plane_near(inner_own)
-    else:
-        inner_near = ()
-    output_pieces |= depth_gathered(after(late_output, mine), more_shifts)
-    share_pieces = depth_sent(share_parts, [first_shift]) | {0: share_parts[0]}
-    inner_own, inner_near, output_pieces, share_parts, share_pieces = sync(
-        inner_own, inner_near, output_pieces, share_parts, share_pieces
+        down_far = swapped(down_near[0][0], "y"), swapped(down_near[1][1], "x")
+    inner_own, inner_near, output_pieces, share_parts, share_pieces, down_far = sync(
+        inner_own, inner_near, output_pieces, share_parts, share_pieces, down_far
     )
 
     middle = 512
@@ -1137,13 +1186,19 @@
     output_mine, output_send = split_output(here, in_order(output_pieces))
     output_came = swapped(output_send, "c")
     other_tokens = swapped(after(own_tokens, inner_own), "c")
-    share_pieces |= depth_sent(after(share_parts, inner_own), more_shifts[1:])
+    share_pieces |= depth_sent(share_parts, [last_shift])
+    share_split = hidden_width // 256 * 128
     inner_weights, output_mine, output_came, other_tokens, share_pieces = sync(
         inner_weights, output_mine, output_came, other_tokens, share_pieces
     )
 
     output_own = jnp.stack([output_mine, output_came], axis=1)
-    share_pieces |= depth_sent(after(share_parts, output_mine), more_shifts[:1])
+    if nz == 4:
+        gate_part, up_part = after(share_parts[2], output_mine)
+        late_pieces = [shifted(gate_part, 2)]
+    else:
+        share_pieces |= depth_sent(after(share_parts, output_mine), far_shifts())
+        late_pieces = []
     output_near = plane_near(output_own) if in_square else ()
     first_normed, queries, own_pair, lines, weight_inner = inner_projections(
         here,
@@ -1158,8 +1213,10 @@
     weight_inner = weight_inner.reshape(width, -1)
     cosine_chip = cosine.reshape(chip_shape + (HD,))
     sine_chip = sine.reshape(chip_shape + (HD,))
-    own_pair, output_own, output_near, share_pieces = sync(
-        own_pair, output_own, output_near, share_pieces
+    late_upstream = after(upstream, inner_weights)
+    upstream_pieces = depth_gathered(late_upstream, [first_shift]) | {0: late_upstream}
+    own_pair, output_own, output_near, share_pieces, late_pieces, upstream_pieces = sync(
+        own_pair, output_own, output_near, share_pieces, late_pieces, upstream_pieces
     )
 
     middle = half // 2
@@ -1175,48 +1232,55 @@
     else:
         pairs = plane_gathered(own_pair)
         output_weights = (plane_whole(output_own).reshape(width, -1),)
-    gate_own, up_own = place_shares(here, in_order(share_pieces))
-    late_upstream = after(upstream, share_pieces)
-    upstream_pieces = depth_gathered(late_upstream, near_shifts()) | {0: late_upstream}
-    pairs, upstream_pieces, gate_own, up_own, output_weights = sync(
-        pairs, upstream_pieces, gate_own, up_own, output_weights
-    )
-
-    gate_near = plane_near(gate_own) if in_square else ()
-    upstream_pieces |= depth_gathered(after(late_upstream, pairs), far_shifts())
+    if nz == 4:
+        late_pieces.append(shifted(after(up_part, own_pair), 2))
+    pairs, output_weights, late_pieces = sync(pairs, output_weights, late_pieces)
+
+    first_own, second_own = place_shares(here, in_order(share_pieces), late_pieces, share_split)
+    first_near = plane_near(first_own) if in_square else ()
+    upstream_pieces |= depth_gathered(after(upstream, pairs), far_shifts())
     attended, turned, log_sums = attend(here, queries, pairs, allowed)
-    attended, turned, gate_near, upstream_pieces = sync(
-        attended, turned, gate_near, upstream_pieces
-    )
-
-    up_near = plane_near(after(up_own, attended)) if in_square else ()
-    upstream_mine = jnp.concatenate(in_order(upstream_pieces), axis=0)
-    upstream_other = swapped(upstream_mine, "c")
+    attended, turned, first_near, second_own, upstream_pieces = sync(
+        attended, turned, first_near, second_own, upstream_pieces
+    )
+
+    first_far = ()
+    if in_square:
+        first_far = swapped(first_near[0][0], "y"), swapped(first_near[1][1], "x")
+    upstream_pieces |= depth_gathered(after(upstream, attended), [last_shift])
     came = swapped(turned.reshape(chip_count, half), "c")
     part, send, attended_all, weight_output = output_projection(
         here, attended.reshape(chip_count, half), came, output_weights
     )
     weight_output = weight_output.reshape(width, half)
     first_hidden, second_normed = second_norm(here, own_tokens, part, swapped(send, "c"), lines)
-    second_normed, up_near, upstream_other = sync(second_normed, up_near, upstream_other)
+    second_normed, first_far, upstream_pieces = sync(second_normed, first_far, upstream_pieces)
 
     second_pieces = depth_gathered(second_normed, every_shift()) | {0: second_normed}
     if in_square:
-        gate_far, up_far = swapped(gate_near[0], "y"), swapped(up_near[1], "x")
-        weights = (gate_own, *gate_near, gate_far, up_own, *up_near, up_far)
+        second_near = plane_near(after(second_own, second_normed))
+        second_far = swapped(second_near[0][0], "y"), swapped(second_near[1][1], "x")
+        weights = (first_own, *first_near, *first_far, second_own, *second_near, *second_far)
         second_pieces, weights = sync(second_pieces, weights)
         y, x = lax.axis_index("y"), lax.axis_index("x")
         weight_down = jnp.zeros((2, 2, lane, width), jnp.bfloat16)
         for block, index in (
             (down_weight, (y, x, 0, 0)),
-            (down_near[0], (y, 1 - x, 0, 0)),
-            (down_near[1], (1 - y, x, 0, 0)),
+            (down_near[0][0], (y, 1 - x, 0, 0)),
+            (down_near[1][0], (y, 1 - x, cut, 0)),
+            (down_near[0][1], (1 - y, x, 0, 0)),
+            (down_near[1][1], (1 - y, x, cut, 0)),
             (down_far[0], (1 - y, 1 - x, 0, 0)),
             (down_far[1], (1 - y, 1 - x, cut, 0)),
         ):
             weight_down = lax.dynamic_update_slice(weight_down, block[None, None], index)
     else:
-        weights = tuple(plane_whole(v).reshape(width, -1) for v in (gate_own, up_own))
+        weights = tuple(
+            jnp.concatenate(
+                [plane_whole(v[m]).reshape(width, -1) for v in (first_own, second_own)], axis=1
+            )
+            for m in range(2)
+        )
         weight_down = lax.all_gather(down_weight, PLANE, axis=0)
         weight_down = jnp.pad(weight_down, ((0, 0), (0, lane - unit), (0, 0)))
         second_pieces, weights, weight_down = sync(second_pieces, weights, weight_down)
@@ -1224,7 +1288,8 @@
 
     second_mine = jnp.concatenate(in_order(second_pieces), axis=0)
     second_group = (swapped(second_mine, "c"), second_mine)
-    upstream_group = (upstream_other, upstream_mine)
+    upstream_mine = jnp.concatenate(in_order(upstream_pieces), axis=0)
+    upstream_group = (swapped(upstream_mine, "c"), upstream_mine)
     normed_send, normed_own, hidden, gate_grad, up_grad = feed_forward(
         here, second_group, upstream_group, weights, weight_down
     )
@@ -1289,7 +1354,7 @@
     four = (nz, nc, owned, hidden_width)
     if in_square:
         came_gate, came_up = swapped(send_gate, "x"), swapped(send_up, "y")
-    output_pieces = depth_sent(output_parts, near_shifts())
+    output_pieces = depth_sent(output_parts, far_shifts())
     if in_square:
         send_a, keep_a, send_b, keep_b = share_grads(
             here,
@@ -1323,26 +1388,19 @@
         (came_gate.reshape(four), came_up.reshape(four)),
     )
     came_shares = swapped(send_shares, "c")
-    output_pieces |= depth_sent(after(output_parts, part_near), far_shifts())
+    output_pieces |= depth_sent(after(output_parts, part_near), [first_shift])
     if in_square:
         step = low(wide(part_near) + wide(swapped(part_far, "y")))
-        send_a, send_b = after((send_a, send_b), step)
         pair_sum = wide(step[0]) + wide(swapped(step[1], "x"))
-        came_a, came_b = swapped(send_a, "y"), swapped(send_b, "x")
     else:
         pair_sum = plane_summed(jnp.concatenate([part_near, part_far], axis=0))
-    else_came = (came_a, came_b) if in_square else ()
-    pair_sum, shares, came_shares, output_pieces, else_came = sync(
-        pair_sum, shares, came_shares, output_pieces, else_came
-    )
-    layer_output = first_hidden + output_own + sum(wide(v) for v in in_order(output_pieces))
-
     share_parts = dict(enumerate(share_blocks(here, shares, came_shares)))
+    pair_sum, share_parts, output_pieces = sync(pair_sum, share_parts, output_pieces)
+
     share_pieces = depth_sent(share_parts, near_shifts()) | {0: share_parts[0]}
     if in_square:
-        came_a, came_b = else_came
-        first_send, first_keep, second_send, second_keep = after(down_parts, pair_sum)
-        came_first, came_second = swapped(first_send, "y"), swapped(second_send, "x")
+        send_a, send_b = after((send_a, send_b), pair_sum)
+        came_a, came_b = swapped(send_a, "y"), swapped(send_b, "x")
     else:
         down_sum = lax.psum_scatter(
             down_parts.reshape(ny * nx, lane, width), PLANE, scatter_dimension=0, tiled=False
@@ -1371,8 +1429,8 @@
             rows,
             vector_terms,
         )
-        send_c, keep_c, send_d, keep_d, came_first, came_second, share_parts, share_pieces = sync(
-            send_c, keep_c, send_d, keep_d, came_first, came_second, share_parts, share_pieces
+        send_c, keep_c, send_d, keep_d, came_a, came_b, share_parts, share_pieces = sync(
+            send_c, keep_c, send_d, keep_d, came_a, came_b, share_parts, share_pieces
         )
         share_pieces |= depth_sent(share_parts, far_shifts())
         send_a, keep_a, send_b, keep_b = plane_step(here, (keep_a, keep_b), (came_a, came_b))
@@ -1383,10 +1441,8 @@
         )
         send_c, keep_c, send_d, keep_d = plane_step(here, (keep_c, keep_d), (came_c, came_d))
         came_c, came_d = swapped(send_c, "x"), swapped(send_d, "y")
-        first_send, first_keep, second_send, second_keep = down_step(
-            here, (first_keep, second_keep), (came_first, came_second)
-        )
-        came_c, came_d, first_send, second_send = sync(came_c, came_d, first_send, second_send)
+        output_pieces |= depth_sent(after(output_parts, share_pieces), [last_shift])
+        came_c, came_d, output_pieces = sync(came_c, came_d, output_pieces)
         keeps, cames = (
             [v.reshape(nz, nc, owned, -1) for v in group]
             for group in ((keep_a, keep_b, keep_c, keep_d), (came_a, came_b, came_c, came_d))
@@ -1404,12 +1460,21 @@
             for v in (output_term, inner_term)
         ]
         cames = [jnp.zeros_like(v) for v in keeps]
+    if not in_square:
+        output_pieces |= depth_sent(output_parts, [last_shift])
+    layer_output = first_hidden + output_own + sum(wide(v) for v in in_order(output_pieces))
     gate_sum, up_sum = collect_columns(here, in_order(share_pieces), sizes, unit, lane)
 
     own, *parts = inner_blocks(here, keeps, cames)
     parts = dict(enumerate(parts, 1))
     pieces = depth_sent(parts, every_shift())
     if in_square:
+        first_send, first_keep, second_send, second_keep = after(down_parts, came_c)
+        came_first, came_second = swapped(first_send, "y"), swapped(second_send, "x")
+        first_send, first_keep, second_send, second_keep = down_step(
+            here, (first_keep, second_keep), (came_first, came_second)
+        )
+        first_send, second_send = after((first_send, second_send), pieces[first_shift])
         came_first, came_second = swapped(first_send, "x"), swapped(second_send, "y")
         down_sum = jnp.concatenate(
             [

time: 493 us -> 466 us (0.945)
  waiting for transfers between devices: 246 us -> 227 us
  Pallas kernels: 114 us -> 96.8 us
  starting transfers between devices: 88.2 us -> 96.8 us
    ppermute x53 -> x56, waiting for transfers between devices: 109 us -> 92.2 us  [swapped(): return lax.ppermute(values, axis, [(0, 1), (1, 0)])]
    ppermute x53 -> x56, starting transfers between devices: 48.8 us -> 61.2 us  [swapped(): return lax.ppermute(values, axis, [(0, 1), (1, 0)])]
    pallas_call x10, Pallas kernels: 45.1 us -> 36.6 us  [run_grid(): pl.pallas_call(kernel, grid=(grid,), in_specs=[SMEM] + list(specs), out_s...]
    ppermute x27 -> x29, starting transfers between devices: 39.4 us -> 35.6 us  [shifted(): lax.ppermute(values, 'z', [(i, (i + amount) % count) for i in range(count)])]
    ppermute x27 -> x29, waiting for transfers between devices: 137 us -> 135 us  [shifted(): lax.ppermute(values, 'z', [(i, (i + amount) % count) for i in range(count)])]
    unnamed x134 -> x128, local copies, waits for them, and re-layouts: 17.2 us -> 17.2 us
  transfers between devices with their start and end apart: 80 -> 85, of which waited for: 42 -> 42; matrix products, arithmetic and copies ran while one was open for 2% -> 3% of each run, Pallas kernels for 15% -> 12%
where the time goes in v4:
time: 466 us; the launch traced here: 457 us
  waiting for transfers between devices  227 us (49%)
  starting transfers between devices  96.8 us (21%)
  Pallas kernels  96.8 us (21%)
  local copies, waits for them, and re-layouts  26.1 us (6%)
  other arithmetic  8.69 us (2%)
    ppermute x29, waiting for transfers between devices, shifted(): lax.ppermute(values, 'z', [(i, (i + amount) % count) for i in range(count)])  135 us
    ppermute x56, waiting for transfers between devices, swapped(): return lax.ppermute(values, axis, [(0, 1), (1, 0)])  92.2 us
    ppermute x56, starting transfers between devices, swapped(): return lax.ppermute(values, axis, [(0, 1), (1, 0)])  61.2 us
    pallas_call x10, Pallas kernels, run_grid(): pl.pallas_call(kernel, grid=(grid,), in_specs=[SMEM] + list(specs), out_s...  36.6 us
    ppermute x29, starting transfers between devices, shifted(): lax.ppermute(values, 'z', [(i, (i + amount) % count) for i in range(count)])  35.6 us
    pallas_call x1, Pallas kernels, feed_forward(): pl.pallas_call(kernel, grid=(2 * steps,), in_specs=[SMEM, spec_a, spec_b,...  29.8 us
    pallas_call x18, Pallas kernels, run(): pl.pallas_call(kernel, in_specs=[SMEM] + [VMEM] * len(arrays), out_specs=...  22.1 us
    unnamed x128, local copies, waits for them, and re-layouts  17.2 us
  transfers between devices with their start and end apart: 85, of which 42 were waited for; matrix products, arithmetic and copies ran while one was open for 3% of the time, Pallas kernels for 12%

profile of v4, /device:TPU:29, one launch (start us, length us, event | category | flops | bytes accessed | tf_op | source)
XLA Modules:
  0.0 457.3 jit_solution(2950094729227368432)
XLA Ops:
  14.7 5.0 %collective-permute-done.1.refs_2_ = bf16[48,2176]{1,0:T(8,128)(2,1)S(1)} collective-permute-done((bf16[48,2176]{1,0:T(8,128)(2,1)S(1)}, bf16[48,2176]{1,0:T(8,128)(2,1)S(1)}, u32[]{:S(2)}, u32[]{:S(2)}) %collective-permute-start.1) | collective-permute-done | bytes 208928 | tf_op jit(solution)/shard_map/ppermute | solution.py:116
  35.3 3.9 collective-permute-done.6.refs_1_
  48.4 19.7 %collective-permute-done.14 = bf16[128,1536]{1,0:T(8,128)(2,1)S(1)} collective-permute-done((bf16[128,1536]{1,0:T(8,128)(2,1)}, bf16[128,1536]{1,0:T(8,128)(2,1)S(1)}, u32[]{:S(2)}, u32[]{:S(2)}) %collective-permute-start.14) | collective-permute-done | bytes 393248 | tf_op jit(solution)/shard_map/ppermute | solution.py:111
  90.3 12.0 %collective-permute-done.23.refs_3_ = bf16[2,48,1152]{2,1,0:T(8,128)(2,1)S(1)} collective-permute-done((bf16[2,48,1152]{2,1,0:T(8,128)(2,1)S(1)}, bf16[2,48,1152]{2,1,0:T(8,128)(2,1)S(1)}, u32[]{:S(2)}, u32[]{:S(2)}) %collective-permute-start.23) | collective-permute-done | bytes 221216 | tf_op jit(solution)/shard_map/ppermute | solution.py:116
  102.4 4.0 collective-permute-done.25
  121.0 5.3 %shard_map.258 = (bf16[2,2,64,768]{3,2,1,0:T(8,128)(2,1)S(1)}, bf16[2,2,64,768]{3,2,1,0:T(8,128)(2,1)S(1)}, f32[2,6,128,128]{3,2,1,0:T(8,128)S(1)}) custom-call(s32[4]{0:T(128)S(1)} %pad_add_fusion.here_ref, bf16[2,6,2,64,128]{4,3,2,1,0:T(8,128)(2,1)S(1)} %get-tuple-element.354.q_ref, bf16[4,2,2,64,256]{4,3,2,1,0:T(8,128)(2,1)S(1)} %pad_maximum_fusion.3.pair_ref, ...), custom_call_target="tpu_custom_call" | custom-call | flops 1 | bytes 1 | tf_op jit(solution)/shard_map/pallas_call | solution.py:191
  130.8 13.1 %collective-permute-start.33 = (bf16[256,768]{1,0:T(8,128)(2,1)S(1)}, bf16[256,768]{1,0:T(8,128)(2,1)S(1)}, u32[]{:S(2)}, u32[]{:S(2)}) collective-permute-start(bf16[256,768]{1,0:T(8,128)(2,1)S(1)} %bitcast.112), channel_id=1, source_target_pairs={{0,1},{1,0},{2,3},{3,2},{4,5},{5,4},{6,7},{7,6},{8,9},{9,8},{10,11... | collective-permute-start | bytes 1179656 | tf_op jit(solution)/shard_map/ppermute | solution.py:111
  156.0 4.5 collective-permute-done.37
  166.9 15.8 %collective-permute-done.42.refs_7_ = bf16[2,4,2,48,640]{4,3,2,1,0:T(8,128)(2,1)S(1)} collective-permute-done((bf16[2,4,2,48,640]{4,3,2,1,0:T(8,128)(2,1)S(1)}, bf16[2,4,2,48,640]{4,3,2,1,0:T(8,128)(2,1)S(1)}, u32[]{:S(2)}, u32[]{:S(2)}) %collective-permute-start.42) | collective-permute-done | bytes 983072 | tf_op jit(solution)/shard_map/ppermute | solution.py:111
  201.0 29.8 %shard_map.262 = (bf16[512,1536]{1,0:T(8,128)(2,1)S(1)}, bf16[512,1536]{1,0:T(8,128)(2,1)S(1)}, bf16[1024,1152]{1,0:T(8,128)(2,1)}, bf16[1024,1152]{1,0:T(8,128)(2,1)}, bf16[1024,1152]{1,0:T(8,128)(2,1)}) custom-call(s32[4]{0:T(128)S(1)} %pad_add_fusion.here_ref, bf16[512,1536]{1,0:T(8,128)(2,1)S(1)} %collective-permute-done.45.na_ref.refs_0_, ...), custom_call_target="tpu_custom_call" | custom-call | flops 1 | bytes 1 | tf_op jit(solution)/shard_map/pallas_call | solution.py:656
  236.3 9.9 %shard_map.264 = (bf16[4,2,96,1152]{3,2,1,0:T(8,128)(2,1)S(1)}, bf16[4,2,96,1152]{3,2,1,0:T(8,128)(2,1)S(1)}, bf16[4,2,96,1152]{3,2,1,0:T(8,128)(2,1)S(1)}, bf16[4,2,96,1152]{3,2,1,0:T(8,128)(2,1)S(1)}) custom-call(s32[4]{0:T(128)S(1)} %pad_add_fusion.here_ref, bf16[512,1536]{1,0:T(8,128)(2,1)S(1)} %collective-permute-done.45.na_ref.refs_0_, ...), custom_call_target="tpu_custom_call" | custom-call | flops 1 | bytes 1 | tf_op jit(solution)/shard_map/pallas_call | solution.py:191
  254.2 5.6 %shard_map.266 = (bf16[512,1536]{1,0:T(8,128)(2,1)S(1)}, bf16[512,1536]{1,0:T(8,128)(2,1)S(1)}) custom-call(s32[4]{0:T(128)S(1)} %pad_add_fusion.here_ref, bf16[1024,1152]{1,0:T(8,128)(2,1)S(1)} %copy-done.2, bf16[1152,1536]{1,0:T(8,128)(2,1)S(1)} %bitcast.78), custom_call_target="tpu_custom_call" | custom-call | flops 1 | bytes 1 | tf_op jit(solution)/shard_map/pallas_call | solution.py:191
  259.9 5.3 %shard_map.265 = (bf16[2,144,1536]{2,1,0:T(8,128)(2,1)S(1)}, bf16[2,144,1536]{2,1,0:T(8,128)(2,1)S(1)}, bf16[2,144,1536]{2,1,0:T(8,128)(2,1)S(1)}, bf16[2,144,1536]{2,1,0:T(8,128)(2,1)S(1)}) custom-call(s32[4]{0:T(128)S(1)} %pad_add_fusion.here_ref, bf16[1024,1152]{1,0:T(8,128)(2,1)S(1)} %copy-done.2, bf16[512,1536]{1,0:T(8,128)(2,1)S(1)} %copy-done.8, ...), custom_call_target="tpu_custom_call" | custom-call | flops 1 | bytes 1 | tf_op jit(solution)/shard_map/pallas_call | solution.py:889
  265.2 21.0 %collective-permute-done.49.refs_1_ = bf16[128,1536]{1,0:T(8,128)(2,1)S(1)} collective-permute-done((bf16[128,1536]{1,0:T(8,128)(2,1)S(1)}, bf16[128,1536]{1,0:T(8,128)(2,1)S(1)}, u32[]{:S(2)}, u32[]{:S(2)}) %collective-permute-start.49) | collective-permute-done | bytes 393248 | tf_op jit(solution)/shard_map/ppermute | solution.py:116
  303.5 6.2 %shard_map.270 = (bf16[2,2,64,768]{3,2,1,0:T(8,128)(2,1)S(1)}, bf16[2,2,2,64,256]{4,3,2,1,0:T(8,128)(2,1)S(1)}, bf16[2,2,2,64,256]{4,3,2,1,0:T(8,128)(2,1)S(1)}) custom-call(s32[4]{0:T(128)S(1)} %pad_add_fusion.here_ref, bf16[2,6,2,64,128]{4,3,2,1,0:T(8,128)(2,1)S(1)} %copy-done.24, bf16[4,2,2,64,256]{4,3,2,1,0:T(8,128)(2,1)S(1)} %pad_maximum_fusion.3.pair_ref, ...), custom_call_target="tpu_custom_call" | custom-call | flops 1 | bytes 1 | tf_op jit(solution)/shard_map/pallas_call | solution.py:191
  309.6 9.6 %collective-permute-done.58 = bf16[128,1536]{1,0:T(8,128)(2,1)S(1)} collective-permute-done((bf16[128,1536]{1,0:T(8,128)(2,1)S(1)}, bf16[128,1536]{1,0:T(8,128)(2,1)S(1)}, u32[]{:S(2)}, u32[]{:S(2)}) %collective-permute-start.58) | collective-permute-done | bytes 393248 | tf_op jit(solution)/shard_map/ppermute | solution.py:116
  344.0 4.9 %collective-permute-done.66.refs_1_ = bf16[2,2,48,1152]{3,2,1,0:T(8,128)(2,1)S(1)} collective-permute-done((bf16[2,2,48,1152]{3,2,1,0:T(8,128)(2,1)S(1)}, bf16[2,2,48,1152]{3,2,1,0:T(8,128)(2,1)S(1)}, u32[]{:S(2)}, u32[]{:S(2)}) %collective-permute-start.66) | collective-permute-done | bytes 442400 | tf_op jit(solution)/shard_map/ppermute | solution.py:116
  348.9 10.1 %collective-permute-done.67.refs_4_ = bf16[2,2,48,1152]{3,2,1,0:T(8,128)(2,1)S(1)} collective-permute-done((bf16[2,2,48,1152]{3,2,1,0:T(8,128)(2,1)S(1)}, bf16[2,2,48,1152]{3,2,1,0:T(8,128)(2,1)S(1)}, u32[]{:S(2)}, u32[]{:S(2)}) %collective-permute-start.67) | collective-permute-done | bytes 442400 | tf_op jit(solution)/shard_map/ppermute | solution.py:116
  363.8 9.1 %collective-permute-done.72.refs_2_ = bf16[2,48,1152]{2,1,0:T(8,128)(2,1)S(1)} collective-permute-done((bf16[2,48,1152]{2,1,0:T(8,128)(2,1)S(1)}, bf16[2,48,1152]{2,1,0:T(8,128)(2,1)S(1)}, u32[]{:S(2)}, u32[]{:S(2)}) %collective-permute-start.72) | collective-permute-done | bytes 221216 | tf_op jit(solution)/shard_map/ppermute | solution.py:116
  372.9 12.7 %collective-permute-done.73.refs_3_ = bf16[2,48,1152]{2,1,0:T(8,128)(2,1)S(1)} collective-permute-done((bf16[2,48,1152]{2,1,0:T(8,128)(2,1)S(1)}, bf16[2,48,1152]{2,1,0:T(8,128)(2,1)S(1)}, u32[]{:S(2)}, u32[]{:S(2)}) %collective-permute-start.73) | collective-permute-done | bytes 221216 | tf_op jit(solution)/shard_map/ppermute | solution.py:116
  391.6 8.3 %collective-permute-done.76 = bf16[128,1536]{1,0:T(8,128)(2,1)S(1)} collective-permute-done((bf16[128,1536]{1,0:T(8,128)(2,1)S(1)}, bf16[128,1536]{1,0:T(8,128)(2,1)S(1)}, u32[]{:S(2)}, u32[]{:S(2)}) %collective-permute-start.76) | collective-permute-done | bytes 393248 | tf_op jit(solution)/shard_map/ppermute | solution.py:116
  403.7 14.0 %collective-permute-done.80.first_came = bf16[2,144,1536]{2,1,0:T(8,128)(2,1)S(1)} collective-permute-done((bf16[2,144,1536]{2,1,0:T(8,128)(2,1)S(1)}, bf16[2,144,1536]{2,1,0:T(8,128)(2,1)S(1)}, u32[]{:S(2)}, u32[]{:S(2)}) %collective-permute-start.80) | collective-permute-done | bytes 884768 | tf_op jit(solution)/shard_map/ppermute | solution.py:111
  427.0 4.6 collective-permute-done.83
  431.9 18.5 %collective-permute-done.78.refs_1_ = bf16[2,48,1920]{2,1,0:T(8,128)(2,1)S(1)} collective-permute-done((bf16[2,48,1920]{2,1,0:T(8,128)(2,1)S(1)}, bf16[2,48,1920]{2,1,0:T(8,128)(2,1)S(1)}, u32[]{:S(2)}, u32[]{:S(2)}) %collective-permute-start.78) | collective-permute-done | bytes 368672 | tf_op jit(solution)/shard_map/ppermute | solution.py:116
  (365 shorter events, 202.1 us)
Async XLA Ops:
  39.4 31.2 %collective-permute-start.11 = (bf16[4,2,48,1152]{3,2,1,0:T(8,128)(2,1)S(1)}, bf16[4,2,48,1152]{3,2,1,0:T(8,128)(2,1)S(1)}, u32[]{:S(2)}, u32[]{:S(2)}) collective-permute-start(bf16[4,2,48,1152]{3,2,1,0:T(8,128)(2,1)S(1)} %pad_maximum_fusion.1.refs_0_), channel_id=1, source_target_pairs={{0,4},{4,0},{1,5},{5,1},{2,6},{6,2},{3,7},{7,3},{8,12},{12,8},{9,1... | collective-permute-start | bytes 2654216 | tf_op jit(solution)/shard_map/ppermute | solution.py:111
  40.7 29.9 %collective-permute-start.10 = (bf16[4,2,48,1152]{3,2,1,0:T(8,128)(2,1)S(1)}, bf16[4,2,48,1152]{3,2,1,0:T(8,128)(2,1)S(1)}, u32[]{:S(2)}, u32[]{:S(2)}) collective-permute-start(bf16[4,2,48,1152]{3,2,1,0:T(8,128)(2,1)S(1)} %pad_maximum_fusion.1.refs_0_), channel_id=1, source_target_pairs={{0,2},{2,0},{1,3},{3,1},{4,6},{6,4},{5,7},{7,5},{8,10},{10,8},{9,1... | collective-permute-start | bytes 2654216 | tf_op jit(solution)/shard_map/ppermute | solution.py:111
  43.9 26.7 %collective-permute-start.15 = (bf16[152,1536]{1,0:T(8,128)(2,1)S(1)}, bf16[152,1536]{1,0:T(8,128)(2,1)S(1)}, u32[]{:S(2)}, u32[]{:S(2)}) collective-permute-start(bf16[152,1536]{1,0:T(8,128)(2,1)S(1)} %collective-permute-done.9), channel_id=1, source_target_pairs={{0,2},{2,0},{1,3},{3,1},{4,6},{6,4},{5,7},{7,5},{8,10},{10,8},{9,1... | collective-permute-start | bytes 1400840 | tf_op jit(solution)/shard_map/ppermute | solution.py:111
  44.9 23.2 %collective-permute-start.13 = (bf16[2,2,48,1152]{3,2,1,0:T(8,128)(2,1)S(1)}, bf16[2,2,48,1152]{3,2,1,0:T(8,128)(2,1)S(1)}, u32[]{:S(2)}, u32[]{:S(2)}) collective-permute-start(bf16[2,2,48,1152]{3,2,1,0:T(8,128)(2,1)S(1)} %get-tuple-element.326), channel_id=1, source_target_pairs={{0,8},{8,16},{16,24},{24,0},{1,9},{9,17},{17,25},{25,1},{2,10},{10... | collective-permute-start | bytes 1327112 | tf_op jit(solution)/shard_map/ppermute | solution.py:116
  48.1 20.0 %collective-permute-start.14 = (bf16[128,1536]{1,0:T(8,128)(2,1)}, bf16[128,1536]{1,0:T(8,128)(2,1)S(1)}, u32[]{:S(2)}, u32[]{:S(2)}) collective-permute-start(bf16[128,1536]{1,0:T(8,128)(2,1)} %collective-permute-done.3), channel_id=1, source_target_pairs={{0,4},{4,0},{1,5},{5,1},{2,6},{6,2},{3,7},{7,3},{8,12},{12,8},{9,1... | collective-permute-start | bytes 1179656 | tf_op jit(solution)/shard_map/ppermute | solution.py:111
  160.5 22.1 %collective-permute-start.42 = (bf16[2,4,2,48,640]{4,3,2,1,0:T(8,128)(2,1)S(1)}, bf16[2,4,2,48,640]{4,3,2,1,0:T(8,128)(2,1)S(1)}, u32[]{:S(2)}, u32[]{:S(2)}) collective-permute-start(bf16[2,4,2,48,640]{4,3,2,1,0:T(8,128)(2,1)S(1)} %copy-done.30), channel_id=1, source_target_pairs={{0,4},{4,0},{1,5},{5,1},{2,6},{6,2},{3,7},{7,3},{8,12},{12,8},{9,1... | collective-permute-start | bytes 2949128 | tf_op jit(solution)/shard_map/ppermute | solution.py:111
  161.4 22.0 %collective-permute-start.41 = (bf16[2,4,2,48,640]{4,3,2,1,0:T(8,128)(2,1)S(1)}, bf16[2,4,2,48,640]{4,3,2,1,0:T(8,128)(2,1)S(1)}, u32[]{:S(2)}, u32[]{:S(2)}) collective-permute-start(bf16[2,4,2,48,640]{4,3,2,1,0:T(8,128)(2,1)S(1)} %copy-done.30), channel_id=1, source_target_pairs={{0,2},{2,0},{1,3},{3,1},{4,6},{6,4},{5,7},{7,5},{8,10},{10,8},{9,1... | collective-permute-start | bytes 2949128 | tf_op jit(solution)/shard_map/ppermute | solution.py:111
  162.6 22.5 %collective-permute-start.40 = (bf16[128,1536]{1,0:T(8,128)(2,1)S(1)}, bf16[128,1536]{1,0:T(8,128)(2,1)S(1)}, u32[]{:S(2)}, u32[]{:S(2)}) collective-permute-start(bf16[128,1536]{1,0:T(8,128)(2,1)S(1)} %get-tuple-element.411), channel_id=1, source_target_pairs={{0,24},{8,0},{16,8},{24,16},{1,25},{9,1},{17,9},{25,17},{2,26},{10... | collective-permute-start | bytes 1179656 | tf_op jit(solution)/shard_map/ppermute | solution.py:116
  162.6 28.0 %collective-permute-start.39 = (bf16[128,1536]{1,0:T(8,128)(2,1)S(1)}, bf16[128,1536]{1,0:T(8,128)(2,1)S(1)}, u32[]{:S(2)}, u32[]{:S(2)}) collective-permute-start(bf16[128,1536]{1,0:T(8,128)(2,1)S(1)} %get-tuple-element.411), channel_id=1, source_target_pairs={{0,16},{8,24},{16,0},{24,8},{1,17},{9,25},{17,1},{25,9},{2,18},{10... | collective-permute-start | bytes 1179656 | tf_op jit(solution)/shard_map/ppermute | solution.py:116
  164.1 26.6 %collective-permute-start.38 = (bf16[128,1536]{1,0:T(8,128)(2,1)S(1)}, bf16[128,1536]{1,0:T(8,128)(2,1)S(1)}, u32[]{:S(2)}, u32[]{:S(2)}) collective-permute-start(bf16[128,1536]{1,0:T(8,128)(2,1)S(1)} %get-tuple-element.411), channel_id=1, source_target_pairs={{0,8},{8,16},{16,24},{24,0},{1,9},{9,17},{17,25},{25,1},{2,10},{10... | collective-permute-start | bytes 1179656 | tf_op jit(solution)/shard_map/ppermute | solution.py:116
  249.7 36.5 %collective-permute-start.49 = (bf16[128,1536]{1,0:T(8,128)(2,1)S(1)}, bf16[128,1536]{1,0:T(8,128)(2,1)S(1)}, u32[]{:S(2)}, u32[]{:S(2)}) collective-permute-start(bf16[128,1536]{1,0:T(8,128)(2,1)S(1)} %get-tuple-element.447), channel_id=1, source_target_pairs={{0,16},{8,24},{16,0},{24,8},{1,17},{9,25},{17,1},{25,9},{2,18},{10... | collective-permute-start | bytes 1179656 | tf_op jit(solution)/shard_map/ppermute | solution.py:116
  251.9 34.3 %collective-permute-start.50 = (bf16[128,1536]{1,0:T(8,128)(2,1)S(1)}, bf16[128,1536]{1,0:T(8,128)(2,1)S(1)}, u32[]{:S(2)}, u32[]{:S(2)}) collective-permute-start(bf16[128,1536]{1,0:T(8,128)(2,1)S(1)} %get-tuple-element.448), channel_id=1, source_target_pairs={{0,24},{8,0},{16,8},{24,16},{1,25},{9,1},{17,9},{25,17},{2,26},{10... | collective-permute-start | bytes 1179656 | tf_op jit(solution)/shard_map/ppermute | solution.py:116
  252.1 44.0 %collective-permute-start.54 = (bf16[4,2,96,1152]{3,2,1,0:T(8,128)(2,1)S(1)}, bf16[4,2,96,1152]{3,2,1,0:T(8,128)(2,1)S(1)}, u32[]{:S(2)}, u32[]{:S(2)}) collective-permute-start(bf16[4,2,96,1152]{3,2,1,0:T(8,128)(2,1)S(1)} %get-tuple-element.468), channel_id=1, source_target_pairs={{0,4},{4,0},{1,5},{5,1},{2,6},{6,2},{3,7},{7,3},{8,12},{12,8},{9,1... | collective-permute-start | bytes 5308424 | tf_op jit(solution)/shard_map/ppermute | solution.py:111
  253.4 42.8 %collective-permute-start.55 = (bf16[4,2,96,1152]{3,2,1,0:T(8,128)(2,1)S(1)}, bf16[4,2,96,1152]{3,2,1,0:T(8,128)(2,1)S(1)}, u32[]{:S(2)}, u32[]{:S(2)}) collective-permute-start(bf16[4,2,96,1152]{3,2,1,0:T(8,128)(2,1)S(1)} %get-tuple-element.469), channel_id=1, source_target_pairs={{0,2},{2,0},{1,3},{3,1},{4,6},{6,4},{5,7},{7,5},{8,10},{10,8},{9,1... | collective-permute-start | bytes 5308424 | tf_op jit(solution)/shard_map/ppermute | solution.py:111
  297.9 21.3 %collective-permute-start.56 = (bf16[4,96,1152]{2,1,0:T(8,128)(2,1)S(1)}, bf16[4,96,1152]{2,1,0:T(8,128)(2,1)S(1)}, u32[]{:S(2)}, u32[]{:S(2)}) collective-permute-start(bf16[4,96,1152]{2,1,0:T(8,128)(2,1)S(1)} %get-tuple-element.484), channel_id=1, source_target_pairs={{0,2},{2,0},{1,3},{3,1},{4,6},{6,4},{5,7},{7,5},{8,10},{10,8},{9,1... | collective-permute-start | bytes 2654216 | tf_op jit(solution)/shard_map/ppermute | solution.py:111
  299.4 20.5 %collective-permute-start.57 = (bf16[4,96,1152]{2,1,0:T(8,128)(2,1)S(1)}, bf16[4,96,1152]{2,1,0:T(8,128)(2,1)S(1)}, u32[]{:S(2)}, u32[]{:S(2)}) collective-permute-start(bf16[4,96,1152]{2,1,0:T(8,128)(2,1)S(1)} %get-tuple-element.485), channel_id=1, source_target_pairs={{0,4},{4,0},{1,5},{5,1},{2,6},{6,2},{3,7},{7,3},{8,12},{12,8},{9,1... | collective-permute-start | bytes 2654216 | tf_op jit(solution)/shard_map/ppermute | solution.py:111
  336.8 22.2 %collective-permute-start.64 = (bf16[4,2,96,384]{3,2,1,0:T(8,128)(2,1)S(1)}, bf16[4,2,96,384]{3,2,1,0:T(8,128)(2,1)S(1)}, u32[]{:S(2)}, u32[]{:S(2)}) collective-permute-start(bf16[4,2,96,384]{3,2,1,0:T(8,128)(2,1)S(1)} %get-tuple-element.523), channel_id=1, source_target_pairs={{0,4},{4,0},{1,5},{5,1},{2,6},{6,2},{3,7},{7,3},{8,12},{12,8},{9,1... | collective-permute-start | bytes 1769480 | tf_op jit(solution)/shard_map/ppermute | solution.py:111
  337.7 21.3 %collective-permute-start.65 = (bf16[4,2,96,384]{3,2,1,0:T(8,128)(2,1)S(1)}, bf16[4,2,96,384]{3,2,1,0:T(8,128)(2,1)S(1)}, u32[]{:S(2)}, u32[]{:S(2)}) collective-permute-start(bf16[4,2,96,384]{3,2,1,0:T(8,128)(2,1)S(1)} %get-tuple-element.524), channel_id=1, source_target_pairs={{0,2},{2,0},{1,3},{3,1},{4,6},{6,4},{5,7},{7,5},{8,10},{10,8},{9,1... | collective-permute-start | bytes 1769480 | tf_op jit(solution)/shard_map/ppermute | solution.py:111
  359.0 28.4 %collective-permute-start.71 = (bf16[4,2,96,640]{3,2,1,0:T(8,128)(2,1)S(1)}, bf16[4,2,96,640]{3,2,1,0:T(8,128)(2,1)S(1)}, u32[]{:S(2)}, u32[]{:S(2)}) collective-permute-start(bf16[4,2,96,640]{3,2,1,0:T(8,128)(2,1)S(1)} %get-tuple-element.540), channel_id=1, source_target_pairs={{0,2},{2,0},{1,3},{3,1},{4,6},{6,4},{5,7},{7,5},{8,10},{10,8},{9,1... | collective-permute-start | bytes 2949128 | tf_op jit(solution)/shard_map/ppermute | solution.py:111
  360.4 27.0 %collective-permute-start.70 = (bf16[4,2,96,512]{3,2,1,0:T(8,128)(2,1)S(1)}, bf16[4,2,96,512]{3,2,1,0:T(8,128)(2,1)S(1)}, u32[]{:S(2)}, u32[]{:S(2)}) collective-permute-start(bf16[4,2,96,512]{3,2,1,0:T(8,128)(2,1)S(1)} %get-tuple-element.539), channel_id=1, source_target_pairs={{0,4},{4,0},{1,5},{5,1},{2,6},{6,2},{3,7},{7,3},{8,12},{12,8},{9,1... | collective-permute-start | bytes 2359304 | tf_op jit(solution)/shard_map/ppermute | solution.py:111
  362.7 24.7 %collective-permute-start.68 = (bf16[4,96,384]{2,1,0:T(8,128)(2,1)S(1)}, bf16[4,96,384]{2,1,0:T(8,128)(2,1)S(1)}, u32[]{:S(2)}, u32[]{:S(2)}) collective-permute-start(bf16[4,96,384]{2,1,0:T(8,128)(2,1)S(1)} %get-tuple-element.537), channel_id=1, source_target_pairs={{0,2},{2,0},{1,3},{3,1},{4,6},{6,4},{5,7},{7,5},{8,10},{10,8},{9,1... | collective-permute-start | bytes 884744 | tf_op jit(solution)/shard_map/ppermute | solution.py:111
  363.5 23.9 %collective-permute-start.69 = (bf16[4,96,384]{2,1,0:T(8,128)(2,1)S(1)}, bf16[4,96,384]{2,1,0:T(8,128)(2,1)S(1)}, u32[]{:S(2)}, u32[]{:S(2)}) collective-permute-start(bf16[4,96,384]{2,1,0:T(8,128)(2,1)S(1)} %get-tuple-element.538), channel_id=1, source_target_pairs={{0,4},{4,0},{1,5},{5,1},{2,6},{6,2},{3,7},{7,3},{8,12},{12,8},{9,1... | collective-permute-start | bytes 884744 | tf_op jit(solution)/shard_map/ppermute | solution.py:111
  423.2 27.1 %collective-permute-start.78 = (bf16[2,48,1920]{2,1,0:T(8,128)(2,1)S(1)}, bf16[2,48,1920]{2,1,0:T(8,128)(2,1)S(1)}, u32[]{:S(2)}, u32[]{:S(2)}) collective-permute-start(bf16[2,48,1920]{2,1,0:T(8,128)(2,1)S(1)} %get-tuple-element.573), channel_id=1, source_target_pairs={{0,16},{8,24},{16,0},{24,8},{1,17},{9,25},{17,1},{25,9},{2,18},{10... | collective-permute-start | bytes 1105928 | tf_op jit(solution)/shard_map/ppermute | solution.py:116
  423.2 27.1 %collective-permute-start.79 = (bf16[2,48,1920]{2,1,0:T(8,128)(2,1)S(1)}, bf16[2,48,1920]{2,1,0:T(8,128)(2,1)S(1)}, u32[]{:S(2)}, u32[]{:S(2)}) collective-permute-start(bf16[2,48,1920]{2,1,0:T(8,128)(2,1)S(1)} %get-tuple-element.574), channel_id=1, source_target_pairs={{0,24},{8,0},{16,8},{24,16},{1,25},{9,1},{17,9},{25,17},{2,26},{10... | collective-permute-start | bytes 1105928 | tf_op jit(solution)/shard_map/ppermute | solution.py:116
  (122 other events, 1236.1 us)

commit v5 on v4

--- a/solution.py
+++ b/solution.py
@@ -166,8 +166,8 @@
 
 
 LITTLE = pl.CostEstimate(flops=1, bytes_accessed=1, transcendentals=0)
-SPACE = pltpu.CompilerParams(vmem_limit_bytes=20 << 20)
-ROOM = pltpu.CompilerParams(vmem_limit_bytes=14 << 20)
+SPACE = pltpu.CompilerParams(vmem_limit_bytes=16 << 20)
+ROOM = pltpu.CompilerParams(vmem_limit_bytes=12 << 20)
 VMEM = pl.BlockSpec(memory_space=pltpu.VMEM)
 SMEM = pl.BlockSpec(memory_space=pltpu.SMEM)
 
@@ -201,7 +201,7 @@
 
 def whole_block(array):
     dims = len(array.shape)
-    return pl.BlockSpec(array.shape, lambda i: (0,) * dims)
+    return pl.BlockSpec(array.shape, lambda i: (0,) * dims, pipeline_mode=pl.Buffered(1))
 
 
 def lead_block(shape):
@@ -661,7 +661,7 @@
         out_specs=[spec_a, spec_b, rows, rows, rows],
         out_shape=[group, group, wide_rows, wide_rows, wide_rows],
         scratch_shapes=scratch,
-        compiler_params=pltpu.CompilerParams(vmem_limit_bytes=42 << 20),
+        compiler_params=pltpu.CompilerParams(vmem_limit_bytes=30 << 20),
         cost_estimate=LITTLE,
     )(here, *normed, *upstream, weight_down, *weights)
 
@@ -1056,21 +1056,26 @@
     return run(kernel, shapes, here, *keeps, *cames)
 
 
-def inner_sums(here, own, pieces):
-    cores, rows, columns = own.shape
-    number = len(pieces)
-
-    def kernel(here_ref, own_ref, *refs):
-        mine_ref, send_ref = refs[number:]
+def inner_sums(here, groups):
+    rows = groups[0][0].shape[1]
+    columns = sum(own.shape[2] for own, pieces in groups)
+    counts = [1 + len(pieces) for own, pieces in groups]
+
+    def kernel(here_ref, *refs):
+        mine_ref, send_ref = refs[sum(counts) :]
         core = here_ref[3]
         for at, out in ((core, mine_ref), (1 - core, send_ref)):
-            total = own_ref[at]
-            for ref in refs[:number]:
-                total = total + wide(ref[at])
-            out[...] = total.astype(out.dtype)
+            parts, first = [], 0
+            for count in counts:
+                total = refs[first][at]
+                for ref in refs[first + 1 : first + count]:
+                    total = total + wide(ref[at])
+                parts.append(total)
+                first += count
+            out[...] = jnp.concatenate(parts, axis=1).astype(out.dtype)
 
     shapes = (shape_of((rows, columns), jnp.float32), shape_of((rows, columns)))
-    return run(kernel, shapes, here, own, *pieces)
+    return run(kernel, shapes, here, *(v for own, pieces in groups for v in (own, *pieces)))
 
 
 def inner_results(here, mine, came, width, key_width):
@@ -1429,23 +1434,31 @@
             rows,
             vector_terms,
         )
+        send_a, keep_a, send_b, keep_b = plane_step(here, (keep_a, keep_b), (came_a, came_b))
+        came_a, came_b = swapped(send_a, "x"), swapped(send_b, "y")
         send_c, keep_c, send_d, keep_d, came_a, came_b, share_parts, share_pieces = sync(
             send_c, keep_c, send_d, keep_d, came_a, came_b, share_parts, share_pieces
         )
         share_pieces |= depth_sent(share_parts, far_shifts())
-        send_a, keep_a, send_b, keep_b = plane_step(here, (keep_a, keep_b), (came_a, came_b))
-        came_a, came_b = swapped(send_a, "x"), swapped(send_b, "y")
         came_c, came_d = swapped(send_c, "y"), swapped(send_d, "x")
-        came_a, came_b, came_c, came_d, share_pieces = sync(
-            came_a, came_b, came_c, came_d, share_pieces
-        )
+        came_c, came_d, share_pieces = sync(came_c, came_d, share_pieces)
         send_c, keep_c, send_d, keep_d = plane_step(here, (keep_c, keep_d), (came_c, came_d))
         came_c, came_d = swapped(send_c, "x"), swapped(send_d, "y")
-        output_pieces |= depth_sent(after(output_parts, share_pieces), [last_shift])
-        came_c, came_d, output_pieces = sync(came_c, came_d, output_pieces)
+        keep_a, came_a, keep_b, came_b = (
+            v.reshape(nz, nc, owned, -1) for v in (keep_a, came_a, keep_b, came_b)
+        )
+        own, *parts = inner_blocks(here, (keep_a, keep_b), (came_a, came_b))
+        parts = dict(enumerate(parts, 1))
+        parts = after(parts, share_pieces)
+        pieces = depth_sent(parts, every_shift())
+        gate_sum, up_sum = collect_columns(here, in_order(share_pieces), sizes, unit, lane)
+        came_c, came_d, pieces, gate_sum, up_sum = sync(
+            came_c, came_d, pieces, gate_sum, up_sum
+        )
+        groups = [(own, in_order(pieces))]
         keeps, cames = (
             [v.reshape(nz, nc, owned, -1) for v in group]
-            for group in ((keep_a, keep_b, keep_c, keep_d), (came_a, came_b, came_c, came_d))
+            for group in ((keep_c, keep_d), (came_c, came_d))
         )
     else:
         share_pieces |= depth_sent(share_parts, far_shifts())
@@ -1460,10 +1473,11 @@
             for v in (output_term, inner_term)
         ]
         cames = [jnp.zeros_like(v) for v in keeps]
+        groups = []
     if not in_square:
         output_pieces |= depth_sent(output_parts, [last_shift])
-    layer_output = first_hidden + output_own + sum(wide(v) for v in in_order(output_pieces))
-    gate_sum, up_sum = collect_columns(here, in_order(share_pieces), sizes, unit, lane)
+    if not in_square:
+        gate_sum, up_sum = collect_columns(here, in_order(share_pieces), sizes, unit, lane)
 
     own, *parts = inner_blocks(here, keeps, cames)
     parts = dict(enumerate(parts, 1))
@@ -1474,7 +1488,10 @@
         first_send, first_keep, second_send, second_keep = down_step(
             here, (first_keep, second_keep), (came_first, came_second)
         )
-        first_send, second_send = after((first_send, second_send), pieces[first_shift])
+        early = in_order(pieces)
+        first_send, second_send = after((first_send, second_send), early)
+        groups.append((own, in_order(pieces)))
+        output_pieces |= depth_sent(after(output_parts, early), [last_shift])
         came_first, came_second = swapped(first_send, "x"), swapped(second_send, "y")
         down_sum = jnp.concatenate(
             [
@@ -1483,8 +1500,11 @@
             ],
             axis=0,
         )
-    pieces, down_sum = sync(pieces, down_sum)
-    mine, send = inner_sums(here, own, in_order(pieces))
+    else:
+        groups = [(own, in_order(pieces))]
+    layer_output = first_hidden + output_own + sum(wide(v) for v in in_order(output_pieces))
+    groups, down_sum = sync(groups, down_sum)
+    mine, send = inner_sums(here, groups)
     output_sum, query_sum, key_sum, value_sum, vector_sums = inner_results(
         here, mine, swapped(send, "c"), width, key_width
     )

time: 466 us -> 444 us (0.953)
  the two profiles are of different devices: /device:TPU:29 before, /device:TPU:1 now
where the time goes in v5:
time: 444 us; the launch traced here: 437 us
  waiting for transfers between devices  210 us (47%)
  starting transfers between devices  103 us (23%)
  Pallas kernels  95.3 us (21%)
  local copies, waits for them, and re-layouts  17.1 us (4%)
  other arithmetic  8.67 us (2%)
    ppermute x32, waiting for transfers between devices, shifted(): lax.ppermute(values, 'z', [(i, (i + amount) % count) for i in range(count)])  127 us
    ppermute x56, waiting for transfers between devices, swapped(): return lax.ppermute(values, axis, [(0, 1), (1, 0)])  83.5 us
    ppermute x56, starting transfers between devices, swapped(): return lax.ppermute(values, axis, [(0, 1), (1, 0)])  58.8 us
    ppermute x32, starting transfers between devices, shifted(): lax.ppermute(values, 'z', [(i, (i + amount) % count) for i in range(count)])  44.4 us
    pallas_call x10, Pallas kernels, run_grid(): pl.pallas_call(kernel, grid=(grid,), in_specs=[SMEM] + list(specs), out_s...  36.5 us
    pallas_call x1, Pallas kernels, feed_forward(): pl.pallas_call(kernel, grid=(2 * steps,), in_specs=[SMEM, spec_a, spec_b,...  27.8 us
    pallas_call x19, Pallas kernels, run(): pl.pallas_call(kernel, in_specs=[SMEM] + [VMEM] * len(arrays), out_specs=...  22.6 us
  transfers between devices with their start and end apart: 88, of which 43 were waited for; matrix products, arithmetic and copies ran while one was open for 4% of the time, Pallas kernels for 14%

profile of v5, /device:TPU:1, one launch (start us, length us, event | category | flops | bytes accessed | tf_op | source)
XLA Modules:
  0.0 436.6 jit_solution(11295826734916515245)
XLA Ops:
  17.1 7.6 %collective-permute-done.1.refs_2_ = bf16[48,2176]{1,0:T(8,128)(2,1)S(1)} collective-permute-done((bf16[48,2176]{1,0:T(8,128)(2,1)S(1)}, bf16[48,2176]{1,0:T(8,128)(2,1)S(1)}, u32[]{:S(2)}, u32[]{:S(2)}) %collective-permute-start.1) | collective-permute-done | bytes 208928 | tf_op jit(solution)/shard_map/ppermute | solution.py:116
  35.3 5.4 %collective-permute-done.6.refs_1_ = bf16[48,1536]{1,0:T(8,128)(2,1)S(1)} collective-permute-done((bf16[48,1536]{1,0:T(8,128)(2,1)S(1)}, bf16[48,1536]{1,0:T(8,128)(2,1)S(1)}, u32[]{:S(2)}, u32[]{:S(2)}) %collective-permute-start.6) | collective-permute-done | bytes 147488 | tf_op jit(solution)/shard_map/ppermute | solution.py:116
  46.5 15.7 %collective-permute-done.12.refs_2_ = bf16[48,1536]{1,0:T(8,128)(2,1)S(1)} collective-permute-done((bf16[48,1536]{1,0:T(8,128)(2,1)S(1)}, bf16[48,1536]{1,0:T(8,128)(2,1)S(1)}, u32[]{:S(2)}, u32[]{:S(2)}) %collective-permute-start.12) | collective-permute-done | bytes 147488 | tf_op jit(solution)/shard_map/ppermute | solution.py:116
  63.2 9.2 %collective-permute-done.14 = bf16[128,1536]{1,0:T(8,128)(2,1)S(1)} collective-permute-done((bf16[128,1536]{1,0:T(8,128)(2,1)}, bf16[128,1536]{1,0:T(8,128)(2,1)S(1)}, u32[]{:S(2)}, u32[]{:S(2)}) %collective-permute-start.14) | collective-permute-done | bytes 393248 | tf_op jit(solution)/shard_map/ppermute | solution.py:111
  90.2 15.7 %collective-permute-done.23.refs_3_ = bf16[2,48,1152]{2,1,0:T(8,128)(2,1)S(1)} collective-permute-done((bf16[2,48,1152]{2,1,0:T(8,128)(2,1)S(1)}, bf16[2,48,1152]{2,1,0:T(8,128)(2,1)S(1)}, u32[]{:S(2)}, u32[]{:S(2)}) %collective-permute-start.23) | collective-permute-done | bytes 221216 | tf_op jit(solution)/shard_map/ppermute | solution.py:116
  125.9 5.3 %shard_map.258 = (bf16[2,2,64,768]{3,2,1,0:T(8,128)(2,1)S(1)}, bf16[2,2,64,768]{3,2,1,0:T(8,128)(2,1)S(1)}, f32[2,6,128,128]{3,2,1,0:T(8,128)S(1)}) custom-call(s32[4]{0:T(128)S(1)} %pad_add_fusion.here_ref, bf16[2,6,2,64,128]{4,3,2,1,0:T(8,128)(2,1)S(1)} %get-tuple-element.366.q_ref, bf16[4,2,2,64,256]{4,3,2,1,0:T(8,128)(2,1)S(1)} %pad_maximum_fusion.3.pair_ref, ...), custom_call_target="tpu_custom_call" | custom-call | flops 1 | bytes 1 | tf_op jit(solution)/shard_map/pallas_call | solution.py:191
  131.2 9.1 %collective-permute-done.32 = bf16[128,1536]{1,0:T(8,128)(2,1)} collective-permute-done((bf16[128,1536]{1,0:T(8,128)(2,1)}, bf16[128,1536]{1,0:T(8,128)(2,1)}, u32[]{:S(2)}, u32[]{:S(2)}) %collective-permute-start.32) | collective-permute-done | bytes 393248 | tf_op jit(solution)/shard_map/ppermute | solution.py:116
  164.9 16.2 %collective-permute-done.42.refs_7_ = bf16[2,4,2,48,640]{4,3,2,1,0:T(8,128)(2,1)S(1)} collective-permute-done((bf16[2,4,2,48,640]{4,3,2,1,0:T(8,128)(2,1)S(1)}, bf16[2,4,2,48,640]{4,3,2,1,0:T(8,128)(2,1)S(1)}, u32[]{:S(2)}, u32[]{:S(2)}) %collective-permute-start.42) | collective-permute-done | bytes 983072 | tf_op jit(solution)/shard_map/ppermute | solution.py:111
  186.7 7.9 %collective-permute-done.39 = bf16[128,1536]{1,0:T(8,128)(2,1)S(1)} collective-permute-done((bf16[128,1536]{1,0:T(8,128)(2,1)S(1)}, bf16[128,1536]{1,0:T(8,128)(2,1)S(1)}, u32[]{:S(2)}, u32[]{:S(2)}) %collective-permute-start.39) | collective-permute-done | bytes 393248 | tf_op jit(solution)/shard_map/ppermute | solution.py:116
  200.8 27.8 %shard_map.262 = (bf16[512,1536]{1,0:T(8,128)(2,1)S(1)}, bf16[512,1536]{1,0:T(8,128)(2,1)S(1)}, bf16[1024,1152]{1,0:T(8,128)(2,1)S(1)}, bf16[1024,1152]{1,0:T(8,128)(2,1)S(1)}, bf16[1024,1152]{1,0:T(8,128)(2,1)S(1)}) custom-call(s32[4]{0:T(128)S(1)} %pad_add_fusion.here_ref, bf16[512,1536]{1,0:T(8,128)(2,1)S(1)} %collective-permute-done.45.na_ref.refs_0_, ...), custom_call_target="tpu_custom_call" | custom-call | flops 1 | bytes 1 | tf_op jit(solution)/shard_map/pallas_call | solution.py:656
  229.1 9.9 %shard_map.264 = (bf16[4,2,96,1152]{3,2,1,0:T(8,128)(2,1)S(1)}, bf16[4,2,96,1152]{3,2,1,0:T(8,128)(2,1)S(1)}, bf16[4,2,96,1152]{3,2,1,0:T(8,128)(2,1)S(1)}, bf16[4,2,96,1152]{3,2,1,0:T(8,128)(2,1)S(1)}) custom-call(s32[4]{0:T(128)S(1)} %pad_add_fusion.here_ref, bf16[512,1536]{1,0:T(8,128)(2,1)S(1)} %collective-permute-done.45.na_ref.refs_0_, ...), custom_call_target="tpu_custom_call" | custom-call | flops 1 | bytes 1 | tf_op jit(solution)/shard_map/pallas_call | solution.py:191
  247.4 5.6 %shard_map.266 = (bf16[512,1536]{1,0:T(8,128)(2,1)S(1)}, bf16[512,1536]{1,0:T(8,128)(2,1)S(1)}) custom-call(s32[4]{0:T(128)S(1)} %pad_add_fusion.here_ref, bf16[1024,1152]{1,0:T(8,128)(2,1)S(1)} %get-tuple-element.462.hidden_ref, bf16[1152,1536]{1,0:T(8,128)(2,1)S(1)} %bitcast.78), custom_call_target="tpu_custom_call" | custom-call | flops 1 | bytes 1 | tf_op jit(solution)/shard_map/pallas_call | solution.py:191
  253.0 5.3 %shard_map.265 = (bf16[2,144,1536]{2,1,0:T(8,128)(2,1)S(1)}, bf16[2,144,1536]{2,1,0:T(8,128)(2,1)S(1)}, bf16[2,144,1536]{2,1,0:T(8,128)(2,1)S(1)}, bf16[2,144,1536]{2,1,0:T(8,128)(2,1)S(1)}) custom-call(s32[4]{0:T(128)S(1)} %pad_add_fusion.here_ref, bf16[1024,1152]{1,0:T(8,128)(2,1)S(1)} %get-tuple-element.462.hidden_ref, ...), custom_call_target="tpu_custom_call" | custom-call | flops 1 | bytes 1 | tf_op jit(solution)/shard_map/pallas_call | solution.py:889
  258.4 11.3 %collective-permute-done.49.refs_1_ = bf16[128,1536]{1,0:T(8,128)(2,1)S(1)} collective-permute-done((bf16[128,1536]{1,0:T(8,128)(2,1)S(1)}, bf16[128,1536]{1,0:T(8,128)(2,1)S(1)}, u32[]{:S(2)}, u32[]{:S(2)}) %collective-permute-start.49) | collective-permute-done | bytes 393248 | tf_op jit(solution)/shard_map/ppermute | solution.py:116
  279.2 5.4 %collective-permute-done.54.first_came = bf16[4,2,96,1152]{3,2,1,0:T(8,128)(2,1)S(1)} collective-permute-done((bf16[4,2,96,1152]{3,2,1,0:T(8,128)(2,1)S(1)}, bf16[4,2,96,1152]{3,2,1,0:T(8,128)(2,1)S(1)}, u32[]{:S(2)}, u32[]{:S(2)}) %collective-permute-start.54) | collective-permute-done | bytes 1769504 | tf_op jit(solution)/shard_map/ppermute | solution.py:111
  293.6 6.2 %shard_map.270 = (bf16[2,2,64,768]{3,2,1,0:T(8,128)(2,1)S(1)}, bf16[2,2,2,64,256]{4,3,2,1,0:T(8,128)(2,1)S(1)}, bf16[2,2,2,64,256]{4,3,2,1,0:T(8,128)(2,1)S(1)}) custom-call(s32[4]{0:T(128)S(1)} %pad_add_fusion.here_ref, bf16[2,6,2,64,128]{4,3,2,1,0:T(8,128)(2,1)S(1)} %get-tuple-element.366.q_ref, ...), custom_call_target="tpu_custom_call" | custom-call | flops 1 | bytes 1 | tf_op jit(solution)/shard_map/pallas_call | solution.py:191
  299.8 7.0 %collective-permute-done.58 = bf16[128,1536]{1,0:T(8,128)(2,1)S(1)} collective-permute-done((bf16[128,1536]{1,0:T(8,128)(2,1)S(1)}, bf16[128,1536]{1,0:T(8,128)(2,1)S(1)}, u32[]{:S(2)}, u32[]{:S(2)}) %collective-permute-start.58) | collective-permute-done | bytes 393248 | tf_op jit(solution)/shard_map/ppermute | solution.py:116
  319.8 6.3 %collective-permute-done.62 = bf16[128,1536]{1,0:T(8,128)(2,1)S(1)} collective-permute-done((bf16[128,1536]{1,0:T(8,128)(2,1)S(1)}, bf16[128,1536]{1,0:T(8,128)(2,1)S(1)}, u32[]{:S(2)}, u32[]{:S(2)}) %collective-permute-start.62) | collective-permute-done | bytes 393248 | tf_op jit(solution)/shard_map/ppermute | solution.py:116
  333.6 6.8 %collective-permute-done.64.first_came = bf16[4,2,96,384]{3,2,1,0:T(8,128)(2,1)S(1)} collective-permute-done((bf16[4,2,96,384]{3,2,1,0:T(8,128)(2,1)S(1)}, bf16[4,2,96,384]{3,2,1,0:T(8,128)(2,1)S(1)}, u32[]{:S(2)}, u32[]{:S(2)}) %collective-permute-start.64) | collective-permute-done | bytes 589856 | tf_op jit(solution)/shard_map/ppermute | solution.py:111
  355.8 14.9 %collective-permute-done.72.refs_2_ = bf16[2,48,1152]{2,1,0:T(8,128)(2,1)S(1)} collective-permute-done((bf16[2,48,1152]{2,1,0:T(8,128)(2,1)S(1)}, bf16[2,48,1152]{2,1,0:T(8,128)(2,1)S(1)}, u32[]{:S(2)}, u32[]{:S(2)}) %collective-permute-start.72) | collective-permute-done | bytes 221216 | tf_op jit(solution)/shard_map/ppermute | solution.py:116
  370.7 4.7 %collective-permute-done.73.refs_3_ = bf16[2,48,1152]{2,1,0:T(8,128)(2,1)S(1)} collective-permute-done((bf16[2,48,1152]{2,1,0:T(8,128)(2,1)S(1)}, bf16[2,48,1152]{2,1,0:T(8,128)(2,1)S(1)}, u32[]{:S(2)}, u32[]{:S(2)}) %collective-permute-start.73) | collective-permute-done | bytes 221216 | tf_op jit(solution)/shard_map/ppermute | solution.py:116
  385.3 4.7 %collective-permute-done.77.refs_2_ = bf16[2,48,768]{2,1,0:T(8,128)(2,1)S(1)} collective-permute-done((bf16[2,48,768]{2,1,0:T(8,128)(2,1)S(1)}, bf16[2,48,768]{2,1,0:T(8,128)(2,1)S(1)}, u32[]{:S(2)}, u32[]{:S(2)}) %collective-permute-start.77) | collective-permute-done | bytes 147488 | tf_op jit(solution)/shard_map/ppermute | solution.py:116
  399.0 9.2 %collective-permute-done.83.first_came = bf16[2,144,1536]{2,1,0:T(8,128)(2,1)S(1)} collective-permute-done((bf16[2,144,1536]{2,1,0:T(8,128)(2,1)S(1)}, bf16[2,144,1536]{2,1,0:T(8,128)(2,1)S(1)}, u32[]{:S(2)}, u32[]{:S(2)}) %collective-permute-start.83) | collective-permute-done | bytes 884768 | tf_op jit(solution)/shard_map/ppermute | solution.py:111
  412.4 4.9 %collective-permute-start.82 = (bf16[128,1536]{1,0:T(8,128)(2,1)S(1)}, bf16[128,1536]{1,0:T(8,128)(2,1)S(1)}, u32[]{:S(2)}, u32[]{:S(2)}) collective-permute-start(bf16[128,1536]{1,0:T(8,128)(2,1)S(1)} %get-tuple-element.587), channel_id=1, source_target_pairs={{0,24},{8,0},{16,8},{24,16},{1,25},{9,1},{17,9},{25,17},{2,26},{10... | collective-permute-start | bytes 1179656 | tf_op jit(solution)/shard_map/ppermute | solution.py:116
  (322 shorter events, 212.3 us)
Async XLA Ops:
  41.4 31.0 %collective-permute-start.11 = (bf16[4,2,48,1152]{3,2,1,0:T(8,128)(2,1)S(1)}, bf16[4,2,48,1152]{3,2,1,0:T(8,128)(2,1)S(1)}, u32[]{:S(2)}, u32[]{:S(2)}) collective-permute-start(bf16[4,2,48,1152]{3,2,1,0:T(8,128)(2,1)S(1)} %pad_maximum_fusion.1.refs_0_), channel_id=1, source_target_pairs={{0,4},{4,0},{1,5},{5,1},{2,6},{6,2},{3,7},{7,3},{8,12},{12,8},{9,1... | collective-permute-start | bytes 2654216 | tf_op jit(solution)/shard_map/ppermute | solution.py:111
  41.8 30.6 %collective-permute-start.10 = (bf16[4,2,48,1152]{3,2,1,0:T(8,128)(2,1)S(1)}, bf16[4,2,48,1152]{3,2,1,0:T(8,128)(2,1)S(1)}, u32[]{:S(2)}, u32[]{:S(2)}) collective-permute-start(bf16[4,2,48,1152]{3,2,1,0:T(8,128)(2,1)S(1)} %pad_maximum_fusion.1.refs_0_), channel_id=1, source_target_pairs={{0,2},{2,0},{1,3},{3,1},{4,6},{6,4},{5,7},{7,5},{8,10},{10,8},{9,1... | collective-permute-start | bytes 2654216 | tf_op jit(solution)/shard_map/ppermute | solution.py:111
  43.0 19.2 %collective-permute-start.12 = (bf16[48,1536]{1,0:T(8,128)(2,1)S(1)}, bf16[48,1536]{1,0:T(8,128)(2,1)S(1)}, u32[]{:S(2)}, u32[]{:S(2)}) collective-permute-start(bf16[48,1536]{1,0:T(8,128)(2,1)S(1)} %copy-done.23), channel_id=1, source_target_pairs={{0,16},{8,24},{16,0},{24,8},{1,17},{9,25},{17,1},{25,9},{2,18},{10... | collective-permute-start | bytes 442376 | tf_op jit(solution)/shard_map/ppermute | solution.py:116
  45.5 26.9 %collective-permute-start.15 = (bf16[152,1536]{1,0:T(8,128)(2,1)S(1)}, bf16[152,1536]{1,0:T(8,128)(2,1)S(1)}, u32[]{:S(2)}, u32[]{:S(2)}) collective-permute-start(bf16[152,1536]{1,0:T(8,128)(2,1)S(1)} %collective-permute-done.9), channel_id=1, source_target_pairs={{0,2},{2,0},{1,3},{3,1},{4,6},{6,4},{5,7},{7,5},{8,10},{10,8},{9,1... | collective-permute-start | bytes 1400840 | tf_op jit(solution)/shard_map/ppermute | solution.py:111
  46.4 25.9 %collective-permute-start.13 = (bf16[2,2,48,1152]{3,2,1,0:T(8,128)(2,1)S(1)}, bf16[2,2,48,1152]{3,2,1,0:T(8,128)(2,1)S(1)}, u32[]{:S(2)}, u32[]{:S(2)}) collective-permute-start(bf16[2,2,48,1152]{3,2,1,0:T(8,128)(2,1)S(1)} %get-tuple-element.338), channel_id=1, source_target_pairs={{0,8},{8,16},{16,24},{24,0},{1,9},{9,17},{17,25},{25,1},{2,10},{10... | collective-permute-start | bytes 1327112 | tf_op jit(solution)/shard_map/ppermute | solution.py:116
  83.8 22.2 %collective-permute-start.22 = (bf16[4,2,48,768]{3,2,1,0:T(8,128)(2,1)S(1)}, bf16[4,2,48,768]{3,2,1,0:T(8,128)(2,1)S(1)}, u32[]{:S(2)}, u32[]{:S(2)}) collective-permute-start(bf16[4,2,48,768]{3,2,1,0:T(8,128)(2,1)S(1)} %pad_maximum_fusion.2.refs_0_), channel_id=1, source_target_pairs={{0,4},{4,0},{1,5},{5,1},{2,6},{6,2},{3,7},{7,3},{8,12},{12,8},{9,1... | collective-permute-start | bytes 1769480 | tf_op jit(solution)/shard_map/ppermute | solution.py:111
  84.4 21.6 %collective-permute-start.21 = (bf16[4,2,48,768]{3,2,1,0:T(8,128)(2,1)S(1)}, bf16[4,2,48,768]{3,2,1,0:T(8,128)(2,1)S(1)}, u32[]{:S(2)}, u32[]{:S(2)}) collective-permute-start(bf16[4,2,48,768]{3,2,1,0:T(8,128)(2,1)S(1)} %pad_maximum_fusion.2.refs_0_), channel_id=1, source_target_pairs={{0,2},{2,0},{1,3},{3,1},{4,6},{6,4},{5,7},{7,5},{8,10},{10,8},{9,1... | collective-permute-start | bytes 1769480 | tf_op jit(solution)/shard_map/ppermute | solution.py:111
  84.5 21.4 %collective-permute-start.24 = (bf16[128,1536]{1,0:T(8,128)(2,1)}, bf16[128,1536]{1,0:T(8,128)(2,1)S(1)}, u32[]{:S(2)}, u32[]{:S(2)}) collective-permute-start(bf16[128,1536]{1,0:T(8,128)(2,1)} %bitcast.14.up_ref), channel_id=1, source_target_pairs={{0,8},{8,16},{16,24},{24,0},{1,9},{9,17},{17,25},{25,1},{2,10},{10... | collective-permute-start | bytes 1179656 | tf_op jit(solution)/shard_map/ppermute | solution.py:116
  85.1 20.8 %collective-permute-start.23 = (bf16[2,48,1152]{2,1,0:T(8,128)(2,1)S(1)}, bf16[2,48,1152]{2,1,0:T(8,128)(2,1)S(1)}, u32[]{:S(2)}, u32[]{:S(2)}) collective-permute-start(bf16[2,48,1152]{2,1,0:T(8,128)(2,1)S(1)} %get-tuple-element.375), channel_id=1, source_target_pairs={{0,16},{8,24},{16,0},{24,8},{1,17},{9,25},{17,1},{25,9},{2,18},{10... | collective-permute-start | bytes 663560 | tf_op jit(solution)/shard_map/ppermute | solution.py:116
  159.3 21.8 %collective-permute-start.42 = (bf16[2,4,2,48,640]{4,3,2,1,0:T(8,128)(2,1)S(1)}, bf16[2,4,2,48,640]{4,3,2,1,0:T(8,128)(2,1)S(1)}, u32[]{:S(2)}, u32[]{:S(2)}) collective-permute-start(bf16[2,4,2,48,640]{4,3,2,1,0:T(8,128)(2,1)S(1)} %copy-done.12), channel_id=1, source_target_pairs={{0,4},{4,0},{1,5},{5,1},{2,6},{6,2},{3,7},{7,3},{8,12},{12,8},{9,1... | collective-permute-start | bytes 2949128 | tf_op jit(solution)/shard_map/ppermute | solution.py:111
  159.5 22.4 %collective-permute-start.41 = (bf16[2,4,2,48,640]{4,3,2,1,0:T(8,128)(2,1)S(1)}, bf16[2,4,2,48,640]{4,3,2,1,0:T(8,128)(2,1)S(1)}, u32[]{:S(2)}, u32[]{:S(2)}) collective-permute-start(bf16[2,4,2,48,640]{4,3,2,1,0:T(8,128)(2,1)S(1)} %copy-done.12), channel_id=1, source_target_pairs={{0,2},{2,0},{1,3},{3,1},{4,6},{6,4},{5,7},{7,5},{8,10},{10,8},{9,1... | collective-permute-start | bytes 2949128 | tf_op jit(solution)/shard_map/ppermute | solution.py:111
  161.6 22.1 %collective-permute-start.40 = (bf16[128,1536]{1,0:T(8,128)(2,1)S(1)}, bf16[128,1536]{1,0:T(8,128)(2,1)S(1)}, u32[]{:S(2)}, u32[]{:S(2)}) collective-permute-start(bf16[128,1536]{1,0:T(8,128)(2,1)S(1)} %get-tuple-element.423), channel_id=1, source_target_pairs={{0,24},{8,0},{16,8},{24,16},{1,25},{9,1},{17,9},{25,17},{2,26},{10... | collective-permute-start | bytes 1179656 | tf_op jit(solution)/shard_map/ppermute | solution.py:116
  163.5 31.1 %collective-permute-start.39 = (bf16[128,1536]{1,0:T(8,128)(2,1)S(1)}, bf16[128,1536]{1,0:T(8,128)(2,1)S(1)}, u32[]{:S(2)}, u32[]{:S(2)}) collective-permute-start(bf16[128,1536]{1,0:T(8,128)(2,1)S(1)} %get-tuple-element.423), channel_id=1, source_target_pairs={{0,16},{8,24},{16,0},{24,8},{1,17},{9,25},{17,1},{25,9},{2,18},{10... | collective-permute-start | bytes 1179656 | tf_op jit(solution)/shard_map/ppermute | solution.py:116
  163.5 31.1 %collective-permute-start.38 = (bf16[128,1536]{1,0:T(8,128)(2,1)S(1)}, bf16[128,1536]{1,0:T(8,128)(2,1)S(1)}, u32[]{:S(2)}, u32[]{:S(2)}) collective-permute-start(bf16[128,1536]{1,0:T(8,128)(2,1)S(1)} %get-tuple-element.423), channel_id=1, source_target_pairs={{0,8},{8,16},{16,24},{24,0},{1,9},{9,17},{17,25},{25,1},{2,10},{10... | collective-permute-start | bytes 1179656 | tf_op jit(solution)/shard_map/ppermute | solution.py:116
  241.0 28.7 %collective-permute-start.49 = (bf16[128,1536]{1,0:T(8,128)(2,1)S(1)}, bf16[128,1536]{1,0:T(8,128)(2,1)S(1)}, u32[]{:S(2)}, u32[]{:S(2)}) collective-permute-start(bf16[128,1536]{1,0:T(8,128)(2,1)S(1)} %get-tuple-element.459), channel_id=1, source_target_pairs={{0,16},{8,24},{16,0},{24,8},{1,17},{9,25},{17,1},{25,9},{2,18},{10... | collective-permute-start | bytes 1179656 | tf_op jit(solution)/shard_map/ppermute | solution.py:116
  243.0 26.7 %collective-permute-start.50 = (bf16[128,1536]{1,0:T(8,128)(2,1)S(1)}, bf16[128,1536]{1,0:T(8,128)(2,1)S(1)}, u32[]{:S(2)}, u32[]{:S(2)}) collective-permute-start(bf16[128,1536]{1,0:T(8,128)(2,1)S(1)} %get-tuple-element.460), channel_id=1, source_target_pairs={{0,24},{8,0},{16,8},{24,16},{1,25},{9,1},{17,9},{25,17},{2,26},{10... | collective-permute-start | bytes 1179656 | tf_op jit(solution)/shard_map/ppermute | solution.py:116
  245.4 39.1 %collective-permute-start.54 = (bf16[4,2,96,1152]{3,2,1,0:T(8,128)(2,1)S(1)}, bf16[4,2,96,1152]{3,2,1,0:T(8,128)(2,1)S(1)}, u32[]{:S(2)}, u32[]{:S(2)}) collective-permute-start(bf16[4,2,96,1152]{3,2,1,0:T(8,128)(2,1)S(1)} %get-tuple-element.480), channel_id=1, source_target_pairs={{0,4},{4,0},{1,5},{5,1},{2,6},{6,2},{3,7},{7,3},{8,12},{12,8},{9,1... | collective-permute-start | bytes 5308424 | tf_op jit(solution)/shard_map/ppermute | solution.py:111
  246.4 38.8 %collective-permute-start.55 = (bf16[4,2,96,1152]{3,2,1,0:T(8,128)(2,1)S(1)}, bf16[4,2,96,1152]{3,2,1,0:T(8,128)(2,1)S(1)}, u32[]{:S(2)}, u32[]{:S(2)}) collective-permute-start(bf16[4,2,96,1152]{3,2,1,0:T(8,128)(2,1)S(1)} %get-tuple-element.481), channel_id=1, source_target_pairs={{0,2},{2,0},{1,3},{3,1},{4,6},{6,4},{5,7},{7,5},{8,10},{10,8},{9,1... | collective-permute-start | bytes 5308424 | tf_op jit(solution)/shard_map/ppermute | solution.py:111
  286.9 19.9 %collective-permute-start.56 = (bf16[4,96,1152]{2,1,0:T(8,128)(2,1)S(1)}, bf16[4,96,1152]{2,1,0:T(8,128)(2,1)S(1)}, u32[]{:S(2)}, u32[]{:S(2)}) collective-permute-start(bf16[4,96,1152]{2,1,0:T(8,128)(2,1)S(1)} %get-tuple-element.494), channel_id=1, source_target_pairs={{0,2},{2,0},{1,3},{3,1},{4,6},{6,4},{5,7},{7,5},{8,10},{10,8},{9,1... | collective-permute-start | bytes 2654216 | tf_op jit(solution)/shard_map/ppermute | solution.py:111
  288.0 18.8 %collective-permute-start.57 = (bf16[4,96,1152]{2,1,0:T(8,128)(2,1)S(1)}, bf16[4,96,1152]{2,1,0:T(8,128)(2,1)S(1)}, u32[]{:S(2)}, u32[]{:S(2)}) collective-permute-start(bf16[4,96,1152]{2,1,0:T(8,128)(2,1)S(1)} %get-tuple-element.495), channel_id=1, source_target_pairs={{0,4},{4,0},{1,5},{5,1},{2,6},{6,2},{3,7},{7,3},{8,12},{12,8},{9,1... | collective-permute-start | bytes 2654216 | tf_op jit(solution)/shard_map/ppermute | solution.py:111
  330.2 21.3 %collective-permute-start.69 = (bf16[2,2,48,1152]{3,2,1,0:T(8,128)(2,1)S(1)}, bf16[2,2,48,1152]{3,2,1,0:T(8,128)(2,1)S(1)}, u32[]{:S(2)}, u32[]{:S(2)}) collective-permute-start(bf16[2,2,48,1152]{3,2,1,0:T(8,128)(2,1)S(1)} %get-tuple-element.547), channel_id=1, source_target_pairs={{0,24},{8,0},{16,8},{24,16},{1,25},{9,1},{17,9},{25,17},{2,26},{10... | collective-permute-start | bytes 1327112 | tf_op jit(solution)/shard_map/ppermute | solution.py:116
  351.5 24.0 %collective-permute-start.71 = (bf16[4,2,96,640]{3,2,1,0:T(8,128)(2,1)S(1)}, bf16[4,2,96,640]{3,2,1,0:T(8,128)(2,1)S(1)}, u32[]{:S(2)}, u32[]{:S(2)}) collective-permute-start(bf16[4,2,96,640]{3,2,1,0:T(8,128)(2,1)S(1)} %get-tuple-element.552), channel_id=1, source_target_pairs={{0,2},{2,0},{1,3},{3,1},{4,6},{6,4},{5,7},{7,5},{8,10},{10,8},{9,1... | collective-permute-start | bytes 2949128 | tf_op jit(solution)/shard_map/ppermute | solution.py:111
  352.2 23.3 %collective-permute-start.70 = (bf16[4,2,96,512]{3,2,1,0:T(8,128)(2,1)S(1)}, bf16[4,2,96,512]{3,2,1,0:T(8,128)(2,1)S(1)}, u32[]{:S(2)}, u32[]{:S(2)}) collective-permute-start(bf16[4,2,96,512]{3,2,1,0:T(8,128)(2,1)S(1)} %get-tuple-element.551), channel_id=1, source_target_pairs={{0,4},{4,0},{1,5},{5,1},{2,6},{6,2},{3,7},{7,3},{8,12},{12,8},{9,1... | collective-permute-start | bytes 2359304 | tf_op jit(solution)/shard_map/ppermute | solution.py:111
  355.5 20.0 %collective-permute-start.73 = (bf16[2,48,1152]{2,1,0:T(8,128)(2,1)S(1)}, bf16[2,48,1152]{2,1,0:T(8,128)(2,1)S(1)}, u32[]{:S(2)}, u32[]{:S(2)}) collective-permute-start(bf16[2,48,1152]{2,1,0:T(8,128)(2,1)S(1)} %get-tuple-element.556), channel_id=1, source_target_pairs={{0,16},{8,24},{16,0},{24,8},{1,17},{9,25},{17,1},{25,9},{2,18},{10... | collective-permute-start | bytes 663560 | tf_op jit(solution)/shard_map/ppermute | solution.py:116
  (100 other events, 1132.6 us)
